TPU v7x, 256 devices: a whole 4x4x8 slice. The times are simulated.
256 devices in a mesh: dp: 16 (over z_lo, y), ctx: 16 (over x, z_hi, core).
Axes of the slice: x: 4, y: 4, z: 8 (z_hi: 2, z_lo: 4; z = z_hi * 4 + z_lo), core: 2. Of those that a mesh axis runs over, the one named last changes fastest.
Arguments:
- queries: bfloat16 [2, 16, 2048, 2560], P(None, 'dp', 'ctx'), may hold values from -100 to 100
- keys_values: bfloat16 [16, 2048, 1024], P('dp', 'ctx'), may hold values from -5 to 5
- grad_out: bfloat16 [2, 16, 2048, 2560], P(None, 'dp', 'ctx'), may hold values from -6 to 6
- hidden_kv: bfloat16 [16, 2048, 5120], P(None, 'ctx', 'dp'), may hold values from -6 to 6
- doc_lengths: int32 [16, 16], P('dp'), may hold values from 1 to 256, 2048 in all within a row
Outputs:
- query_grad: bfloat16 [2, 16, 2048, 2560], P(None, 'dp', 'ctx')
- key_value_grad: bfloat16 [16, 2048, 1024], P('dp', 'ctx')
- weight_grad: float32 [5120, 1024], P(('dp', 'ctx'))
All inputs are finite; a program needn't handle non-finite values.
Results may differ from a plain program's by a relative error of at most 0.0077.
Values may be sent and summed in bfloat16 or wider, within the bound.
No kernel may reach another device: no remote copies, remote signals or barrier semaphores. Data moves between devices by JAX's collectives and lax.ppermute only.
A program may use at most 64 MiB of HBM per device.

v0:
```python
import math

import jax
import jax.numpy as jnp
from jax import lax
from jax.sharding import PartitionSpec as P

KV_HEADS = 4
GROUP = 5
HEAD_DIM = 128
LAYERS = 2
REACH = 2


def from_behind(value, axis, by):
    size = lax.axis_size(axis)
    pairs = [(i, i + by) for i in range(size) if 0 <= i + by < size]
    return lax.ppermute(value, axis, pairs)


def visibility(query_pos, key_pos, lengths):
    ends = jnp.cumsum(lengths)
    query_doc = jnp.sum((query_pos[:, None] >= ends[None, :]).astype(jnp.int32), axis=1)
    key_doc = jnp.sum((key_pos[:, None] >= ends[None, :]).astype(jnp.int32), axis=1)
    return (
        (key_pos[None, :] >= 0)
        & (key_pos[None, :] <= query_pos[:, None])
        & (key_doc[None, :] == query_doc[:, None])
    )


def window_grads(q_block, do_block, window, visible):
    tok_rows = q_block.shape[0]
    width = window.shape[0]
    factor = 1.0 / math.sqrt(HEAD_DIM)
    split_at = KV_HEADS * HEAD_DIM
    q_heads = q_block.reshape(tok_rows, KV_HEADS, GROUP, HEAD_DIM)
    do_heads = do_block.reshape(tok_rows, KV_HEADS, GROUP, HEAD_DIM)
    keys = window[:, :split_at].reshape(width, KV_HEADS, HEAD_DIM)
    values = window[:, split_at:].reshape(width, KV_HEADS, HEAD_DIM)
    scores = (
        jnp.einsum("tkgd,wkd->kgtw", q_heads, keys, preferred_element_type=jnp.float32) * factor
    )
    scores = jnp.where(visible[None, None], scores, -jnp.inf)
    probs = jax.nn.softmax(scores, axis=-1)
    probs_b = probs.astype(jnp.bfloat16)
    attn = jnp.einsum("kgtw,wkd->tkgd", probs_b, values, preferred_element_type=jnp.float32)
    delta = jnp.einsum("tkgd,tkgd->kgt", do_heads.astype(jnp.float32), attn)
    dprobs = jnp.einsum("tkgd,wkd->kgtw", do_heads, values, preferred_element_type=jnp.float32)
    dscores_b = (probs * (dprobs - delta[..., None])).astype(jnp.bfloat16)
    dq = jnp.einsum("kgtw,wkd->tkgd", dscores_b, keys, preferred_element_type=jnp.float32) * factor
    dk = (
        jnp.einsum("kgtw,tkgd->wkd", dscores_b, q_heads, preferred_element_type=jnp.float32)
        * factor
    )
    dv = jnp.einsum("kgtw,tkgd->wkd", probs_b, do_heads, preferred_element_type=jnp.float32)
    both = jnp.concatenate([dk.reshape(width, split_at), dv.reshape(width, split_at)], axis=1)
    return (dq.reshape(tok_rows, KV_HEADS * GROUP * HEAD_DIM), both)


def on_device(queries, keys_values, grad_out, hidden_kv, doc_lengths):
    tok_rows = keys_values.shape[1]
    width = (REACH + 1) * tok_rows
    own_kv = keys_values[0]
    position = lax.axis_index("ctx") * tok_rows
    earlier = []
    for distance in range(REACH, 0, -1):
        earlier.append(from_behind(own_kv, "ctx", distance))
    window = jnp.concatenate(earlier + [own_kv], axis=0)
    query_pos = position + jnp.arange(tok_rows, dtype=jnp.int32)
    key_pos = position - REACH * tok_rows + jnp.arange(width, dtype=jnp.int32)
    visible = visibility(query_pos, key_pos, doc_lengths[0])
    query_grads = []
    layer_terms = []
    for layer in range(LAYERS):
        dq, both = window_grads(queries[layer, 0], grad_out[layer, 0], window, visible)
        query_grads.append(dq.astype(jnp.bfloat16))
        layer_terms.append(both)
    kv_total = layer_terms[0][REACH * tok_rows :]
    for layer in range(LAYERS):
        if layer > 0:
            kv_total = kv_total + layer_terms[layer][REACH * tok_rows :]
        for distance in range(REACH, 0, -1):
            offset = (REACH - distance) * tok_rows
            piece = layer_terms[layer][offset : offset + tok_rows]
            kv_total = kv_total + from_behind(piece.astype(jnp.bfloat16), "ctx", -distance).astype(
                piece.dtype
            )
    kv_grad = kv_total.astype(jnp.bfloat16)
    partial_rows = lax.dot_general(
        hidden_kv,
        lax.all_gather(kv_grad[None], "dp", axis=0, tiled=True),
        (((0, 1), (0, 1)), ((), ())),
        preferred_element_type=jnp.float32,
    )
    weight_grad = lax.psum_scatter(partial_rows, "ctx", scatter_dimension=0, tiled=True)
    query_grad = jnp.stack(query_grads)[:, None]
    return (query_grad, kv_grad[None], weight_grad)


def solution(mesh):
    placed = (
        P(None, "dp", "ctx", None),
        P("dp", "ctx", None),
        P(None, "dp", "ctx", None),
        P(None, "ctx", "dp"),
        P("dp", None),
    )
    return jax.shard_map(
        on_device,
        mesh=mesh,
        in_specs=placed,
        out_specs=(P(None, "dp", "ctx", None), P("dp", "ctx", None), P(("dp", "ctx"), None)),
        check_vma=False,
    )
```

profile of v0, /device:TPU:3, one launch (start us, length us, event | category | flops | bytes accessed | tf_op | source)
XLA Modules:
  0.0 293.0 jit_solution(2308253683154612859)
XLA Ops:
  7.2 1.9 copy.81
  9.1 9.4 %collective-permute-start.1 = (bf16[128,1024]{0,1:T(8,128)(2,1)}, bf16[128,1024]{0,1:T(8,128)(2,1)}, u32[]{:S(2)}, u32[]{:S(2)}) collective-permute-start(bf16[128,1024]{0,1:T(8,128)(2,1)} %bitcast.4), channel_id=1, source_target_pairs={{0,1},{1,2},{2,3},{3,4},{4,5},{5,6},{6,7},{7,8},{8,9},{9,10},{10,1... | collective-permute-start | bytes 786440 | tf_op jit(solution)/shard_map/ppermute | solution.py:18
  18.5 1.9 collective-permute-start
  20.4 0.7 copy.82
  21.5 2.3 fusion.43
  23.9 2.2 copy.151
  26.1 1.1 copy.153
  27.2 1.1 copy.152
  28.8 7.3 %collective-permute-done = bf16[128,1024]{0,1:T(8,128)(2,1)} collective-permute-done((bf16[128,1024]{0,1:T(8,128)(2,1)}, bf16[128,1024]{0,1:T(8,128)(2,1)}, u32[]{:S(2)}, u32[]{:S(2)}) %collective-permute-start) | collective-permute-done | bytes 262176 | tf_op jit(solution)/shard_map/ppermute | solution.py:18
  36.1 1.2 pad_maximum_fusion.2
  37.5 3.2 %fusion.48 = (f32[4,5,128]{2,1,0:T(8,128)S(1)}, f32[4,5,128,384]{2,3,1,0:T(8,128)}) fusion(pred[128,384]{0,1:T(8,128)(4,1)S(1)} %compare_and_fusion, bf16[384,4,128,1]{0,2,3,1:T(8,128)(2,1)S(1)} %bitcast.161, bf16[128,4,5,128]{0,3,2,1:T(8,128)(2,1)S(1)} %bitcast.176), kind=kOutput, calls=%fused_computation.75 | convolution fusion | flops 255590784 | bytes 5040128 | tf_op jit(solution)/shard_map/sub | solution.py:45
  40.7 2.6 fusion.16
  43.3 1.6 fusion.51
  45.0 0.6 fusion.26
  45.7 2.1 fusion.4
  47.8 2.3 copy.108
  50.1 2.7 fusion.24
  52.8 2.3 copy.107
  55.0 1.5 fusion.17
  56.5 0.8 fusion.46
  57.4 7.7 %collective-permute-start.4 = (bf16[128,1024]{1,0:T(8,128)(2,1)}, bf16[128,1024]{1,0:T(8,128)(2,1)S(1)}, u32[]{:S(2)}, u32[]{:S(2)}) collective-permute-start(bf16[128,1024]{1,0:T(8,128)(2,1)} %get-tuple-element.9), channel_id=1, source_target_pairs={{2,0},{3,1},{4,2},{5,3},{6,4},{7,5},{8,6},{9,7},{10,8},{11,9},{12,... | collective-permute-start | bytes 786440 | tf_op jit(solution)/shard_map/ppermute | solution.py:18
  65.1 2.5 collective-permute-start.5
  67.6 4.4 %fusion.49 = (f32[4,5,128]{2,1,0:T(8,128)S(1)}, f32[4,5,128,384]{2,3,1,0:T(8,128)}) fusion(pred[128,384]{0,1:T(8,128)(4,1)} %copy-done.14, bf16[384,4,128,1]{0,2,3,1:T(8,128)(2,1)} %bitcast.162, bf16[128,4,5,128]{0,3,2,1:T(8,128)(2,1)} %bitcast.173), kind=kOutput, calls=%fused_computation.76 | convolution fusion | flops 255590784 | bytes 5040128 | tf_op jit(solution)/shard_map/sub | solution.py:45
  72.1 2.7 fusion.15
  74.8 0.6 fusion.25
  75.4 1.6 fusion.50
  77.0 2.2 fusion.6
  79.2 2.3 copy.104
  81.4 3.3 %fusion.23 = f32[4,384,128]{1,2,0:T(8,128)} fusion(bf16[4,5,128,384]{2,3,1,0:T(8,128)(2,1)} %fusion.6, bf16[128,4,5,128]{0,3,2,1:T(8,128)(2,1)} %bitcast.174), kind=kOutput, calls=%fused_computation.44 | convolution fusion | flops 251854848 | bytes 3407872 | tf_op jit(solution)/shard_map/kgtw,tkgd->wkd/dot_general | solution.py:53
  84.7 2.3 copy.103
  87.0 1.6 fusion.18
  88.7 1.9 collective-permute-start.2
  90.7 2.1 collective-permute-start.3
  92.8 12.1 %collective-permute-done.2 = bf16[128,1024]{1,0:T(8,128)(2,1)S(1)} collective-permute-done((bf16[128,1024]{1,0:T(8,128)(2,1)S(1)}, bf16[128,1024]{1,0:T(8,128)(2,1)S(1)}, u32[]{:S(2)}, u32[]{:S(2)}) %collective-permute-start.2) | collective-permute-done | bytes 262176 | tf_op jit(solution)/shard_map/ppermute | solution.py:18
  104.9 6.7 %collective-permute-done.3 = bf16[128,1024]{1,0:T(8,128)(2,1)S(1)} collective-permute-done((bf16[128,1024]{1,0:T(8,128)(2,1)S(1)}, bf16[128,1024]{1,0:T(8,128)(2,1)S(1)}, u32[]{:S(2)}, u32[]{:S(2)}) %collective-permute-start.3) | collective-permute-done | bytes 262176 | tf_op jit(solution)/shard_map/ppermute | solution.py:18
  111.6 1.9 fusion.31
  114.8 2.4 fusion.22
  117.2 1.3 copy.100
  118.5 2.3 fusion.21
  121.1 71.2 %all-gather.3.cloned.1.call-done = bf16[2048,1024]{1,0:T(8,128)(2,1)} async-done(((bf16[128,1024]{1,0:T(8,128)(2,1)}), bf16[2048,1024]{1,0:T(8,128)(2,1)}) %all-gather.3.cloned.1.call-update) | async-done | bytes 4194320 | tf_op jit(solution)/shard_map/all_gather | solution.py:92
  192.3 4.8 %convolution_bitcast_fusion = f32[320,1024]{1,0:T(8,128)} fusion(bf16[16,128,320]{1,2,0:T(8,128)(2,1)S(1)} %copy-done, bf16[16,128,1024]{2,1,0:T(8,128)(2,1)} %bitcast.181), kind=kOutput, calls=%fused_computation.34 | convolution fusion | flops 1342177280 | bytes 6815744 | tf_op jit(solution)/shard_map/dot_general | solution.py:90
  197.0 61.4 %fusion = f32[24,1024]{1,0:T(8,128)S(1)} fusion(f32[320,1024]{1,0:T(8,128)} %convolution_bitcast_fusion), kind=kCustom, calls=%all-reduce-scatter | all-reduce-scatter fusion | flops 393217 | bytes 1410048
  258.4 6.7 %collective-permute-start.7 = (f32[24,1024]{1,0:T(8,128)S(1)}, f32[24,1024]{1,0:T(8,128)S(1)}, u32[]{:S(2)}, u32[]{:S(2)}) collective-permute-start(f32[24,1024]{1,0:T(8,128)S(1)} %fusion), channel_id=1, source_target_pairs={{0,2},{1,3},{2,4},{3,5},{4,6},{5,7},{6,8},{7,9},{8,10},{9,11},{10,... | collective-permute-start | bytes 294920
  265.1 9.5 %collective-permute-start.6 = (f32[24,1024]{1,0:T(8,128)S(1)}, f32[24,1024]{1,0:T(8,128)S(1)}, u32[]{:S(2)}, u32[]{:S(2)}) collective-permute-start(f32[24,1024]{1,0:T(8,128)S(1)} %fusion), channel_id=1, source_target_pairs={{0,1},{1,2},{2,3},{3,4},{4,5},{5,6},{6,7},{7,8},{8,9},{9,10},{10,1... | collective-permute-start | bytes 294920
  274.6 1.9 collective-permute-start.8
  276.5 1.2 maximum_bitcast_fusion
  277.7 7.3 %collective-permute-done.8 = f32[12,1024]{1,0:T(8,128)S(1)} collective-permute-done((f32[12,1024]{1,0:T(8,128)S(1)}, f32[12,1024]{1,0:T(8,128)S(1)}, u32[]{:S(2)}, u32[]{:S(2)}) %collective-permute-start.8) | collective-permute-done | bytes 49184
  285.5 0.7 constant_dynamic-slice_fusion
  (55 shorter events, 2.7 us)
Async XLA Ops:
  7.2 185.1 %copy-start = (bf16[16,128,320]{1,2,0:T(8,128)(2,1)S(1)}, bf16[16,128,320]{1,2,0:T(8,128)(2,1)}, u32[]{:S(2)}) copy-start(bf16[16,128,320]{1,2,0:T(8,128)(2,1)} %param.8) | copy-start | bytes 3932164
  7.2 185.1 %all-gather.3.cloned.1.call-start = ((), (), s32[]{:S(2)}) async-start(), calls=%async_computation | async-start | bytes 4456448 | tf_op jit(solution)/shard_map/all_gather | solution.py:92
  9.1 19.7 %collective-permute-start.1 = (bf16[128,1024]{0,1:T(8,128)(2,1)}, bf16[128,1024]{0,1:T(8,128)(2,1)}, u32[]{:S(2)}, u32[]{:S(2)}) collective-permute-start(bf16[128,1024]{0,1:T(8,128)(2,1)} %bitcast.4), channel_id=1, source_target_pairs={{0,1},{1,2},{2,3},{3,4},{4,5},{5,6},{6,7},{7,8},{8,9},{9,10},{10,1... | collective-permute-start | bytes 786440 | tf_op jit(solution)/shard_map/ppermute | solution.py:18
  18.5 17.7 %collective-permute-start = (bf16[128,1024]{0,1:T(8,128)(2,1)}, bf16[128,1024]{0,1:T(8,128)(2,1)}, u32[]{:S(2)}, u32[]{:S(2)}) collective-permute-start(bf16[128,1024]{0,1:T(8,128)(2,1)} %bitcast.4), channel_id=1, source_target_pairs={{0,2},{1,3},{2,4},{3,5},{4,6},{5,7},{6,8},{7,9},{8,10},{9,11},{10,... | collective-permute-start | bytes 786440 | tf_op jit(solution)/shard_map/ppermute | solution.py:18
  21.3 2.5 copy-start.13
  28.2 9.2 %copy-start.12 = (bf16[1,1,128,2560]{2,3,1,0:T(8,128)(2,1)S(1)}, bf16[1,1,128,2560]{2,3,1,0:T(8,128)(2,1)}, u32[]{:S(2)}) copy-start(bf16[1,1,128,2560]{2,3,1,0:T(8,128)(2,1)} %copy.153) | copy-start | bytes 1966084
  28.6 16.4 %copy-start.6 = (bf16[1,1,128,2560]{2,3,1,0:T(8,128)(2,1)}, bf16[1,1,128,2560]{2,3,1,0:T(8,128)(2,1)S(1)}, u32[]{:S(2)}) copy-start(bf16[1,1,128,2560]{2,3,1,0:T(8,128)(2,1)S(1)} %copy.154) | copy-start | bytes 1966084
  28.8 11.9 %copy-start.14 = (pred[128,384]{0,1:T(8,128)(4,1)}, pred[128,384]{0,1:T(8,128)(4,1)S(1)}, u32[]{:S(2)}) copy-start(pred[128,384]{0,1:T(8,128)(4,1)S(1)} %compare_and_fusion) | copy-start | bytes 147460
  37.4 3.2 %copy-start.9 = (bf16[384,512]{0,1:T(8,128)(2,1)}, bf16[384,512]{0,1:T(8,128)(2,1)S(1)}, u32[]{:S(2)}) copy-start(bf16[384,512]{0,1:T(8,128)(2,1)S(1)} %get-tuple-element.12) | copy-start | bytes 1179652
  37.5 7.5 %copy-start.10 = (bf16[384,512]{0,1:T(8,128)(2,1)}, bf16[384,512]{0,1:T(8,128)(2,1)S(1)}, u32[]{:S(2)}) copy-start(bf16[384,512]{0,1:T(8,128)(2,1)S(1)} %get-tuple-element.11) | copy-start | bytes 1179652
  43.3 2.4 copy-start.8
  57.4 35.4 %collective-permute-start.4 = (bf16[128,1024]{1,0:T(8,128)(2,1)}, bf16[128,1024]{1,0:T(8,128)(2,1)S(1)}, u32[]{:S(2)}, u32[]{:S(2)}) collective-permute-start(bf16[128,1024]{1,0:T(8,128)(2,1)} %get-tuple-element.9), channel_id=1, source_target_pairs={{2,0},{3,1},{4,2},{5,3},{6,4},{7,5},{8,6},{9,7},{10,8},{11,9},{12,... | collective-permute-start | bytes 786440 | tf_op jit(solution)/shard_map/ppermute | solution.py:18
  65.1 27.7 %collective-permute-start.5 = (bf16[128,1024]{1,0:T(8,128)(2,1)}, bf16[128,1024]{1,0:T(8,128)(2,1)}, u32[]{:S(2)}, u32[]{:S(2)}) collective-permute-start(bf16[128,1024]{1,0:T(8,128)(2,1)} %get-tuple-element.10), channel_id=1, source_target_pairs={{1,0},{2,1},{3,2},{4,3},{5,4},{6,5},{7,6},{8,7},{9,8},{10,9},{11,1... | collective-permute-start | bytes 786440 | tf_op jit(solution)/shard_map/ppermute | solution.py:18
  72.1 2.7 copy-start.5
  72.1 2.7 copy-start.11
  74.8 2.2 copy-start.7
  87.0 24.6 %copy-start.1 = (f32[384,512]{1,0:T(8,128)S(1)}, f32[384,512]{1,0:T(8,128)}, u32[]{:S(2)}) copy-start(f32[384,512]{1,0:T(8,128)} %copy.108) | copy-start | bytes 2359300
  87.0 24.6 %copy-start.2 = (f32[384,512]{1,0:T(8,128)S(1)}, f32[384,512]{1,0:T(8,128)}, u32[]{:S(2)}) copy-start(f32[384,512]{1,0:T(8,128)} %copy.107) | copy-start | bytes 2359300
  87.0 24.6 %copy-start.3 = (f32[384,512]{1,0:T(8,128)S(1)}, f32[384,512]{1,0:T(8,128)}, u32[]{:S(2)}) copy-start(f32[384,512]{1,0:T(8,128)} %copy.104) | copy-start | bytes 2359300
  87.0 24.6 %copy-start.4 = (f32[384,512]{1,0:T(8,128)S(1)}, f32[384,512]{1,0:T(8,128)}, u32[]{:S(2)}) copy-start(f32[384,512]{1,0:T(8,128)} %copy.103) | copy-start | bytes 2359300
  88.7 16.2 %collective-permute-start.2 = (bf16[128,1024]{1,0:T(8,128)(2,1)S(1)}, bf16[128,1024]{1,0:T(8,128)(2,1)S(1)}, u32[]{:S(2)}, u32[]{:S(2)}) collective-permute-start(bf16[128,1024]{1,0:T(8,128)(2,1)S(1)} %get-tuple-element.7), channel_id=1, source_target_pairs={{2,0},{3,1},{4,2},{5,3},{6,4},{7,5},{8,6},{9,7},{10,8},{11,9},{12,... | collective-permute-start | bytes 786440 | tf_op jit(solution)/shard_map/ppermute | solution.py:18
  90.6 22.9 %copy-start.15 = (u32[256]{0:T(256)S(1)}, u32[256]{0:T(256)}, u32[]{:S(2)}) copy-start(u32[256]{0:T(256)} %constant.32) | copy-start | bytes 3076
  90.7 20.9 %collective-permute-start.3 = (bf16[128,1024]{1,0:T(8,128)(2,1)S(1)}, bf16[128,1024]{1,0:T(8,128)(2,1)S(1)}, u32[]{:S(2)}, u32[]{:S(2)}) collective-permute-start(bf16[128,1024]{1,0:T(8,128)(2,1)S(1)} %get-tuple-element.8), channel_id=1, source_target_pairs={{1,0},{2,1},{3,2},{4,3},{5,4},{6,5},{7,6},{8,7},{9,8},{10,9},{11,1... | collective-permute-start | bytes 786440 | tf_op jit(solution)/shard_map/ppermute | solution.py:18
  258.4 26.6 %collective-permute-start.7 = (f32[24,1024]{1,0:T(8,128)S(1)}, f32[24,1024]{1,0:T(8,128)S(1)}, u32[]{:S(2)}, u32[]{:S(2)}) collective-permute-start(f32[24,1024]{1,0:T(8,128)S(1)} %fusion), channel_id=1, source_target_pairs={{0,2},{1,3},{2,4},{3,5},{4,6},{5,7},{6,8},{7,9},{8,10},{9,11},{10,... | collective-permute-start | bytes 294920
  265.1 19.9 %collective-permute-start.6 = (f32[24,1024]{1,0:T(8,128)S(1)}, f32[24,1024]{1,0:T(8,128)S(1)}, u32[]{:S(2)}, u32[]{:S(2)}) collective-permute-start(f32[24,1024]{1,0:T(8,128)S(1)} %fusion), channel_id=1, source_target_pairs={{0,1},{1,2},{2,3},{3,4},{4,5},{5,6},{6,7},{7,8},{8,9},{9,10},{10,1... | collective-permute-start | bytes 294920
  274.6 10.4 %collective-permute-start.8 = (f32[12,1024]{1,0:T(8,128)S(1)}, f32[12,1024]{1,0:T(8,128)S(1)}, u32[]{:S(2)}, u32[]{:S(2)}) collective-permute-start(f32[12,1024]{1,0:T(8,128)S(1)} %slice.64), channel_id=1, source_target_pairs={{0,3},{1,4},{2,5},{3,6},{4,7},{5,8},{6,9},{7,10},{8,11},{9,12},{10... | collective-permute-start | bytes 147464
Sparse Core Ops, SparseCore 0:
  113.7 78.5 all-gather.2
where the time goes:
time: 294 us; the launch traced here: 293 us
  waiting for transfers between devices  105 us (36%)
  blocking collectives  61.4 us (21%)
  starting transfers between devices  43.7 us (15%)
  matrix products  31.7 us (11%)
  local copies, waits for them, and re-layouts  23.3 us (8%)
  between operations  15.1 us (5%)
  other arithmetic  13.3 us (5%)
    all_gather x1, waiting for transfers between devices, on_device(): lax.all_gather(kv_grad[None], 'dp', axis=0, tiled=True)  71.2 us
    unnamed x1, blocking collectives  61.4 us
    ppermute x6, waiting for transfers between devices, from_behind(): return lax.ppermute(value, axis, pairs)  26.1 us
    ppermute x6, starting transfers between devices, from_behind(): return lax.ppermute(value, axis, pairs)  25.6 us
    unnamed x3, starting transfers between devices  18.1 us
    unnamed x41, local copies, waits for them, and re-layouts  8.45 us
    sub x2, matrix products, window_grads(): probs = jax.nn.softmax(scores, axis=-1)  7.61 us
    unnamed x4, waiting for transfers between devices  7.31 us
  transfers between devices with their start and end apart: 10, of which 5 were waited for; matrix products, arithmetic and copies ran while one was open for 13% of the time, Pallas kernels for 0%

commit v1 on v0

v1 whole, which is shorter than its diff:
```python
import functools
import math

import jax
import jax.numpy as jnp
from jax import lax
from jax.experimental import pallas as pl
from jax.experimental.pallas import tpu as pltpu
from jax.sharding import Mesh, PartitionSpec as P

KV_HEADS = 4
GROUP = 5
HEAD_DIM = 128
LAYERS = 2
TOK = 128
FACTOR = 1.0 / math.sqrt(HEAD_DIM)
AXES = ("zl", "y", "x", "zh", "core")
SIZES = {"zl": 4, "y": 4, "x": 4, "zh": 2, "core": 2}
GATHER = "zl"
SPREAD = "y"


def shift(value, axis, by):
    size = SIZES[axis]
    return lax.ppermute(value, axis, [(i, (i + by) % size) for i in range(size)])


def ctx_shift(value, by):
    pairs = [(i, i + by) for i in range(16) if 0 <= i + by < 16]
    return lax.ppermute(value, ("x", "zh", "core"), pairs)


def attention_kernel(bias_ref, q_ref, do_ref, k0_ref, k1_ref, k2_ref, v0_ref, v1_ref, v2_ref, dq_ref, own_ref, one_ref, two_ref):
    keys = jnp.concatenate([k0_ref[...], k1_ref[...], k2_ref[...]], axis=0)
    values = jnp.concatenate([v0_ref[...], v1_ref[...], v2_ref[...]], axis=0)
    keys_t = keys.T
    bias = jnp.concatenate([bias_ref[...]] * LAYERS, axis=1)
    shape = (TOK, LAYERS * TOK)
    key_at = lax.broadcasted_iota(jnp.int32, shape, 0)
    query_at = lax.broadcasted_iota(jnp.int32, shape, 1) % TOK
    lower = key_at <= query_at
    lower_b = lower.astype(jnp.float32).astype(jnp.bfloat16)
    upper_b = 1 - lower_b
    nt = (((1,), (1,)), ((), ()))
    dk = jnp.zeros((3 * TOK, HEAD_DIM), jnp.float32)
    dv = jnp.zeros((3 * TOK, HEAD_DIM), jnp.float32)
    for g in range(GROUP):
        cols = slice(g * HEAD_DIM, (g + 1) * HEAD_DIM)
        q = jnp.concatenate([q_ref[0, :, cols], q_ref[1, :, cols]], axis=0)
        do = jnp.concatenate([do_ref[0, :, cols], do_ref[1, :, cols]], axis=0)
        s = lax.dot_general(keys, q, nt, preferred_element_type=jnp.float32)
        dp = lax.dot_general(values, do, nt, preferred_element_type=jnp.float32)
        s = jnp.concatenate([jnp.where(lower, s[:TOK], s[2 * TOK :]), s[TOK : 2 * TOK]], axis=0)
        dp = jnp.concatenate([jnp.where(lower, dp[:TOK], dp[2 * TOK :]), dp[TOK : 2 * TOK]], axis=0)
        s = s * (FACTOR * math.log2(math.e)) + bias
        e = jnp.exp2(s - jnp.max(s, axis=0, keepdims=True))
        p = e * (1.0 / jnp.sum(e, axis=0, keepdims=True))
        delta = jnp.sum(p * dp, axis=0, keepdims=True)
        ds = (p * (dp - delta)).astype(jnp.bfloat16)
        p = p.astype(jnp.bfloat16)
        p = jnp.concatenate([p[:TOK] * lower_b, p[TOK:], p[:TOK] * upper_b], axis=0)
        ds = jnp.concatenate([ds[:TOK] * lower_b, ds[TOK:], ds[:TOK] * upper_b], axis=0)
        dv += jnp.dot(p, do, preferred_element_type=jnp.float32)
        dk += jnp.dot(ds, q, preferred_element_type=jnp.float32)
        dq = jnp.dot(keys_t, ds, preferred_element_type=jnp.float32) * FACTOR
        dq = dq.astype(jnp.bfloat16).T
        dq_ref[0, :, cols] = dq[:TOK]
        dq_ref[1, :, cols] = dq[TOK:]
    dk = dk * FACTOR
    both = jnp.concatenate([dk, dv], axis=1)
    own_ref[...] = both[:TOK]
    one_ref[...] = both[TOK : 2 * TOK].astype(jnp.bfloat16)
    two_ref[...] = both[2 * TOK :].astype(jnp.bfloat16)


def attention(bias, queries, grad_out, kv0, kv1, kv2):
    wide = GROUP * HEAD_DIM
    rows = pl.BlockSpec((LAYERS, TOK, wide), lambda h: (0, 0, h))
    key_cols = pl.BlockSpec((TOK, HEAD_DIM), lambda h: (0, h))
    value_cols = pl.BlockSpec((TOK, HEAD_DIM), lambda h: (0, KV_HEADS + h))
    pair = pl.BlockSpec((TOK, 2 * HEAD_DIM), lambda h: (0, h))
    full = (TOK, KV_HEADS * 2 * HEAD_DIM)
    return pl.pallas_call(
        attention_kernel,
        grid=(KV_HEADS,),
        in_specs=[pl.BlockSpec((2 * TOK, TOK), lambda h: (0, 0)), rows, rows] + [key_cols] * 3 + [value_cols] * 3,
        out_specs=[rows, pair, pair, pair],
        out_shape=[
            jax.ShapeDtypeStruct(queries.shape, jnp.bfloat16),
            jax.ShapeDtypeStruct(full, jnp.float32),
            jax.ShapeDtypeStruct(full, jnp.bfloat16),
            jax.ShapeDtypeStruct(full, jnp.bfloat16),
        ],
        compiler_params=pltpu.CompilerParams(vmem_limit_bytes=32 * 1024 * 1024),
        cost_estimate=pl.CostEstimate(flops=6_000_000_000, bytes_accessed=9_000_000, transcendentals=1_400_000),
        name="attention",
    )(bias, queries, grad_out, kv0, kv1, kv2, kv0, kv1, kv2)


def mask_bias(position, lengths):
    ends = jnp.cumsum(lengths)
    own = jnp.arange(TOK, dtype=jnp.int32)

    def doc(pos):
        return jnp.sum((pos[:, None] >= ends[None, :]).astype(jnp.int32), axis=1)

    query_doc = doc(position + own)
    zero, one, two = ((position - back * TOK + own) for back in (0, 1, 2))
    lower = own[:, None] <= own[None, :]
    seen = [(pos >= 0)[:, None] & (doc(pos)[:, None] == query_doc[None, :]) for pos in (zero, one, two)]
    seen = jnp.concatenate([jnp.where(lower, seen[0], seen[2]), seen[1]], axis=0)
    return jnp.where(seen, 0.0, -jnp.inf).astype(jnp.float32)


def pick(value, index, axis):
    return lax.dynamic_index_in_dim(value, index, axis, keepdims=False)


def spread_hidden(hidden):
    me = lax.axis_index(SPREAD)
    parts = hidden.reshape(4, 4, TOK, 320)
    axis = 1 if SPREAD == "y" else 0
    got = [pick(parts, me, axis)]
    for by in (1, 2, 3):
        got.append(shift(pick(parts, (me + by) % 4, axis), SPREAD, by))
    other = [shift(part, "core", 1) for part in got]
    return got, other


def total(parts):
    acc = parts[0].astype(jnp.float32)
    for part in parts[1:]:
        acc = acc + part.astype(jnp.float32)
    return acc


def on_device(queries, keys_values, grad_out, hidden_kv, doc_lengths):
    core = lax.axis_index("core")
    zh = lax.axis_index("zh")
    x = lax.axis_index("x")
    me = lax.axis_index(SPREAD)
    position = ((x * 2 + zh) * 2 + core) * TOK
    kv0 = keys_values[0]
    kv2 = ctx_shift(kv0, 2)
    kv1 = shift(jnp.where(core == 1, kv2, kv0), "core", 1)
    bias = mask_bias(position, doc_lengths[0])
    hidden_own, hidden_other = spread_hidden(hidden_kv)
    dq, own, one, two = attention(bias, queries[:, 0], grad_out[:, 0], kv0, kv1, kv2)

    one = shift(one, "core", 1)
    is_first = core == 0
    back = jnp.where(is_first, two, (two.astype(jnp.float32) + one.astype(jnp.float32)).astype(jnp.bfloat16))
    back = ctx_shift(back, -2)
    kv_grad = (own + back.astype(jnp.float32) + jnp.where(is_first, one.astype(jnp.float32), 0.0)).astype(jnp.bfloat16)
    heads = kv_grad.reshape(TOK, KV_HEADS, 2, HEAD_DIM)
    kv_out = heads.transpose(0, 2, 1, 3).reshape(TOK, 2 * KV_HEADS * HEAD_DIM)

    lo, hi = kv_grad[:, :512], kv_grad[:, 512:]
    mine = jnp.where(is_first, lo, hi)
    theirs = shift(jnp.where(is_first, hi, lo), "core", 1)
    block = jnp.concatenate([mine, theirs], axis=0)
    at = lax.axis_index(GATHER)
    gathered = [block] + [shift(block, GATHER, by) for by in (1, 2, 3)]

    acc = 0.0
    own_all = jnp.stack(hidden_own)
    other_all = jnp.stack(hidden_other)
    for by in range(4):
        seq = (at - by) % 4
        states = jnp.concatenate([pick(own_all, seq, 1), pick(other_all, seq, 1)], axis=1)
        acc = acc + lax.dot_general(states, gathered[by], (((1,), (0,)), ((), ())), preferred_element_type=jnp.float32)
    partial = acc.astype(jnp.bfloat16).reshape(4, 4, 80, 512)
    got = [pick(partial, x, 1)] + [shift(pick(partial, (x + by) % 4, 1), "x", by) for by in (1, 2, 3)]
    partial = total(got).astype(jnp.bfloat16)
    got = [partial[0]] + [shift(partial[by], SPREAD, -by) for by in (1, 2, 3)]
    partial = total(got).astype(jnp.bfloat16).reshape(2, 2, 20, 512)
    here, there = pick(partial, zh, 0), pick(partial, 1 - zh, 0)
    mine_here, mine_there = pick(here, core, 0), pick(there, core, 0)
    next_here, next_there = pick(here, 1 - core, 0), pick(there, 1 - core, 0)
    corner = lax.ppermute(next_there, ("zh", "core"), [(0, 3), (1, 2), (2, 1), (3, 0)])
    my_cols = total([mine_here, shift(mine_there, "zh", 1)])
    other_cols = total([shift(next_here, "core", 1), corner])
    cols = jnp.concatenate([jnp.where(is_first, my_cols, other_cols), jnp.where(is_first, other_cols, my_cols)], axis=1)
    weight = cols.reshape(20, KV_HEADS, 2, HEAD_DIM).transpose(0, 2, 1, 3).reshape(20, 2 * KV_HEADS * HEAD_DIM)
    return dq[:, None], kv_out[None], weight


def solution(mesh):
    fine = Mesh(mesh.devices.reshape(4, 4, 4, 2, 2), AXES)
    dp, ctx = ("zl", "y"), ("x", "zh", "core")
    placed = (
        P(None, dp, ctx, None),
        P(dp, ctx, None),
        P(None, dp, ctx, None),
        P(None, ctx, dp),
        P(dp, None),
    )
    return jax.shard_map(
        on_device,
        mesh=fine,
        in_specs=placed,
        out_specs=(P(None, dp, ctx, None), P(dp, ctx, None), P(dp + ctx, None)),
        check_vma=False,
    )
```

time: 294 us -> 127 us (0.43)
  the two profiles are of different devices: /device:TPU:3 before, /device:TPU:34 now
where the time goes in v1:
time: 127 us
  waiting for transfers between devices  52.8 us (42%)
  starting transfers between devices  51.2 us (40%)
  Pallas kernels  11.5 us (9%)
  local copies, waits for them, and re-layouts  6.14 us (5%)
  other arithmetic  2.46 us (2%)
  matrix products  2.01 us (2%)
    ppermute x21, waiting for transfers between devices, shift(): lax.ppermute(value, axis, [(i, (i + by) % size) for i in range(size)])  45.9 us
    ppermute x21, starting transfers between devices, shift(): lax.ppermute(value, axis, [(i, (i + by) % size) for i in range(size)])  32.6 us
    ppermute x2, starting transfers between devices, ctx_shift(): return lax.ppermute(value, ('x', 'zh', 'core'), pairs)  15.6 us
    pallas_call x1, Pallas kernels, attention(): pl.pallas_call(attention_kernel, grid=(KV_HEADS,), in_specs=[pl.BlockSpec...  11.5 us
    ppermute x2, waiting for transfers between devices, ctx_shift(): return lax.ppermute(value, ('x', 'zh', 'core'), pairs)  6.96 us
    ppermute x1, starting transfers between devices, on_device(): lax.ppermute(next_there, ('zh', 'core'), [(0, 3), (1, 2), (2, 1), (3, 0)])  3.01 us
  transfers between devices with their start and end apart: 24, of which 14 were waited for; matrix products, arithmetic and copies ran while one was open for 6% of the time, Pallas kernels for 9%

profile of v1, /device:TPU:34, one launch (start us, length us, event | category | flops | bytes accessed | tf_op | source)
XLA Modules:
  0.0 127.1 jit_solution(4297172223736452127)
XLA Ops:
  0.6 8.2 %collective-permute-start = (bf16[128,1024]{1,0:T(8,128)(2,1)}, bf16[128,1024]{1,0:T(8,128)(2,1)S(1)}, u32[]{:S(2)}, u32[]{:S(2)}) collective-permute-start(bf16[128,1024]{1,0:T(8,128)(2,1)} %bitcast.93), channel_id=1, source_target_pairs={{0,2},{1,3},{2,4},{3,5},{4,6},{5,7},{6,8},{7,9},{8,10},{9,11},{10,... | collective-permute-start | bytes 786440 | tf_op jit(solution)/shard_map/ppermute | solution.py:30
  8.9 2.5 %dynamic-slice_bitcast_fusion.15 = (bf16[1,4,128,320]{2,3,1,0:T(8,128)(2,1)S(1)}, bf16[4,128,320]{1,2,0:T(8,128)(2,1)S(1)}, bf16[4,128,320]{1,2,0:T(8,128)(2,1)}...) fusion(bf16[4,4,128,320]{2,3,1,0:T(8,128)(2,1)} %bitcast.100, s32[]{:T(128)S(6)} %select_n.169, s32[]{:T(128)S(6)} %select_n.175, ...), kind=kLoop, calls=%fused_computation.44 | loop fusion | bytes 2949136 | tf_op jit(solution)/shard_map/stack | solution.py:166
  11.4 3.0 %collective-permute-start.6 = (bf16[4,128,320]{1,2,0:T(8,128)(2,1)}, bf16[4,128,320]{1,2,0:T(8,128)(2,1)}, u32[]{:S(2)}, u32[]{:S(2)}) collective-permute-start(bf16[4,128,320]{1,2,0:T(8,128)(2,1)} %get-tuple-element.39), channel_id=1, source_target_pairs={{0,48},{16,0},{32,16},{48,32},{1,49},{17,1},{33,17},{49,33},{2,50}... | collective-permute-start | bytes 983048 | tf_op jit(solution)/shard_map/ppermute | solution.py:25
  14.4 0.6 collective-permute-start.5
  15.1 1.0 collective-permute-start.4
  16.2 0.1 reduce
  16.4 1.5 %collective-permute-done.k2_ref.v2_ref = bf16[128,1024]{1,0:T(8,128)(2,1)S(1)} collective-permute-done((bf16[128,1024]{1,0:T(8,128)(2,1)}, bf16[128,1024]{1,0:T(8,128)(2,1)S(1)}, u32[]{:S(2)}, u32[]{:S(2)}) %collective-permute-start) | collective-permute-done | bytes 262176 | tf_op jit(solution)/shard_map/ppermute | solution.py:30
  18.1 0.2 fusion.32
  18.3 1.3 %collective-permute-done.1.k1_ref.v1_ref = bf16[128,1024]{1,0:T(8,128)(2,1)S(1)} collective-permute-done((bf16[128,1024]{1,0:T(8,128)(2,1)S(1)}, bf16[128,1024]{1,0:T(8,128)(2,1)S(1)}, u32[]{:S(2)}, u32[]{:S(2)}) %collective-permute-start.1) | collective-permute-done | bytes 262176 | tf_op jit(solution)/shard_map/ppermute | solution.py:25
  19.6 1.3 %copy-done.2 = bf16[2,1,128,2560]{3,2,1,0:T(8,128)(2,1)S(1)} copy-done((bf16[2,1,128,2560]{3,2,1,0:T(8,128)(2,1)S(1)}, bf16[2,1,128,2560]{3,2,1,0:T(8,128)(2,1)}, u32[]{:S(2)}) %copy-start.2) | copy-done | bytes 1310744
  20.9 11.5 %attention.1 = (bf16[2,128,2560]{2,1,0:T(8,128)(2,1)}, f32[128,1024]{1,0:T(8,128)S(1)}, bf16[128,1024]{1,0:T(8,128)(2,1)S(1)}, bf16[128,1024]{1,0:T(8,128)(2,1)S(1)}) custom-call(f32[256,128]{1,0:T(8,128)S(1)} %add_select_fusion.bias_ref, bf16[2,128,2560]{2,1,0:T(8,128)(2,1)S(1)} %bitcast.96, bf16[2,128,2560]{2,1,0:T(8,128)(2,1)S(1)} %bitcast.97, ...), custom_call_target="tpu_custom_call" | custom-call | flops 6000000000 | bytes 9000000 | tf_op jit(solution)/shard_map/attention/pallas_call | solution.py:83
  32.5 0.1 collective-permute-start.2
  32.6 0.4 collective-permute-start.7
  33.0 0.1 collective-permute-start.10
  33.1 0.4 collective-permute-start.9
  33.5 0.1 collective-permute-start.8
  33.6 0.4 collective-permute-done.2
  34.1 7.4 %collective-permute-start.3 = (bf16[128,1024]{1,0:T(8,128)(2,1)S(1)}, bf16[128,1024]{1,0:T(8,128)(2,1)S(1)}, u32[]{:S(2)}, u32[]{:S(2)}) collective-permute-start(bf16[128,1024]{1,0:T(8,128)(2,1)S(1)} %fusion.24), channel_id=1, source_target_pairs={{2,0},{3,1},{4,2},{5,3},{6,4},{7,5},{8,6},{9,7},{10,8},{11,9},{12,... | collective-permute-start | bytes 786440 | tf_op jit(solution)/shard_map/ppermute | solution.py:30
  41.5 1.3 %pad_maximum_fusion = bf16[4,4,128,320]{2,3,1,0:T(8,128)(2,1)S(1)} fusion(bf16[1,4,128,320]{2,3,1,0:T(8,128)(2,1)} %bitcast.14, bf16[1,4,128,320]{2,3,1,0:T(8,128)(2,1)} %bitcast.12, bf16[1,4,128,320]{2,3,1,0:T(8,128)(2,1)} %bitcast.10, bf16[1,4,128,320]{2,3,1,0:T(8,128)(2,1)S(1)} %get-tuple-element.37), kind=kLoop, calls=%fused_computation.1 | loop fusion | flops 1966080 | bytes 2621440 | tf_op jit(solution)/shard_map/stack | solution.py:166
  42.9 5.4 %collective-permute-done.3 = bf16[128,1024]{1,0:T(8,128)(2,1)S(1)} collective-permute-done((bf16[128,1024]{1,0:T(8,128)(2,1)S(1)}, bf16[128,1024]{1,0:T(8,128)(2,1)S(1)}, u32[]{:S(2)}, u32[]{:S(2)}) %collective-permute-start.3) | collective-permute-done | bytes 262176 | tf_op jit(solution)/shard_map/ppermute | solution.py:30
  48.6 0.2 pad_maximum_fusion.1
  48.8 1.1 collective-permute-done.11
  49.9 11.1 %collective-permute-start.13 = (bf16[256,512]{1,0:T(8,128)(2,1)S(1)}, bf16[256,512]{1,0:T(8,128)(2,1)S(1)}, u32[]{:S(2)}, u32[]{:S(2)}) collective-permute-start(bf16[256,512]{1,0:T(8,128)(2,1)S(1)} %pad_maximum_fusion.2), channel_id=1, source_target_pairs={{0,128},{64,192},{128,0},{192,64},{1,129},{65,193},{129,1},{193,65... | collective-permute-start | bytes 786440 | tf_op jit(solution)/shard_map/ppermute | solution.py:25
  61.2 2.0 %collective-permute-start.14 = (bf16[256,512]{1,0:T(8,128)(2,1)S(1)}, bf16[256,512]{1,0:T(8,128)(2,1)S(1)}, u32[]{:S(2)}, u32[]{:S(2)}) collective-permute-start(bf16[256,512]{1,0:T(8,128)(2,1)S(1)} %pad_maximum_fusion.2), channel_id=1, source_target_pairs={{0,192},{64,0},{128,64},{192,128},{1,193},{65,1},{129,65},{193,129... | collective-permute-start | bytes 786440 | tf_op jit(solution)/shard_map/ppermute | solution.py:25
  63.2 0.5 fusion
  63.7 9.8 %collective-permute-done.13 = bf16[256,512]{1,0:T(8,128)(2,1)S(1)} collective-permute-done((bf16[256,512]{1,0:T(8,128)(2,1)S(1)}, bf16[256,512]{1,0:T(8,128)(2,1)S(1)}, u32[]{:S(2)}, u32[]{:S(2)}) %collective-permute-start.13) | collective-permute-done | bytes 262176 | tf_op jit(solution)/shard_map/ppermute | solution.py:25
  73.4 0.5 fusion.8
  73.9 9.8 %collective-permute-done.12 = bf16[256,512]{1,0:T(8,128)(2,1)S(1)} collective-permute-done((bf16[256,512]{1,0:T(8,128)(2,1)S(1)}, bf16[256,512]{1,0:T(8,128)(2,1)S(1)}, u32[]{:S(2)}, u32[]{:S(2)}) %collective-permute-start.12) | collective-permute-done | bytes 262176 | tf_op jit(solution)/shard_map/ppermute | solution.py:25
  83.7 0.5 fusion.4
  84.2 0.5 add_convert_fusion
  84.9 2.9 %collective-permute-start.16 = (bf16[4,80,512]{2,1,0:T(8,128)(2,1)S(1)}, bf16[4,80,512]{2,1,0:T(8,128)(2,1)S(1)}, u32[]{:S(2)}, u32[]{:S(2)}) collective-permute-start(bf16[4,80,512]{2,1,0:T(8,128)(2,1)S(1)} %get-tuple-element.28), channel_id=1, source_target_pairs={{0,8},{4,12},{8,0},{12,4},{1,9},{5,13},{9,1},{13,5},{2,10},{6,14},... | collective-permute-start | bytes 983048 | tf_op jit(solution)/shard_map/ppermute | solution.py:25
  87.9 1.3 %collective-permute-start.15 = (bf16[4,80,512]{2,1,0:T(8,128)(2,1)S(1)}, bf16[4,80,512]{2,1,0:T(8,128)(2,1)S(1)}, u32[]{:S(2)}, u32[]{:S(2)}) collective-permute-start(bf16[4,80,512]{2,1,0:T(8,128)(2,1)S(1)} %get-tuple-element.26), channel_id=1, source_target_pairs={{0,4},{4,8},{8,12},{12,0},{1,5},{5,9},{9,13},{13,1},{2,6},{6,10},{... | collective-permute-start | bytes 983048 | tf_op jit(solution)/shard_map/ppermute | solution.py:25
  89.2 5.7 %collective-permute-done.17 = bf16[4,80,512]{2,1,0:T(8,128)(2,1)S(1)} collective-permute-done((bf16[4,80,512]{2,1,0:T(8,128)(2,1)S(1)}, bf16[4,80,512]{2,1,0:T(8,128)(2,1)S(1)}, u32[]{:S(2)}, u32[]{:S(2)}) %collective-permute-start.17) | collective-permute-done | bytes 327712 | tf_op jit(solution)/shard_map/ppermute | solution.py:25
  94.9 7.2 %collective-permute-done.16 = bf16[4,80,512]{2,1,0:T(8,128)(2,1)S(1)} collective-permute-done((bf16[4,80,512]{2,1,0:T(8,128)(2,1)S(1)}, bf16[4,80,512]{2,1,0:T(8,128)(2,1)S(1)}, u32[]{:S(2)}, u32[]{:S(2)}) %collective-permute-start.16) | collective-permute-done | bytes 327712 | tf_op jit(solution)/shard_map/ppermute | solution.py:25
  102.0 1.0 collective-permute-done.15
  103.1 0.2 fusion.20
  103.3 1.7 %collective-permute-start.20 = (bf16[80,512]{1,0:T(8,128)(2,1)S(1)}, bf16[80,512]{1,0:T(8,128)(2,1)S(1)}, u32[]{:S(2)}, u32[]{:S(2)}) collective-permute-start(bf16[80,512]{1,0:T(8,128)(2,1)S(1)} %get-tuple-element.43), channel_id=1, source_target_pairs={{0,16},{16,32},{32,48},{48,0},{1,17},{17,33},{33,49},{49,1},{2,18}... | collective-permute-start | bytes 245768 | tf_op jit(solution)/shard_map/ppermute | solution.py:25
  104.9 2.9 %collective-permute-start.19 = (bf16[80,512]{1,0:T(8,128)(2,1)S(1)}, bf16[80,512]{1,0:T(8,128)(2,1)S(1)}, u32[]{:S(2)}, u32[]{:S(2)}) collective-permute-start(bf16[80,512]{1,0:T(8,128)(2,1)S(1)} %get-tuple-element.44), channel_id=1, source_target_pairs={{0,32},{16,48},{32,0},{48,16},{1,33},{17,49},{33,1},{49,17},{2,34}... | collective-permute-start | bytes 245768 | tf_op jit(solution)/shard_map/ppermute | solution.py:25
  107.8 1.3 %collective-permute-start.18 = (bf16[80,512]{1,0:T(8,128)(2,1)S(1)}, bf16[80,512]{1,0:T(8,128)(2,1)S(1)}, u32[]{:S(2)}, u32[]{:S(2)}) collective-permute-start(bf16[80,512]{1,0:T(8,128)(2,1)S(1)} %get-tuple-element.42), channel_id=1, source_target_pairs={{0,48},{16,0},{32,16},{48,32},{1,49},{17,1},{33,17},{49,33},{2,50}... | collective-permute-start | bytes 245768 | tf_op jit(solution)/shard_map/ppermute | solution.py:25
  109.2 0.7 collective-permute-done.20
  109.9 1.3 collective-permute-done.19
  111.1 1.1 collective-permute-done.18
  112.4 3.0 %collective-permute-start.23 = (bf16[20,512]{1,0:T(8,128)(2,1)S(1)}, bf16[20,512]{1,0:T(8,128)(2,1)S(1)}, u32[]{:S(2)}, u32[]{:S(2)}) collective-permute-start(bf16[20,512]{1,0:T(8,128)(2,1)S(1)} %get-tuple-element.50), channel_id=1, source_target_pairs={{0,3},{1,2},{2,1},{3,0},{4,7},{5,6},{6,5},{7,4},{8,11},{9,10},{10,... | collective-permute-start | bytes 61448 | tf_op jit(solution)/shard_map/ppermute | solution.py:180
  115.4 3.2 %collective-permute-start.22 = (bf16[20,512]{1,0:T(8,128)(2,1)S(1)}, bf16[20,512]{1,0:T(8,128)(2,1)S(1)}, u32[]{:S(2)}, u32[]{:S(2)}) collective-permute-start(bf16[20,512]{1,0:T(8,128)(2,1)S(1)} %get-tuple-element.51), channel_id=1, source_target_pairs={{0,1},{1,0},{2,3},{3,2},{4,5},{5,4},{6,7},{7,6},{8,9},{9,8},{10,11... | collective-permute-start | bytes 61448 | tf_op jit(solution)/shard_map/ppermute | solution.py:25
  118.7 0.2 reshape.90
  118.9 0.9 broadcast_in_dim_reshape.3
  119.8 6.5 %collective-permute-done.21 = bf16[20,512]{1,0:T(8,128)(2,1)S(1)} collective-permute-done((bf16[20,512]{1,0:T(8,128)(2,1)S(1)}, bf16[20,512]{1,0:T(8,128)(2,1)S(1)}, u32[]{:S(2)}, u32[]{:S(2)}) %collective-permute-start.21) | collective-permute-done | bytes 20512 | tf_op jit(solution)/shard_map/ppermute | solution.py:25
  126.5 0.7 reshape.95
  (47 shorter events, 1.6 us)
Async XLA Ops:
  0.6 17.3 %collective-permute-start = (bf16[128,1024]{1,0:T(8,128)(2,1)}, bf16[128,1024]{1,0:T(8,128)(2,1)S(1)}, u32[]{:S(2)}, u32[]{:S(2)}) collective-permute-start(bf16[128,1024]{1,0:T(8,128)(2,1)} %bitcast.93), channel_id=1, source_target_pairs={{0,2},{1,3},{2,4},{3,5},{4,6},{5,7},{6,8},{7,9},{8,10},{9,11},{10,... | collective-permute-start | bytes 786440 | tf_op jit(solution)/shard_map/ppermute | solution.py:30
  8.9 7.2 %copy-start.3 = (s32[1,16]{1,0:T(1,128)S(1)}, s32[1,16]{1,0:T(1,128)}, u32[]{:S(2)}) copy-start(s32[1,16]{1,0:T(1,128)} %param.9) | copy-start | bytes 196
  8.9 9.0 %copy-start = (bf16[1,128,1024]{2,1,0:T(8,128)(2,1)S(1)}, bf16[1,128,1024]{2,1,0:T(8,128)(2,1)}, u32[]{:S(2)}) copy-start(bf16[1,128,1024]{2,1,0:T(8,128)(2,1)} %param.6) | copy-start | bytes 786436
  8.9 10.7 %copy-start.1 = (bf16[2,1,128,2560]{3,2,1,0:T(8,128)(2,1)S(1)}, bf16[2,1,128,2560]{3,2,1,0:T(8,128)(2,1)}, u32[]{:S(2)}) copy-start(bf16[2,1,128,2560]{3,2,1,0:T(8,128)(2,1)} %param.5) | copy-start | bytes 3932164
  11.4 21.6 %collective-permute-start.6 = (bf16[4,128,320]{1,2,0:T(8,128)(2,1)}, bf16[4,128,320]{1,2,0:T(8,128)(2,1)}, u32[]{:S(2)}, u32[]{:S(2)}) collective-permute-start(bf16[4,128,320]{1,2,0:T(8,128)(2,1)} %get-tuple-element.39), channel_id=1, source_target_pairs={{0,48},{16,0},{32,16},{48,32},{1,49},{17,1},{33,17},{49,33},{2,50}... | collective-permute-start | bytes 983048 | tf_op jit(solution)/shard_map/ppermute | solution.py:25
  14.4 18.7 %collective-permute-start.5 = (bf16[4,128,320]{1,2,0:T(8,128)(2,1)}, bf16[4,128,320]{1,2,0:T(8,128)(2,1)}, u32[]{:S(2)}, u32[]{:S(2)}) collective-permute-start(bf16[4,128,320]{1,2,0:T(8,128)(2,1)} %get-tuple-element.40), channel_id=1, source_target_pairs={{0,32},{16,48},{32,0},{48,16},{1,33},{17,49},{33,1},{49,17},{2,34}... | collective-permute-start | bytes 983048 | tf_op jit(solution)/shard_map/ppermute | solution.py:25
  15.1 18.4 %collective-permute-start.4 = (bf16[4,128,320]{1,2,0:T(8,128)(2,1)}, bf16[4,128,320]{1,2,0:T(8,128)(2,1)}, u32[]{:S(2)}, u32[]{:S(2)}) collective-permute-start(bf16[4,128,320]{1,2,0:T(8,128)(2,1)} %get-tuple-element.41), channel_id=1, source_target_pairs={{0,16},{16,32},{32,48},{48,0},{1,17},{17,33},{33,49},{49,1},{2,18}... | collective-permute-start | bytes 983048 | tf_op jit(solution)/shard_map/ppermute | solution.py:25
  18.0 1.6 %collective-permute-start.1 = (bf16[128,1024]{1,0:T(8,128)(2,1)S(1)}, bf16[128,1024]{1,0:T(8,128)(2,1)S(1)}, u32[]{:S(2)}, u32[]{:S(2)}) collective-permute-start(bf16[128,1024]{1,0:T(8,128)(2,1)S(1)} %broadcast_select_fusion), channel_id=1, source_target_pairs={{0,1},{1,0},{2,3},{3,2},{4,5},{5,4},{6,7},{7,6},{8,9},{9,8},{10,11... | collective-permute-start | bytes 786440 | tf_op jit(solution)/shard_map/ppermute | solution.py:25
  19.6 1.3 %copy-start.2 = (bf16[2,1,128,2560]{3,2,1,0:T(8,128)(2,1)S(1)}, bf16[2,1,128,2560]{3,2,1,0:T(8,128)(2,1)}, u32[]{:S(2)}) copy-start(bf16[2,1,128,2560]{3,2,1,0:T(8,128)(2,1)} %param.7) | copy-start | bytes 3932164
  32.5 1.5 %collective-permute-start.2 = (bf16[128,1024]{1,0:T(8,128)(2,1)S(1)}, bf16[128,1024]{1,0:T(8,128)(2,1)S(1)}, u32[]{:S(2)}, u32[]{:S(2)}) collective-permute-start(bf16[128,1024]{1,0:T(8,128)(2,1)S(1)} %get-tuple-element.10), channel_id=1, source_target_pairs={{0,1},{1,0},{2,3},{3,2},{4,5},{5,4},{6,7},{7,6},{8,9},{9,8},{10,11... | collective-permute-start | bytes 786440 | tf_op jit(solution)/shard_map/ppermute | solution.py:25
  32.6 16.0 %collective-permute-start.7 = (bf16[4,128,320]{1,2,0:T(8,128)(2,1)S(1)}, bf16[4,128,320]{1,2,0:T(8,128)(2,1)S(1)}, u32[]{:S(2)}, u32[]{:S(2)}) collective-permute-start(bf16[4,128,320]{1,2,0:T(8,128)(2,1)S(1)} %get-tuple-element.38), channel_id=1, source_target_pairs={{0,1},{1,0},{2,3},{3,2},{4,5},{5,4},{6,7},{7,6},{8,9},{9,8},{10,11... | collective-permute-start | bytes 983048 | tf_op jit(solution)/shard_map/ppermute | solution.py:25
  33.0 15.6 %collective-permute-start.10 = (bf16[4,128,320]{1,2,0:T(8,128)(2,1)}, bf16[4,128,320]{1,2,0:T(8,128)(2,1)S(1)}, u32[]{:S(2)}, u32[]{:S(2)}) collective-permute-start(bf16[4,128,320]{1,2,0:T(8,128)(2,1)} %collective-permute-done.6), channel_id=1, source_target_pairs={{0,1},{1,0},{2,3},{3,2},{4,5},{5,4},{6,7},{7,6},{8,9},{9,8},{10,11... | collective-permute-start | bytes 983048 | tf_op jit(solution)/shard_map/ppermute | solution.py:25
  33.1 15.5 %collective-permute-start.9 = (bf16[4,128,320]{1,2,0:T(8,128)(2,1)}, bf16[4,128,320]{1,2,0:T(8,128)(2,1)S(1)}, u32[]{:S(2)}, u32[]{:S(2)}) collective-permute-start(bf16[4,128,320]{1,2,0:T(8,128)(2,1)} %collective-permute-done.5), channel_id=1, source_target_pairs={{0,1},{1,0},{2,3},{3,2},{4,5},{5,4},{6,7},{7,6},{8,9},{9,8},{10,11... | collective-permute-start | bytes 983048 | tf_op jit(solution)/shard_map/ppermute | solution.py:25
  33.5 15.1 %collective-permute-start.8 = (bf16[4,128,320]{1,2,0:T(8,128)(2,1)}, bf16[4,128,320]{1,2,0:T(8,128)(2,1)S(1)}, u32[]{:S(2)}, u32[]{:S(2)}) collective-permute-start(bf16[4,128,320]{1,2,0:T(8,128)(2,1)} %collective-permute-done.4), channel_id=1, source_target_pairs={{0,1},{1,0},{2,3},{3,2},{4,5},{5,4},{6,7},{7,6},{8,9},{9,8},{10,11... | collective-permute-start | bytes 983048 | tf_op jit(solution)/shard_map/ppermute | solution.py:25
  34.1 14.2 %collective-permute-start.3 = (bf16[128,1024]{1,0:T(8,128)(2,1)S(1)}, bf16[128,1024]{1,0:T(8,128)(2,1)S(1)}, u32[]{:S(2)}, u32[]{:S(2)}) collective-permute-start(bf16[128,1024]{1,0:T(8,128)(2,1)S(1)} %fusion.24), channel_id=1, source_target_pairs={{2,0},{3,1},{4,2},{5,3},{6,4},{7,5},{8,6},{9,7},{10,8},{11,9},{12,... | collective-permute-start | bytes 786440 | tf_op jit(solution)/shard_map/ppermute | solution.py:30
  48.5 1.4 %collective-permute-start.11 = (bf16[128,512]{1,0:T(8,128)(2,1)S(1)}, bf16[128,512]{1,0:T(8,128)(2,1)S(1)}, u32[]{:S(2)}, u32[]{:S(2)}) collective-permute-start(bf16[128,512]{1,0:T(8,128)(2,1)S(1)} %get-tuple-element.46), channel_id=1, source_target_pairs={{0,1},{1,0},{2,3},{3,2},{4,5},{5,4},{6,7},{7,6},{8,9},{9,8},{10,11... | collective-permute-start | bytes 393224 | tf_op jit(solution)/shard_map/ppermute | solution.py:25
  49.9 23.5 %collective-permute-start.13 = (bf16[256,512]{1,0:T(8,128)(2,1)S(1)}, bf16[256,512]{1,0:T(8,128)(2,1)S(1)}, u32[]{:S(2)}, u32[]{:S(2)}) collective-permute-start(bf16[256,512]{1,0:T(8,128)(2,1)S(1)} %pad_maximum_fusion.2), channel_id=1, source_target_pairs={{0,128},{64,192},{128,0},{192,64},{1,129},{65,193},{129,1},{193,65... | collective-permute-start | bytes 786440 | tf_op jit(solution)/shard_map/ppermute | solution.py:25
  61.1 22.6 %collective-permute-start.12 = (bf16[256,512]{1,0:T(8,128)(2,1)S(1)}, bf16[256,512]{1,0:T(8,128)(2,1)S(1)}, u32[]{:S(2)}, u32[]{:S(2)}) collective-permute-start(bf16[256,512]{1,0:T(8,128)(2,1)S(1)} %pad_maximum_fusion.2), channel_id=1, source_target_pairs={{0,64},{64,128},{128,192},{192,0},{1,65},{65,129},{129,193},{193,1... | collective-permute-start | bytes 786440 | tf_op jit(solution)/shard_map/ppermute | solution.py:25
  61.2 23.1 %collective-permute-start.14 = (bf16[256,512]{1,0:T(8,128)(2,1)S(1)}, bf16[256,512]{1,0:T(8,128)(2,1)S(1)}, u32[]{:S(2)}, u32[]{:S(2)}) collective-permute-start(bf16[256,512]{1,0:T(8,128)(2,1)S(1)} %pad_maximum_fusion.2), channel_id=1, source_target_pairs={{0,192},{64,0},{128,64},{192,128},{1,193},{65,1},{129,65},{193,129... | collective-permute-start | bytes 786440 | tf_op jit(solution)/shard_map/ppermute | solution.py:25
  84.9 10.0 %collective-permute-start.17 = (bf16[4,80,512]{2,1,0:T(8,128)(2,1)S(1)}, bf16[4,80,512]{2,1,0:T(8,128)(2,1)S(1)}, u32[]{:S(2)}, u32[]{:S(2)}) collective-permute-start(bf16[4,80,512]{2,1,0:T(8,128)(2,1)S(1)} %get-tuple-element.27), channel_id=1, source_target_pairs={{0,12},{4,0},{8,4},{12,8},{1,13},{5,1},{9,5},{13,9},{2,14},{6,2},{... | collective-permute-start | bytes 983048 | tf_op jit(solution)/shard_map/ppermute | solution.py:25
  84.9 17.1 %collective-permute-start.16 = (bf16[4,80,512]{2,1,0:T(8,128)(2,1)S(1)}, bf16[4,80,512]{2,1,0:T(8,128)(2,1)S(1)}, u32[]{:S(2)}, u32[]{:S(2)}) collective-permute-start(bf16[4,80,512]{2,1,0:T(8,128)(2,1)S(1)} %get-tuple-element.28), channel_id=1, source_target_pairs={{0,8},{4,12},{8,0},{12,4},{1,9},{5,13},{9,1},{13,5},{2,10},{6,14},... | collective-permute-start | bytes 983048 | tf_op jit(solution)/shard_map/ppermute | solution.py:25
  87.9 15.2 %collective-permute-start.15 = (bf16[4,80,512]{2,1,0:T(8,128)(2,1)S(1)}, bf16[4,80,512]{2,1,0:T(8,128)(2,1)S(1)}, u32[]{:S(2)}, u32[]{:S(2)}) collective-permute-start(bf16[4,80,512]{2,1,0:T(8,128)(2,1)S(1)} %get-tuple-element.26), channel_id=1, source_target_pairs={{0,4},{4,8},{8,12},{12,0},{1,5},{5,9},{9,13},{13,1},{2,6},{6,10},{... | collective-permute-start | bytes 983048 | tf_op jit(solution)/shard_map/ppermute | solution.py:25
  103.3 6.6 %collective-permute-start.20 = (bf16[80,512]{1,0:T(8,128)(2,1)S(1)}, bf16[80,512]{1,0:T(8,128)(2,1)S(1)}, u32[]{:S(2)}, u32[]{:S(2)}) collective-permute-start(bf16[80,512]{1,0:T(8,128)(2,1)S(1)} %get-tuple-element.43), channel_id=1, source_target_pairs={{0,16},{16,32},{32,48},{48,0},{1,17},{17,33},{33,49},{49,1},{2,18}... | collective-permute-start | bytes 245768 | tf_op jit(solution)/shard_map/ppermute | solution.py:25
  104.9 6.2 %collective-permute-start.19 = (bf16[80,512]{1,0:T(8,128)(2,1)S(1)}, bf16[80,512]{1,0:T(8,128)(2,1)S(1)}, u32[]{:S(2)}, u32[]{:S(2)}) collective-permute-start(bf16[80,512]{1,0:T(8,128)(2,1)S(1)} %get-tuple-element.44), channel_id=1, source_target_pairs={{0,32},{16,48},{32,0},{48,16},{1,33},{17,49},{33,1},{49,17},{2,34}... | collective-permute-start | bytes 245768 | tf_op jit(solution)/shard_map/ppermute | solution.py:25
  107.8 4.4 %collective-permute-start.18 = (bf16[80,512]{1,0:T(8,128)(2,1)S(1)}, bf16[80,512]{1,0:T(8,128)(2,1)S(1)}, u32[]{:S(2)}, u32[]{:S(2)}) collective-permute-start(bf16[80,512]{1,0:T(8,128)(2,1)S(1)} %get-tuple-element.42), channel_id=1, source_target_pairs={{0,48},{16,0},{32,16},{48,32},{1,49},{17,1},{33,17},{49,33},{2,50}... | collective-permute-start | bytes 245768 | tf_op jit(solution)/shard_map/ppermute | solution.py:25
  112.4 7.4 %collective-permute-start.23 = (bf16[20,512]{1,0:T(8,128)(2,1)S(1)}, bf16[20,512]{1,0:T(8,128)(2,1)S(1)}, u32[]{:S(2)}, u32[]{:S(2)}) collective-permute-start(bf16[20,512]{1,0:T(8,128)(2,1)S(1)} %get-tuple-element.50), channel_id=1, source_target_pairs={{0,3},{1,2},{2,1},{3,0},{4,7},{5,6},{6,5},{7,4},{8,11},{9,10},{10,... | collective-permute-start | bytes 61448 | tf_op jit(solution)/shard_map/ppermute | solution.py:180
  115.4 4.4 %collective-permute-start.22 = (bf16[20,512]{1,0:T(8,128)(2,1)S(1)}, bf16[20,512]{1,0:T(8,128)(2,1)S(1)}, u32[]{:S(2)}, u32[]{:S(2)}) collective-permute-start(bf16[20,512]{1,0:T(8,128)(2,1)S(1)} %get-tuple-element.51), channel_id=1, source_target_pairs={{0,1},{1,0},{2,3},{3,2},{4,5},{5,4},{6,7},{7,6},{8,9},{9,8},{10,11... | collective-permute-start | bytes 61448 | tf_op jit(solution)/shard_map/ppermute | solution.py:25
  118.6 7.7 %collective-permute-start.21 = (bf16[20,512]{1,0:T(8,128)(2,1)S(1)}, bf16[20,512]{1,0:T(8,128)(2,1)S(1)}, u32[]{:S(2)}, u32[]{:S(2)}) collective-permute-start(bf16[20,512]{1,0:T(8,128)(2,1)S(1)} %get-tuple-element.49), channel_id=1, source_target_pairs={{0,2},{2,0},{1,3},{3,1},{4,6},{6,4},{5,7},{7,5},{8,10},{10,8},{9,1... | collective-permute-start | bytes 61448 | tf_op jit(solution)/shard_map/ppermute | solution.py:25

commit v2 on v1

v2 whole, which is shorter than its diff:
```python
import functools
import math

import jax
import jax.numpy as jnp
from jax import lax
from jax.experimental import pallas as pl
from jax.experimental.pallas import tpu as pltpu
from jax.sharding import Mesh, PartitionSpec as P

KV_HEADS = 4
GROUP = 5
HEAD_DIM = 128
LAYERS = 2
TOK = 128
CHUNKS = 2
PAIR = 2 * HEAD_DIM
FACTOR = 1.0 / math.sqrt(HEAD_DIM)
AXES = ("zl", "y", "x", "zh", "core")
SIZES = {"zl": 4, "y": 4, "x": 4, "zh": 2, "core": 2}


def shift(value, axis, by):
    size = SIZES[axis]
    return lax.ppermute(value, axis, [(i, (i + by) % size) for i in range(size)])


def ctx_shift(value, by):
    pairs = [(i, i + by) for i in range(16) if 0 <= i + by < 16]
    return lax.ppermute(value, ("x", "zh", "core"), pairs)


def z_shift(value, by):
    pairs = []
    for z in range(8):
        to = (z + by) % 8
        pairs.append(((z % 4) * 2 + z // 4, (to % 4) * 2 + to // 4))
    return lax.ppermute(value, ("zl", "zh"), pairs)


def attention_kernel(core_ref, bias_ref, q_ref, do_ref, k0_ref, k1_ref, k2_ref, v0_ref, v1_ref, v2_ref, *rest):
    dq_ref, theirs_ref, mine_ref = rest[-3:]
    keys = jnp.concatenate([k0_ref[...], k1_ref[...], k2_ref[...]], axis=0)
    values = jnp.concatenate([v0_ref[...], v1_ref[...], v2_ref[...]], axis=0)
    keys_t = keys.T
    bias = jnp.concatenate([bias_ref[...]] * LAYERS, axis=1)
    shape = (TOK, LAYERS * TOK)
    key_at = lax.broadcasted_iota(jnp.int32, shape, 0)
    query_at = lax.broadcasted_iota(jnp.int32, shape, 1) % TOK
    lower = key_at <= query_at
    lower_b = lower.astype(jnp.float32).astype(jnp.bfloat16)
    upper_b = 1 - lower_b
    nt = (((1,), (1,)), ((), ()))
    dk = jnp.zeros((3 * TOK, HEAD_DIM), jnp.float32)
    dv = jnp.zeros((3 * TOK, HEAD_DIM), jnp.float32)
    for g in range(GROUP):
        cols = slice(g * HEAD_DIM, (g + 1) * HEAD_DIM)
        q = jnp.concatenate([q_ref[0, :, cols], q_ref[1, :, cols]], axis=0)
        do = jnp.concatenate([do_ref[0, :, cols], do_ref[1, :, cols]], axis=0)
        s = lax.dot_general(keys, q, nt, preferred_element_type=jnp.float32)
        dp = lax.dot_general(values, do, nt, preferred_element_type=jnp.float32)
        s = jnp.concatenate([jnp.where(lower, s[:TOK], s[2 * TOK :]), s[TOK : 2 * TOK]], axis=0)
        dp = jnp.concatenate([jnp.where(lower, dp[:TOK], dp[2 * TOK :]), dp[TOK : 2 * TOK]], axis=0)
        s = s * (FACTOR * math.log2(math.e)) + bias
        e = jnp.exp2(s - jnp.max(s, axis=0, keepdims=True))
        p = e * (1.0 / jnp.sum(e, axis=0, keepdims=True))
        delta = jnp.sum(p * dp, axis=0, keepdims=True)
        ds = (p * (dp - delta)).astype(jnp.bfloat16)
        p = p.astype(jnp.bfloat16)
        p = jnp.concatenate([p[:TOK] * lower_b, p[TOK:], p[:TOK] * upper_b], axis=0)
        ds = jnp.concatenate([ds[:TOK] * lower_b, ds[TOK:], ds[:TOK] * upper_b], axis=0)
        dv += jnp.dot(p, do, preferred_element_type=jnp.float32)
        dk += jnp.dot(ds, q, preferred_element_type=jnp.float32)
        dq = jnp.dot(keys_t, ds, preferred_element_type=jnp.float32) * FACTOR
        dq = dq.astype(jnp.bfloat16).T
        dq_ref[0, :, cols] = dq[:TOK]
        dq_ref[1, :, cols] = dq[TOK:]
    both = jnp.concatenate([dk * FACTOR, dv], axis=1)

    @pl.when(pl.program_id(0) == 0)
    def _():
        theirs_ref[...] = both.astype(jnp.bfloat16)

    @pl.when(pl.program_id(0) == 1)
    def _():
        mine_ref[...] = both


def attention(chunk, core, bias, queries, grad_out, kv0, kv1, kv2, dq):
    wide = GROUP * HEAD_DIM

    def head(i, core_ref):
        return (1 - core_ref[0] + i) % 2

    rows = pl.BlockSpec((LAYERS, TOK, wide), lambda i, c: (0, 0, 2 * chunk + head(i, c)))
    key_cols = pl.BlockSpec((TOK, HEAD_DIM), lambda i, c: (0, head(i, c)))
    value_cols = pl.BlockSpec((TOK, HEAD_DIM), lambda i, c: (0, 2 + head(i, c)))
    whole = pl.BlockSpec((3 * TOK, PAIR), lambda i, c: (0, 0))
    operands = [bias, queries, grad_out, kv0, kv1, kv2, kv0, kv1, kv2]
    in_specs = [pl.BlockSpec((2 * TOK, TOK), lambda i, c: (0, 0)), rows, rows] + [key_cols] * 3 + [value_cols] * 3
    aliases = {}
    if dq is not None:
        operands.append(dq)
        in_specs.append(pl.BlockSpec(memory_space=pl.ANY))
        aliases = {len(operands): 0}
    return pl.pallas_call(
        attention_kernel,
        grid_spec=pltpu.PrefetchScalarGridSpec(
            num_scalar_prefetch=1,
            grid=(2,),
            in_specs=in_specs,
            out_specs=[rows, whole, whole],
        ),
        out_shape=[
            jax.ShapeDtypeStruct(queries.shape, jnp.bfloat16),
            jax.ShapeDtypeStruct((3 * TOK, PAIR), jnp.bfloat16),
            jax.ShapeDtypeStruct((3 * TOK, PAIR), jnp.float32),
        ],
        input_output_aliases=aliases,
        compiler_params=pltpu.CompilerParams(vmem_limit_bytes=32 * 1024 * 1024),
        cost_estimate=pl.CostEstimate(flops=3_000_000_000, bytes_accessed=5_000_000, transcendentals=700_000),
        name="attention",
    )(core[None], *operands)


def mask_bias(position, lengths):
    ends = jnp.cumsum(lengths)
    own = jnp.arange(TOK, dtype=jnp.int32)

    def doc(pos):
        return jnp.sum((pos[:, None] >= ends[None, :]).astype(jnp.int32), axis=1)

    query_doc = doc(position + own)
    zero, one, two = ((position - back * TOK + own) for back in (0, 1, 2))
    lower = own[:, None] <= own[None, :]
    seen = [(pos >= 0)[:, None] & (doc(pos)[:, None] == query_doc[None, :]) for pos in (zero, one, two)]
    seen = jnp.concatenate([jnp.where(lower, seen[0], seen[2]), seen[1]], axis=0)
    return jnp.where(seen, 0.0, -jnp.inf).astype(jnp.float32)


def pick(value, index, axis):
    return lax.dynamic_index_in_dim(value, index, axis, keepdims=False)


def total(parts):
    acc = parts[0].astype(jnp.float32)
    for part in parts[1:]:
        acc = acc + part.astype(jnp.float32)
    return acc


def on_device(queries, keys_values, grad_out, hidden_kv, doc_lengths):
    core, zh, x, y, zl = (lax.axis_index(name) for name in ("core", "zh", "x", "y", "zl"))
    first = core == 0
    position = ((x * 2 + zh) * 2 + core) * TOK
    kv = keys_values[0]
    half = KV_HEADS * HEAD_DIM
    windows = []
    for chunk in range(CHUNKS):
        at = chunk * PAIR
        kv0 = jnp.concatenate([kv[:, at : at + PAIR], kv[:, half + at : half + at + PAIR]], axis=1)
        kv2 = ctx_shift(kv0, 2)
        kv1 = shift(jnp.where(first, kv0, kv2), "core", 1)
        windows.append((kv0, kv1, kv2))
    bias = mask_bias(position, doc_lengths[0])

    hidden, _ = lax.optimization_barrier((hidden_kv, windows[-1][2]))
    hidden = hidden.reshape(4, 4, TOK, 320)
    states = [pick(hidden, zl, 0)] + [shift(pick(hidden, (zl + by) % 4, 0), "zl", by) for by in (1, 2, 3)]
    other_states = [shift(part, "core", 1) for part in states]

    dq = None
    halves = []
    for chunk in range(CHUNKS):
        dq, theirs, mine = attention(chunk, core, bias, queries[:, 0], grad_out[:, 0], *windows[chunk], dq)
        halves.append((mine, shift(theirs, "core", 1).astype(jnp.float32)))

    blocks = []
    for mine, got in halves:
        (m_own, m_one, m_two), (g_own, g_one, g_two) = mine.reshape(3, TOK, PAIR), got.reshape(3, TOK, PAIR)
        back = jnp.concatenate([m_two + jnp.where(first, 0.0, g_one), g_two + jnp.where(first, m_one, 0.0)], axis=0)
        back = ctx_shift(back.astype(jnp.bfloat16), -2).astype(jnp.float32)
        here = jnp.concatenate([m_own + jnp.where(first, g_one, 0.0), g_own + jnp.where(first, 0.0, m_one)], axis=0)
        blocks.append((here + back).astype(jnp.bfloat16))

    reduced = []
    for block in blocks:
        gathered = [block] + [shift(block, "y", by) for by in (1, 2, 3)]
        acc = 0.0
        for by in range(4):
            seq = (y - by) % 4
            rows = jnp.stack([jnp.concatenate([pick(a, seq, 0), pick(b, seq, 0)], axis=0) for a, b in zip(states, other_states)])
            acc = acc + lax.dot_general(rows, gathered[by], (((1,), (0,)), ((), ())), preferred_element_type=jnp.float32)
        partial = acc.astype(jnp.bfloat16).reshape(4, 4, 80, PAIR)
        got = [pick(partial, x, 1)] + [shift(pick(partial, (x + by) % 4, 1), "x", by) for by in (1, 2, 3)]
        reduced.append(total(got).astype(jnp.bfloat16))

    partial = jnp.concatenate(reduced, axis=2).reshape(4, 2, 40, 2 * PAIR)
    got = []
    for by in range(8):
        piece = pick(partial[-by % 4], (zh + (zl + by) // 4) % 2, 0)
        got.append(z_shift(piece, by) if by else piece)
    rows = total(got).reshape(2, 20, 2 * PAIR)
    ours = pick(rows, core, 0)
    others = shift(pick(rows, 1 - core, 0), "core", 1)

    def assemble(own, other):
        count = own.shape[0]
        own = own.reshape(count, CHUNKS, 1, 2, HEAD_DIM)
        other = other.reshape(count, CHUNKS, 1, 2, HEAD_DIM)
        heads = jnp.concatenate([jnp.where(first, own, other), jnp.where(first, other, own)], axis=2)
        return heads.transpose(0, 3, 1, 2, 4).reshape(count, 2 * KV_HEADS * HEAD_DIM)

    weight = assemble(ours, others)
    block = jnp.concatenate(blocks, axis=1)
    kv_out = assemble(block[:TOK], shift(block[TOK:], "core", 1))
    return dq[:, None], kv_out[None], weight


def solution(mesh):
    fine = Mesh(mesh.devices.reshape(4, 4, 4, 2, 2), AXES)
    dp, ctx = ("zl", "y"), ("x", "zh", "core")
    placed = (
        P(None, dp, ctx, None),
        P(dp, ctx, None),
        P(None, dp, ctx, None),
        P(None, ctx, dp),
        P(dp, None),
    )
    return jax.shard_map(
        on_device,
        mesh=fine,
        in_specs=placed,
        out_specs=(P(None, dp, ctx, None), P(dp, ctx, None), P(dp + ctx, None)),
        check_vma=False,
    )
```

time: 127 us -> 143 us (1.13)
  the two profiles are of different devices: /device:TPU:34 before, /device:TPU:3 now
where the time goes in v2:
time: 143 us; the launch traced here: 140 us
  starting transfers between devices  60.3 us (42%)
  waiting for transfers between devices  56.4 us (39%)
  Pallas kernels  12.7 us (9%)
  local copies, waits for them, and re-layouts  4.43 us (3%)
  matrix products  2.74 us (2%)
  other arithmetic  1.9 us (1%)
  between operations  1.74 us (1%)
    ppermute x25, waiting for transfers between devices, shift(): lax.ppermute(value, axis, [(i, (i + by) % size) for i in range(size)])  39.4 us
    ppermute x25, starting transfers between devices, shift(): lax.ppermute(value, axis, [(i, (i + by) % size) for i in range(size)])  26.9 us
    ppermute x4, starting transfers between devices, ctx_shift(): return lax.ppermute(value, ('x', 'zh', 'core'), pairs)  17.8 us
    ppermute x7, starting transfers between devices, z_shift(): return lax.ppermute(value, ('zl', 'zh'), pairs)  15.6 us
    ppermute x4, waiting for transfers between devices, ctx_shift(): return lax.ppermute(value, ('x', 'zh', 'core'), pairs)  12.8 us
    pallas_call x2, Pallas kernels, attention(): pl.pallas_call(attention_kernel, grid_spec=pltpu.PrefetchScalarGridSpec(n...  12.7 us
    ppermute x7, waiting for transfers between devices, z_shift(): return lax.ppermute(value, ('zl', 'zh'), pairs)  4.26 us
  transfers between devices with their start and end apart: 36, of which 12 were waited for; matrix products, arithmetic and copies ran while one was open for 5% of the time, Pallas kernels for 5%

profile of v2, /device:TPU:3, one launch (start us, length us, event | category | flops | bytes accessed | tf_op | source)
XLA Modules:
  0.0 140.2 jit_solution(2146290510823133116)
XLA Ops:
  0.6 1.1 fusion.45
  1.7 8.9 %collective-permute-start = (bf16[128,512]{1,0:T(8,128)(2,1)S(1)}, bf16[128,512]{1,0:T(8,128)(2,1)S(1)}, u32[]{:S(2)}, u32[]{:S(2)}) collective-permute-start(bf16[128,512]{1,0:T(8,128)(2,1)S(1)} %pad_maximum_fusion.5.k0_ref.v0_ref), channel_id=1, source_target_pairs={{0,2},{1,3},{2,4},{3,5},{4,6},{5,7},{6,8},{7,9},{8,10},{9,11},{10,... | collective-permute-start | bytes 393224 | tf_op jit(solution)/shard_map/ppermute | solution.py:30
  10.7 1.9 %collective-permute-start.2 = (bf16[128,512]{1,0:T(8,128)(2,1)S(1)}, bf16[128,512]{1,0:T(8,128)(2,1)S(1)}, u32[]{:S(2)}, u32[]{:S(2)}) collective-permute-start(bf16[128,512]{1,0:T(8,128)(2,1)S(1)} %pad_maximum_fusion.6.k0_ref.v0_ref), channel_id=1, source_target_pairs={{0,2},{1,3},{2,4},{3,5},{4,6},{5,7},{6,8},{7,9},{8,10},{9,11},{10,... | collective-permute-start | bytes 393224 | tf_op jit(solution)/shard_map/ppermute | solution.py:30
  12.8 0.7 copy.26
  14.3 12.8 %collective-permute-done.2.k2_ref.v2_ref = bf16[128,512]{1,0:T(8,128)(2,1)S(1)} collective-permute-done((bf16[128,512]{1,0:T(8,128)(2,1)S(1)}, bf16[128,512]{1,0:T(8,128)(2,1)S(1)}, u32[]{:S(2)}, u32[]{:S(2)}) %collective-permute-start.2) | collective-permute-done | bytes 131104 | tf_op jit(solution)/shard_map/ppermute | solution.py:30
  27.1 0.6 collective-permute-start.3
  27.8 0.8 collective-permute-done.3.k1_ref.v1_ref
  28.7 6.3 %attention.2 = (bf16[2,128,2560]{2,1,0:T(8,128)(2,1)}, bf16[384,256]{1,0:T(8,128)(2,1)S(1)}, f32[384,256]{1,0:T(8,128)S(1)}) custom-call(s32[1]{0:T(128)} %bitcast.core_ref, f32[256,128]{1,0:T(8,128)S(1)} %add_select_fusion.bias_ref, bf16[2,128,2560]{2,1,0:T(8,128)(2,1)S(1)} %bitcast.190, bf16[2,128,2560]{2,1,0:T(8,128)(2,1)S(1)} %bitcast.192, ...), custom_call_target="tpu_custom_call" | custom-call | flops 3000000000 | bytes 5000000 | tf_op jit(solution)/shard_map/attention/pallas_call | solution.py:106
  35.0 6.3 %attention.3 = (bf16[2,128,2560]{2,1,0:T(8,128)(2,1)}, bf16[384,256]{1,0:T(8,128)(2,1)S(1)}, f32[384,256]{1,0:T(8,128)S(1)}) custom-call(s32[1]{0:T(128)} %bitcast.core_ref, f32[256,128]{1,0:T(8,128)S(1)} %add_select_fusion.bias_ref, bf16[2,128,2560]{2,1,0:T(8,128)(2,1)S(1)} %bitcast.191, ...), custom_call_target="tpu_custom_call", output_to_operand_aliasing={{0}: (10, {})} | custom-call | flops 3000000000 | bytes 5000000 | tf_op jit(solution)/shard_map/attention/pallas_call | solution.py:106
  41.3 0.4 collective-permute-start.6
  41.9 1.0 collective-permute-start.12
  42.9 0.4 collective-permute-start.10
  43.3 0.7 collective-permute-start.9
  44.3 1.3 collective-permute-done.4
  45.6 3.7 %collective-permute-start.7 = (bf16[256,256]{1,0:T(8,128)(2,1)S(1)}, bf16[256,256]{1,0:T(8,128)(2,1)S(1)}, u32[]{:S(2)}, u32[]{:S(2)}) collective-permute-start(bf16[256,256]{1,0:T(8,128)(2,1)S(1)} %pad_maximum_fusion.8), channel_id=1, source_target_pairs={{2,0},{3,1},{4,2},{5,3},{6,4},{7,5},{8,6},{9,7},{10,8},{11,9},{12,... | collective-permute-start | bytes 393224 | tf_op jit(solution)/shard_map/ppermute | solution.py:30
  49.4 1.6 %collective-permute-done.14 = bf16[4,128,320]{1,2,0:T(8,128)(2,1)S(1)} collective-permute-done((bf16[4,128,320]{1,2,0:T(8,128)(2,1)S(1)}, bf16[4,128,320]{1,2,0:T(8,128)(2,1)S(1)}, u32[]{:S(2)}, u32[]{:S(2)}) %collective-permute-start.14) | collective-permute-done | bytes 327712 | tf_op jit(solution)/shard_map/ppermute | solution.py:25
  51.0 3.3 %collective-permute-start.5 = (bf16[256,256]{1,0:T(8,128)(2,1)S(1)}, bf16[256,256]{1,0:T(8,128)(2,1)S(1)}, u32[]{:S(2)}, u32[]{:S(2)}) collective-permute-start(bf16[256,256]{1,0:T(8,128)(2,1)S(1)} %pad_maximum_fusion.7), channel_id=1, source_target_pairs={{2,0},{3,1},{4,2},{5,3},{6,4},{7,5},{8,6},{9,7},{10,8},{11,9},{12,... | collective-permute-start | bytes 393224 | tf_op jit(solution)/shard_map/ppermute | solution.py:30
  54.4 25.8 %collective-permute-done.12 = bf16[4,128,320]{1,2,0:T(8,128)(2,1)S(1)} collective-permute-done((bf16[4,128,320]{1,2,0:T(8,128)(2,1)S(1)}, bf16[4,128,320]{1,2,0:T(8,128)(2,1)S(1)}, u32[]{:S(2)}, u32[]{:S(2)}) %collective-permute-start.12) | collective-permute-done | bytes 327712 | tf_op jit(solution)/shard_map/ppermute | solution.py:25
  80.1 1.0 collective-permute-start.15
  81.5 0.6 collective-permute-start.11
  82.1 2.8 %collective-permute-start.18 = (bf16[256,256]{1,0:T(8,128)(2,1)S(1)}, bf16[256,256]{1,0:T(8,128)(2,1)S(1)}, u32[]{:S(2)}, u32[]{:S(2)}) collective-permute-start(bf16[256,256]{1,0:T(8,128)(2,1)S(1)} %fusion.10), channel_id=1, source_target_pairs={{0,48},{16,0},{32,16},{48,32},{1,49},{17,1},{33,17},{49,33},{2,50}... | collective-permute-start | bytes 393224 | tf_op jit(solution)/shard_map/ppermute | solution.py:25
  85.1 1.6 %collective-permute-start.17 = (bf16[256,256]{1,0:T(8,128)(2,1)S(1)}, bf16[256,256]{1,0:T(8,128)(2,1)S(1)}, u32[]{:S(2)}, u32[]{:S(2)}) collective-permute-start(bf16[256,256]{1,0:T(8,128)(2,1)S(1)} %fusion.10), channel_id=1, source_target_pairs={{0,32},{16,48},{32,0},{48,16},{1,33},{17,49},{33,1},{49,17},{2,34}... | collective-permute-start | bytes 393224 | tf_op jit(solution)/shard_map/ppermute | solution.py:25
  86.9 1.1 collective-permute-start.24
  88.0 0.7 collective-permute-start.22
  89.0 4.4 %collective-permute-done.16 = bf16[256,256]{1,0:T(8,128)(2,1)S(1)} collective-permute-done((bf16[256,256]{1,0:T(8,128)(2,1)S(1)}, bf16[256,256]{1,0:T(8,128)(2,1)S(1)}, u32[]{:S(2)}, u32[]{:S(2)}) %collective-permute-start.16) | collective-permute-done | bytes 131104 | tf_op jit(solution)/shard_map/ppermute | solution.py:25
  94.1 2.5 %collective-permute-start.8 = (bf16[128,512]{1,0:T(8,128)(2,1)S(1)}, bf16[128,512]{1,0:T(8,128)(2,1)S(1)}, u32[]{:S(2)}, u32[]{:S(2)}) collective-permute-start(bf16[128,512]{1,0:T(8,128)(2,1)S(1)} %pad_maximum_fusion.4), channel_id=1, source_target_pairs={{0,1},{1,0},{2,3},{3,2},{4,5},{5,4},{6,7},{7,6},{8,9},{9,8},{10,11... | collective-permute-start | bytes 393224 | tf_op jit(solution)/shard_map/ppermute | solution.py:25
  96.6 0.3 fusion.21
  97.0 0.3 fusion.3
  97.5 2.4 %collective-permute-start.20 = (bf16[4,80,256]{2,1,0:T(8,128)(2,1)S(1)}, bf16[4,80,256]{2,1,0:T(8,128)(2,1)S(1)}, u32[]{:S(2)}, u32[]{:S(2)}) collective-permute-start(bf16[4,80,256]{2,1,0:T(8,128)(2,1)S(1)} %get-tuple-element.50), channel_id=1, source_target_pairs={{0,8},{4,12},{8,0},{12,4},{1,9},{5,13},{9,1},{13,5},{2,10},{6,14},... | collective-permute-start | bytes 491528 | tf_op jit(solution)/shard_map/ppermute | solution.py:25
  100.6 1.3 collective-permute-start.19
  101.9 0.3 fusion.15
  102.3 0.3 fusion.2
  103.0 0.4 collective-permute-done.21
  103.3 6.3 %collective-permute-start.26 = (bf16[4,80,256]{2,1,0:T(8,128)(2,1)S(1)}, bf16[4,80,256]{2,1,0:T(8,128)(2,1)S(1)}, u32[]{:S(2)}, u32[]{:S(2)}) collective-permute-start(bf16[4,80,256]{2,1,0:T(8,128)(2,1)S(1)} %get-tuple-element.53), channel_id=1, source_target_pairs={{0,8},{4,12},{8,0},{12,4},{1,9},{5,13},{9,1},{13,5},{2,10},{6,14},... | collective-permute-start | bytes 491528 | tf_op jit(solution)/shard_map/ppermute | solution.py:25
  109.7 2.1 %collective-permute-done.27 = bf16[4,80,256]{2,1,0:T(8,128)(2,1)S(1)} collective-permute-done((bf16[4,80,256]{2,1,0:T(8,128)(2,1)S(1)}, bf16[4,80,256]{2,1,0:T(8,128)(2,1)S(1)}, u32[]{:S(2)}, u32[]{:S(2)}) %collective-permute-start.27) | collective-permute-done | bytes 163872 | tf_op jit(solution)/shard_map/ppermute | solution.py:25
  111.8 2.8 %collective-permute-done.26 = bf16[4,80,256]{2,1,0:T(8,128)(2,1)S(1)} collective-permute-done((bf16[4,80,256]{2,1,0:T(8,128)(2,1)S(1)}, bf16[4,80,256]{2,1,0:T(8,128)(2,1)S(1)}, u32[]{:S(2)}, u32[]{:S(2)}) %collective-permute-start.26) | collective-permute-done | bytes 163872 | tf_op jit(solution)/shard_map/ppermute | solution.py:25
  115.1 7.7 %collective-permute-start.33 = (bf16[40,512]{1,0:T(8,128)(2,1)S(1)}, bf16[40,512]{1,0:T(8,128)(2,1)S(1)}, u32[]{:S(2)}, u32[]{:S(2)}) collective-permute-start(bf16[40,512]{1,0:T(8,128)(2,1)S(1)} %get-tuple-element.99), channel_id=1, source_target_pairs={{0,130},{64,194},{128,0},{192,64},{2,128},{66,192},{130,2},{194,66... | collective-permute-start | bytes 122888 | tf_op jit(solution)/shard_map/ppermute | solution.py:38
  122.8 2.0 %collective-permute-start.31 = (bf16[40,512]{1,0:T(8,128)(2,1)S(1)}, bf16[40,512]{1,0:T(8,128)(2,1)S(1)}, u32[]{:S(2)}, u32[]{:S(2)}) collective-permute-start(bf16[40,512]{1,0:T(8,128)(2,1)S(1)} %dynamic-slice_bitcast_fusion.46), channel_id=1, source_target_pairs={{0,2},{64,66},{128,130},{192,194},{2,0},{66,64},{130,128},{194,192... | collective-permute-start | bytes 122888 | tf_op jit(solution)/shard_map/ppermute | solution.py:38
  124.9 1.6 %collective-permute-start.30 = (bf16[40,512]{1,0:T(8,128)(2,1)S(1)}, bf16[40,512]{1,0:T(8,128)(2,1)S(1)}, u32[]{:S(2)}, u32[]{:S(2)}) collective-permute-start(bf16[40,512]{1,0:T(8,128)(2,1)S(1)} %get-tuple-element.100), channel_id=1, source_target_pairs={{0,192},{64,2},{128,66},{192,130},{2,194},{66,0},{130,64},{194,128... | collective-permute-start | bytes 122888 | tf_op jit(solution)/shard_map/ppermute | solution.py:38
  126.5 3.0 %collective-permute-start.29 = (bf16[40,512]{1,0:T(8,128)(2,1)S(1)}, bf16[40,512]{1,0:T(8,128)(2,1)S(1)}, u32[]{:S(2)}, u32[]{:S(2)}) collective-permute-start(bf16[40,512]{1,0:T(8,128)(2,1)S(1)} %get-tuple-element.98), channel_id=1, source_target_pairs={{0,128},{64,192},{128,2},{192,66},{2,130},{66,194},{130,0},{194,64... | collective-permute-start | bytes 122888 | tf_op jit(solution)/shard_map/ppermute | solution.py:38
  129.5 1.2 collective-permute-start.28
  130.8 0.7 collective-permute-done.29
  131.6 3.5 %collective-permute-done.28 = bf16[40,512]{1,0:T(8,128)(2,1)S(1)} collective-permute-done((bf16[40,512]{1,0:T(8,128)(2,1)S(1)}, bf16[40,512]{1,0:T(8,128)(2,1)S(1)}, u32[]{:S(2)}, u32[]{:S(2)}) %collective-permute-start.28) | collective-permute-done | bytes 40992 | tf_op jit(solution)/shard_map/ppermute | solution.py:38
  135.2 2.5 %collective-permute-start.35 = (f32[20,512]{1,0:T(8,128)S(1)}, f32[20,512]{1,0:T(8,128)S(1)}, u32[]{:S(2)}, u32[]{:S(2)}) collective-permute-start(f32[20,512]{1,0:T(8,128)S(1)} %get-tuple-element.92), channel_id=1, source_target_pairs={{0,1},{1,0},{2,3},{3,2},{4,5},{5,4},{6,7},{7,6},{8,9},{9,8},{10,11... | collective-permute-start | bytes 122888 | tf_op jit(solution)/shard_map/ppermute | solution.py:25
  137.6 0.4 maximum_bitcast_fusion
  138.0 0.4 copy.27
  138.4 0.9 broadcast_in_dim_reshape.3
  139.5 0.7 reshape.222
  (111 shorter events, 4.9 us)
Async XLA Ops:
  0.6 28.0 %copy-start.1 = (bf16[2,1,128,2560]{3,2,1,0:T(8,128)(2,1)S(1)}, bf16[2,1,128,2560]{3,2,1,0:T(8,128)(2,1)}, u32[]{:S(2)}) copy-start(bf16[2,1,128,2560]{3,2,1,0:T(8,128)(2,1)} %param.7) | copy-start | bytes 3932164
  1.7 27.0 %copy-start = (bf16[2,1,128,2560]{3,2,1,0:T(8,128)(2,1)S(1)}, bf16[2,1,128,2560]{3,2,1,0:T(8,128)(2,1)}, u32[]{:S(2)}) copy-start(bf16[2,1,128,2560]{3,2,1,0:T(8,128)(2,1)} %param.5) | copy-start | bytes 3932164
  1.7 25.9 %collective-permute-start = (bf16[128,512]{1,0:T(8,128)(2,1)S(1)}, bf16[128,512]{1,0:T(8,128)(2,1)S(1)}, u32[]{:S(2)}, u32[]{:S(2)}) collective-permute-start(bf16[128,512]{1,0:T(8,128)(2,1)S(1)} %pad_maximum_fusion.5.k0_ref.v0_ref), channel_id=1, source_target_pairs={{0,2},{1,3},{2,4},{3,5},{4,6},{5,7},{6,8},{7,9},{8,10},{9,11},{10,... | collective-permute-start | bytes 393224 | tf_op jit(solution)/shard_map/ppermute | solution.py:30
  10.7 16.3 %collective-permute-start.2 = (bf16[128,512]{1,0:T(8,128)(2,1)S(1)}, bf16[128,512]{1,0:T(8,128)(2,1)S(1)}, u32[]{:S(2)}, u32[]{:S(2)}) collective-permute-start(bf16[128,512]{1,0:T(8,128)(2,1)S(1)} %pad_maximum_fusion.6.k0_ref.v0_ref), channel_id=1, source_target_pairs={{0,2},{1,3},{2,4},{3,5},{4,6},{5,7},{6,8},{7,9},{8,10},{9,11},{10,... | collective-permute-start | bytes 393224 | tf_op jit(solution)/shard_map/ppermute | solution.py:30
  27.1 1.6 %collective-permute-start.3 = (bf16[128,512]{1,0:T(8,128)(2,1)S(1)}, bf16[128,512]{1,0:T(8,128)(2,1)S(1)}, u32[]{:S(2)}, u32[]{:S(2)}) collective-permute-start(bf16[128,512]{1,0:T(8,128)(2,1)S(1)} %broadcast_select_fusion.2), channel_id=1, source_target_pairs={{0,1},{1,0},{2,3},{3,2},{4,5},{5,4},{6,7},{7,6},{8,9},{9,8},{10,11... | collective-permute-start | bytes 393224 | tf_op jit(solution)/shard_map/ppermute | solution.py:25
  27.7 7.3 %collective-permute-start.1 = (bf16[128,512]{1,0:T(8,128)(2,1)S(1)}, bf16[128,512]{1,0:T(8,128)(2,1)S(1)}, u32[]{:S(2)}, u32[]{:S(2)}) collective-permute-start(bf16[128,512]{1,0:T(8,128)(2,1)S(1)} %broadcast_select_fusion.3), channel_id=1, source_target_pairs={{0,1},{1,0},{2,3},{3,2},{4,5},{5,4},{6,7},{7,6},{8,9},{9,8},{10,11... | collective-permute-start | bytes 393224 | tf_op jit(solution)/shard_map/ppermute | solution.py:25
  35.0 6.7 %copy-start.2 = (bf16[16,128,320]{1,2,0:T(8,128)(2,1)S(1)}, bf16[16,128,320]{1,2,0:T(8,128)(2,1)}, u32[]{:S(2)}) copy-start(bf16[16,128,320]{1,2,0:T(8,128)(2,1)} %param.8) | copy-start | bytes 3932164
  41.3 2.8 %collective-permute-start.6 = (bf16[384,256]{1,0:T(8,128)(2,1)S(1)}, bf16[384,256]{1,0:T(8,128)(2,1)S(1)}, u32[]{:S(2)}, u32[]{:S(2)}) collective-permute-start(bf16[384,256]{1,0:T(8,128)(2,1)S(1)} %get-tuple-element.15), channel_id=1, source_target_pairs={{0,1},{1,0},{2,3},{3,2},{4,5},{5,4},{6,7},{7,6},{8,9},{9,8},{10,11... | collective-permute-start | bytes 589832 | tf_op jit(solution)/shard_map/ppermute | solution.py:25
  41.8 9.2 %collective-permute-start.14 = (bf16[4,128,320]{1,2,0:T(8,128)(2,1)S(1)}, bf16[4,128,320]{1,2,0:T(8,128)(2,1)S(1)}, u32[]{:S(2)}, u32[]{:S(2)}) collective-permute-start(bf16[4,128,320]{1,2,0:T(8,128)(2,1)S(1)} %get-tuple-element.37), channel_id=1, source_target_pairs={{0,192},{64,0},{128,64},{192,128},{1,193},{65,1},{129,65},{193,129... | collective-permute-start | bytes 983048 | tf_op jit(solution)/shard_map/ppermute | solution.py:25
  41.9 38.2 %collective-permute-start.12 = (bf16[4,128,320]{1,2,0:T(8,128)(2,1)S(1)}, bf16[4,128,320]{1,2,0:T(8,128)(2,1)S(1)}, u32[]{:S(2)}, u32[]{:S(2)}) collective-permute-start(bf16[4,128,320]{1,2,0:T(8,128)(2,1)S(1)} %get-tuple-element.38), channel_id=1, source_target_pairs={{0,128},{64,192},{128,0},{192,64},{1,129},{65,193},{129,1},{193,65... | collective-permute-start | bytes 983048 | tf_op jit(solution)/shard_map/ppermute | solution.py:25
  42.9 38.3 %collective-permute-start.10 = (bf16[4,128,320]{1,2,0:T(8,128)(2,1)S(1)}, bf16[4,128,320]{1,2,0:T(8,128)(2,1)S(1)}, u32[]{:S(2)}, u32[]{:S(2)}) collective-permute-start(bf16[4,128,320]{1,2,0:T(8,128)(2,1)S(1)} %get-tuple-element.39), channel_id=1, source_target_pairs={{0,64},{64,128},{128,192},{192,0},{1,65},{65,129},{129,193},{193,1... | collective-permute-start | bytes 983048 | tf_op jit(solution)/shard_map/ppermute | solution.py:25
  43.3 43.5 %collective-permute-start.9 = (bf16[4,128,320]{1,2,0:T(8,128)(2,1)S(1)}, bf16[4,128,320]{1,2,0:T(8,128)(2,1)S(1)}, u32[]{:S(2)}, u32[]{:S(2)}) collective-permute-start(bf16[4,128,320]{1,2,0:T(8,128)(2,1)S(1)} %get-tuple-element.36), channel_id=1, source_target_pairs={{0,1},{1,0},{2,3},{3,2},{4,5},{5,4},{6,7},{7,6},{8,9},{9,8},{10,11... | collective-permute-start | bytes 983048 | tf_op jit(solution)/shard_map/ppermute | solution.py:25
  44.1 1.5 %collective-permute-start.4 = (bf16[384,256]{1,0:T(8,128)(2,1)S(1)}, bf16[384,256]{1,0:T(8,128)(2,1)S(1)}, u32[]{:S(2)}, u32[]{:S(2)}) collective-permute-start(bf16[384,256]{1,0:T(8,128)(2,1)S(1)} %get-tuple-element.13), channel_id=1, source_target_pairs={{0,1},{1,0},{2,3},{3,2},{4,5},{5,4},{6,7},{7,6},{8,9},{9,8},{10,11... | collective-permute-start | bytes 589832 | tf_op jit(solution)/shard_map/ppermute | solution.py:25
  45.6 36.5 %collective-permute-start.7 = (bf16[256,256]{1,0:T(8,128)(2,1)S(1)}, bf16[256,256]{1,0:T(8,128)(2,1)S(1)}, u32[]{:S(2)}, u32[]{:S(2)}) collective-permute-start(bf16[256,256]{1,0:T(8,128)(2,1)S(1)} %pad_maximum_fusion.8), channel_id=1, source_target_pairs={{2,0},{3,1},{4,2},{5,3},{6,4},{7,5},{8,6},{9,7},{10,8},{11,9},{12,... | collective-permute-start | bytes 393224 | tf_op jit(solution)/shard_map/ppermute | solution.py:30
  51.0 30.5 %collective-permute-start.5 = (bf16[256,256]{1,0:T(8,128)(2,1)S(1)}, bf16[256,256]{1,0:T(8,128)(2,1)S(1)}, u32[]{:S(2)}, u32[]{:S(2)}) collective-permute-start(bf16[256,256]{1,0:T(8,128)(2,1)S(1)} %pad_maximum_fusion.7), channel_id=1, source_target_pairs={{2,0},{3,1},{4,2},{5,3},{6,4},{7,5},{8,6},{9,7},{10,8},{11,9},{12,... | collective-permute-start | bytes 393224 | tf_op jit(solution)/shard_map/ppermute | solution.py:30
  80.1 4.9 %collective-permute-start.15 = (bf16[4,128,320]{1,2,0:T(8,128)(2,1)S(1)}, bf16[4,128,320]{1,2,0:T(8,128)(2,1)S(1)}, u32[]{:S(2)}, u32[]{:S(2)}) collective-permute-start(bf16[4,128,320]{1,2,0:T(8,128)(2,1)S(1)} %collective-permute-done.14), channel_id=1, source_target_pairs={{0,1},{1,0},{2,3},{3,2},{4,5},{5,4},{6,7},{7,6},{8,9},{9,8},{10,11... | collective-permute-start | bytes 983048 | tf_op jit(solution)/shard_map/ppermute | solution.py:25
  81.2 3.9 %collective-permute-start.13 = (bf16[4,128,320]{1,2,0:T(8,128)(2,1)S(1)}, bf16[4,128,320]{1,2,0:T(8,128)(2,1)S(1)}, u32[]{:S(2)}, u32[]{:S(2)}) collective-permute-start(bf16[4,128,320]{1,2,0:T(8,128)(2,1)S(1)} %collective-permute-done.12), channel_id=1, source_target_pairs={{0,1},{1,0},{2,3},{3,2},{4,5},{5,4},{6,7},{7,6},{8,9},{9,8},{10,11... | collective-permute-start | bytes 983048 | tf_op jit(solution)/shard_map/ppermute | solution.py:25
  81.5 6.5 %collective-permute-start.11 = (bf16[4,128,320]{1,2,0:T(8,128)(2,1)S(1)}, bf16[4,128,320]{1,2,0:T(8,128)(2,1)S(1)}, u32[]{:S(2)}, u32[]{:S(2)}) collective-permute-start(bf16[4,128,320]{1,2,0:T(8,128)(2,1)S(1)} %collective-permute-done.10), channel_id=1, source_target_pairs={{0,1},{1,0},{2,3},{3,2},{4,5},{5,4},{6,7},{7,6},{8,9},{9,8},{10,11... | collective-permute-start | bytes 983048 | tf_op jit(solution)/shard_map/ppermute | solution.py:25
  82.1 12.0 %collective-permute-start.18 = (bf16[256,256]{1,0:T(8,128)(2,1)S(1)}, bf16[256,256]{1,0:T(8,128)(2,1)S(1)}, u32[]{:S(2)}, u32[]{:S(2)}) collective-permute-start(bf16[256,256]{1,0:T(8,128)(2,1)S(1)} %fusion.10), channel_id=1, source_target_pairs={{0,48},{16,0},{32,16},{48,32},{1,49},{17,1},{33,17},{49,33},{2,50}... | collective-permute-start | bytes 393224 | tf_op jit(solution)/shard_map/ppermute | solution.py:25
  85.0 8.4 %collective-permute-start.16 = (bf16[256,256]{1,0:T(8,128)(2,1)S(1)}, bf16[256,256]{1,0:T(8,128)(2,1)S(1)}, u32[]{:S(2)}, u32[]{:S(2)}) collective-permute-start(bf16[256,256]{1,0:T(8,128)(2,1)S(1)} %fusion.10), channel_id=1, source_target_pairs={{0,16},{16,32},{32,48},{48,0},{1,17},{17,33},{33,49},{49,1},{2,18}... | collective-permute-start | bytes 393224 | tf_op jit(solution)/shard_map/ppermute | solution.py:25
  85.1 11.9 %collective-permute-start.17 = (bf16[256,256]{1,0:T(8,128)(2,1)S(1)}, bf16[256,256]{1,0:T(8,128)(2,1)S(1)}, u32[]{:S(2)}, u32[]{:S(2)}) collective-permute-start(bf16[256,256]{1,0:T(8,128)(2,1)S(1)} %fusion.10), channel_id=1, source_target_pairs={{0,32},{16,48},{32,0},{48,16},{1,33},{17,49},{33,1},{49,17},{2,34}... | collective-permute-start | bytes 393224 | tf_op jit(solution)/shard_map/ppermute | solution.py:25
  86.9 13.7 %collective-permute-start.24 = (bf16[256,256]{1,0:T(8,128)(2,1)S(1)}, bf16[256,256]{1,0:T(8,128)(2,1)S(1)}, u32[]{:S(2)}, u32[]{:S(2)}) collective-permute-start(bf16[256,256]{1,0:T(8,128)(2,1)S(1)} %fusion.11), channel_id=1, source_target_pairs={{0,48},{16,0},{32,16},{48,32},{1,49},{17,1},{33,17},{49,33},{2,50}... | collective-permute-start | bytes 393224 | tf_op jit(solution)/shard_map/ppermute | solution.py:25
  88.0 9.5 %collective-permute-start.22 = (bf16[256,256]{1,0:T(8,128)(2,1)S(1)}, bf16[256,256]{1,0:T(8,128)(2,1)S(1)}, u32[]{:S(2)}, u32[]{:S(2)}) collective-permute-start(bf16[256,256]{1,0:T(8,128)(2,1)S(1)} %fusion.11), channel_id=1, source_target_pairs={{0,16},{16,32},{32,48},{48,0},{1,17},{17,33},{33,49},{49,1},{2,18}... | collective-permute-start | bytes 393224 | tf_op jit(solution)/shard_map/ppermute | solution.py:25
  93.4 8.9 %collective-permute-start.23 = (bf16[256,256]{1,0:T(8,128)(2,1)S(1)}, bf16[256,256]{1,0:T(8,128)(2,1)S(1)}, u32[]{:S(2)}, u32[]{:S(2)}) collective-permute-start(bf16[256,256]{1,0:T(8,128)(2,1)S(1)} %fusion.11), channel_id=1, source_target_pairs={{0,32},{16,48},{32,0},{48,16},{1,33},{17,49},{33,1},{49,17},{2,34}... | collective-permute-start | bytes 393224 | tf_op jit(solution)/shard_map/ppermute | solution.py:25
  94.1 30.7 %collective-permute-start.8 = (bf16[128,512]{1,0:T(8,128)(2,1)S(1)}, bf16[128,512]{1,0:T(8,128)(2,1)S(1)}, u32[]{:S(2)}, u32[]{:S(2)}) collective-permute-start(bf16[128,512]{1,0:T(8,128)(2,1)S(1)} %pad_maximum_fusion.4), channel_id=1, source_target_pairs={{0,1},{1,0},{2,3},{3,2},{4,5},{5,4},{6,7},{7,6},{8,9},{9,8},{10,11... | collective-permute-start | bytes 393224 | tf_op jit(solution)/shard_map/ppermute | solution.py:25
  97.4 5.9 %collective-permute-start.21 = (bf16[4,80,256]{2,1,0:T(8,128)(2,1)S(1)}, bf16[4,80,256]{2,1,0:T(8,128)(2,1)S(1)}, u32[]{:S(2)}, u32[]{:S(2)}) collective-permute-start(bf16[4,80,256]{2,1,0:T(8,128)(2,1)S(1)} %get-tuple-element.49), channel_id=1, source_target_pairs={{0,12},{4,0},{8,4},{12,8},{1,13},{5,1},{9,5},{13,9},{2,14},{6,2},{... | collective-permute-start | bytes 491528 | tf_op jit(solution)/shard_map/ppermute | solution.py:25
  97.5 12.1 %collective-permute-start.20 = (bf16[4,80,256]{2,1,0:T(8,128)(2,1)S(1)}, bf16[4,80,256]{2,1,0:T(8,128)(2,1)S(1)}, u32[]{:S(2)}, u32[]{:S(2)}) collective-permute-start(bf16[4,80,256]{2,1,0:T(8,128)(2,1)S(1)} %get-tuple-element.50), channel_id=1, source_target_pairs={{0,8},{4,12},{8,0},{12,4},{1,9},{5,13},{9,1},{13,5},{2,10},{6,14},... | collective-permute-start | bytes 491528 | tf_op jit(solution)/shard_map/ppermute | solution.py:25
  100.6 9.0 %collective-permute-start.19 = (bf16[4,80,256]{2,1,0:T(8,128)(2,1)S(1)}, bf16[4,80,256]{2,1,0:T(8,128)(2,1)S(1)}, u32[]{:S(2)}, u32[]{:S(2)}) collective-permute-start(bf16[4,80,256]{2,1,0:T(8,128)(2,1)S(1)} %get-tuple-element.48), channel_id=1, source_target_pairs={{0,4},{4,8},{8,12},{12,0},{1,5},{5,9},{9,13},{13,1},{2,6},{6,10},{... | collective-permute-start | bytes 491528 | tf_op jit(solution)/shard_map/ppermute | solution.py:25
  102.7 9.1 %collective-permute-start.27 = (bf16[4,80,256]{2,1,0:T(8,128)(2,1)S(1)}, bf16[4,80,256]{2,1,0:T(8,128)(2,1)S(1)}, u32[]{:S(2)}, u32[]{:S(2)}) collective-permute-start(bf16[4,80,256]{2,1,0:T(8,128)(2,1)S(1)} %get-tuple-element.52), channel_id=1, source_target_pairs={{0,12},{4,0},{8,4},{12,8},{1,13},{5,1},{9,5},{13,9},{2,14},{6,2},{... | collective-permute-start | bytes 491528 | tf_op jit(solution)/shard_map/ppermute | solution.py:25
  103.3 11.3 %collective-permute-start.26 = (bf16[4,80,256]{2,1,0:T(8,128)(2,1)S(1)}, bf16[4,80,256]{2,1,0:T(8,128)(2,1)S(1)}, u32[]{:S(2)}, u32[]{:S(2)}) collective-permute-start(bf16[4,80,256]{2,1,0:T(8,128)(2,1)S(1)} %get-tuple-element.53), channel_id=1, source_target_pairs={{0,8},{4,12},{8,0},{12,4},{1,9},{5,13},{9,1},{13,5},{2,10},{6,14},... | collective-permute-start | bytes 491528 | tf_op jit(solution)/shard_map/ppermute | solution.py:25
  109.6 5.2 %collective-permute-start.25 = (bf16[4,80,256]{2,1,0:T(8,128)(2,1)S(1)}, bf16[4,80,256]{2,1,0:T(8,128)(2,1)S(1)}, u32[]{:S(2)}, u32[]{:S(2)}) collective-permute-start(bf16[4,80,256]{2,1,0:T(8,128)(2,1)S(1)} %get-tuple-element.51), channel_id=1, source_target_pairs={{0,4},{4,8},{8,12},{12,0},{1,5},{5,9},{9,13},{13,1},{2,6},{6,10},{... | collective-permute-start | bytes 491528 | tf_op jit(solution)/shard_map/ppermute | solution.py:25
  114.9 11.5 %collective-permute-start.34 = (bf16[40,512]{1,0:T(8,128)(2,1)S(1)}, bf16[40,512]{1,0:T(8,128)(2,1)S(1)}, u32[]{:S(2)}, u32[]{:S(2)}) collective-permute-start(bf16[40,512]{1,0:T(8,128)(2,1)S(1)} %get-tuple-element.101), channel_id=1, source_target_pairs={{0,194},{64,0},{128,64},{192,128},{2,192},{66,2},{130,66},{194,130... | collective-permute-start | bytes 122888 | tf_op jit(solution)/shard_map/ppermute | solution.py:38
  115.1 14.4 %collective-permute-start.33 = (bf16[40,512]{1,0:T(8,128)(2,1)S(1)}, bf16[40,512]{1,0:T(8,128)(2,1)S(1)}, u32[]{:S(2)}, u32[]{:S(2)}) collective-permute-start(bf16[40,512]{1,0:T(8,128)(2,1)S(1)} %get-tuple-element.99), channel_id=1, source_target_pairs={{0,130},{64,194},{128,0},{192,64},{2,128},{66,192},{130,2},{194,66... | collective-permute-start | bytes 122888 | tf_op jit(solution)/shard_map/ppermute | solution.py:38
  122.8 8.0 %collective-permute-start.32 = (bf16[40,512]{1,0:T(8,128)(2,1)S(1)}, bf16[40,512]{1,0:T(8,128)(2,1)S(1)}, u32[]{:S(2)}, u32[]{:S(2)}) collective-permute-start(bf16[40,512]{1,0:T(8,128)(2,1)S(1)} %get-tuple-element.97), channel_id=1, source_target_pairs={{0,66},{64,130},{128,194},{192,0},{2,64},{66,128},{130,192},{194,2... | collective-permute-start | bytes 122888 | tf_op jit(solution)/shard_map/ppermute | solution.py:38
  122.8 8.0 %collective-permute-start.31 = (bf16[40,512]{1,0:T(8,128)(2,1)S(1)}, bf16[40,512]{1,0:T(8,128)(2,1)S(1)}, u32[]{:S(2)}, u32[]{:S(2)}) collective-permute-start(bf16[40,512]{1,0:T(8,128)(2,1)S(1)} %dynamic-slice_bitcast_fusion.46), channel_id=1, source_target_pairs={{0,2},{64,66},{128,130},{192,194},{2,0},{66,64},{130,128},{194,192... | collective-permute-start | bytes 122888 | tf_op jit(solution)/shard_map/ppermute | solution.py:38
  124.9 6.0 %collective-permute-start.30 = (bf16[40,512]{1,0:T(8,128)(2,1)S(1)}, bf16[40,512]{1,0:T(8,128)(2,1)S(1)}, u32[]{:S(2)}, u32[]{:S(2)}) collective-permute-start(bf16[40,512]{1,0:T(8,128)(2,1)S(1)} %get-tuple-element.100), channel_id=1, source_target_pairs={{0,192},{64,2},{128,66},{192,130},{2,194},{66,0},{130,64},{194,128... | collective-permute-start | bytes 122888 | tf_op jit(solution)/shard_map/ppermute | solution.py:38
  126.5 5.1 %collective-permute-start.29 = (bf16[40,512]{1,0:T(8,128)(2,1)S(1)}, bf16[40,512]{1,0:T(8,128)(2,1)S(1)}, u32[]{:S(2)}, u32[]{:S(2)}) collective-permute-start(bf16[40,512]{1,0:T(8,128)(2,1)S(1)} %get-tuple-element.98), channel_id=1, source_target_pairs={{0,128},{64,192},{128,2},{192,66},{2,130},{66,194},{130,0},{194,64... | collective-permute-start | bytes 122888 | tf_op jit(solution)/shard_map/ppermute | solution.py:38
  129.5 5.6 %collective-permute-start.28 = (bf16[40,512]{1,0:T(8,128)(2,1)S(1)}, bf16[40,512]{1,0:T(8,128)(2,1)S(1)}, u32[]{:S(2)}, u32[]{:S(2)}) collective-permute-start(bf16[40,512]{1,0:T(8,128)(2,1)S(1)} %get-tuple-element.96), channel_id=1, source_target_pairs={{0,64},{64,128},{128,192},{192,2},{2,66},{66,130},{130,194},{194,0... | collective-permute-start | bytes 122888 | tf_op jit(solution)/shard_map/ppermute | solution.py:38
  135.2 4.2 %collective-permute-start.35 = (f32[20,512]{1,0:T(8,128)S(1)}, f32[20,512]{1,0:T(8,128)S(1)}, u32[]{:S(2)}, u32[]{:S(2)}) collective-permute-start(f32[20,512]{1,0:T(8,128)S(1)} %get-tuple-element.92), channel_id=1, source_target_pairs={{0,1},{1,0},{2,3},{3,2},{4,5},{5,4},{6,7},{7,6},{8,9},{9,8},{10,11... | collective-permute-start | bytes 122888 | tf_op jit(solution)/shard_map/ppermute | solution.py:25

commit v3 on v2

v3 whole, which is shorter than its diff:
```python
import functools
import math

import jax
import jax.numpy as jnp
from jax import lax
from jax.experimental import pallas as pl
from jax.experimental.pallas import tpu as pltpu
from jax.sharding import Mesh, PartitionSpec as P

KV_HEADS = 4
GROUP = 5
HEAD_DIM = 128
LAYERS = 2
TOK = 128
WIDE = 320
VMEM = 60 * 1024 * 1024
PAIR = 2 * HEAD_DIM
FACTOR = 1.0 / math.sqrt(HEAD_DIM)
AXES = ("zl", "y", "x", "zh", "core")
SIZES = {"zl": 4, "y": 4, "x": 4, "zh": 2, "core": 2}


def shift(value, axis, by):
    size = SIZES[axis]
    return lax.ppermute(value, axis, [(i, (i + by) % size) for i in range(size)])


def ctx_shift(value, by):
    pairs = [(i, i + by) for i in range(16) if 0 <= i + by < 16]
    return lax.ppermute(value, ("x", "zh", "core"), pairs)


def softmax_grad(s, dp, bias, lower, lower_b, upper_b):
    scale = FACTOR * math.log2(math.e)
    s0 = jnp.where(lower, s[:TOK], s[2 * TOK :]) * scale + bias[:TOK]
    s1 = s[TOK : 2 * TOK] * scale + bias[TOK:]
    top = jnp.max(jnp.maximum(s0, s1), axis=0, keepdims=True)
    e0, e1 = jnp.exp2(s0 - top), jnp.exp2(s1 - top)
    inv = 1.0 / jnp.sum(e0 + e1, axis=0, keepdims=True)
    p0, p1 = e0 * inv, e1 * inv
    d0 = p0 * jnp.where(lower, dp[:TOK], dp[2 * TOK :])
    d1 = p1 * dp[TOK : 2 * TOK]
    delta = jnp.sum(d0 + d1, axis=0, keepdims=True)
    d0, d1 = (d0 - p0 * delta).astype(jnp.bfloat16), (d1 - p1 * delta).astype(jnp.bfloat16)
    p0, p1 = p0.astype(jnp.bfloat16), p1.astype(jnp.bfloat16)
    p = jnp.concatenate([p0 * lower_b, p1, p0 * upper_b], axis=0)
    ds = jnp.concatenate([d0 * lower_b, d1, d0 * upper_b], axis=0)
    return p, ds


def attention_kernel(core_ref, bias_ref, q_ref, do_ref, k0_ref, k1_ref, k2_ref, v0_ref, v1_ref, v2_ref, dq_ref, theirs_ref, mine_ref):
    keys = jnp.concatenate([k0_ref[...], k1_ref[...], k2_ref[...]], axis=0)
    values = jnp.concatenate([v0_ref[...], v1_ref[...], v2_ref[...]], axis=0)
    keys_t = keys.T
    bias = bias_ref[...]
    key_at = lax.broadcasted_iota(jnp.int32, (TOK, TOK), 0)
    query_at = lax.broadcasted_iota(jnp.int32, (TOK, TOK), 1)
    lower = key_at <= query_at
    lower_b = lower.astype(jnp.float32).astype(jnp.bfloat16)
    upper_b = 1 - lower_b
    nt = (((1,), (1,)), ((), ()))

    def load(g):
        cols = slice(g * HEAD_DIM, (g + 1) * HEAD_DIM)
        q = jnp.concatenate([q_ref[0, :, cols], q_ref[1, :, cols]], axis=0)
        do = jnp.concatenate([do_ref[0, :, cols], do_ref[1, :, cols]], axis=0)
        s = lax.dot_general(keys, q, nt, preferred_element_type=jnp.float32)
        dp = lax.dot_general(values, do, nt, preferred_element_type=jnp.float32)
        return q, do, s, dp

    def store(g, q, do, p, ds, dk, dv):
        cols = slice(g * HEAD_DIM, (g + 1) * HEAD_DIM)
        dv += jnp.dot(p, do, preferred_element_type=jnp.float32)
        dk += jnp.dot(ds, q, preferred_element_type=jnp.float32)
        dq = jnp.dot(keys_t, ds, preferred_element_type=jnp.float32) * FACTOR
        dq = dq.astype(jnp.bfloat16).T
        dq_ref[0, :, cols] = dq[:TOK]
        dq_ref[1, :, cols] = dq[TOK:]
        return dk, dv

    dk = jnp.zeros((3 * TOK, HEAD_DIM), jnp.float32)
    dv = jnp.zeros((3 * TOK, HEAD_DIM), jnp.float32)
    following, done = load(0), None
    for g in range(GROUP):
        q, do, s, dp = following
        if g + 1 < GROUP:
            following = load(g + 1)
        if done is not None:
            dk, dv = store(*done, dk, dv)
        tiles = [slice(layer * TOK, (layer + 1) * TOK) for layer in range(LAYERS)]
        parts = [softmax_grad(s[:, t], dp[:, t], bias, lower, lower_b, upper_b) for t in tiles]
        p = jnp.concatenate([part[0] for part in parts], axis=1)
        ds = jnp.concatenate([part[1] for part in parts], axis=1)
        done = (g, q, do, p, ds)
    dk, dv = store(*done, dk, dv)
    both = jnp.concatenate([dk * FACTOR, dv], axis=1)

    @pl.when(pl.program_id(0) < 2)
    def _():
        theirs_ref[...] = both.astype(jnp.bfloat16)

    @pl.when(pl.program_id(0) >= 2)
    def _():
        mine_ref[...] = both


def attention(core, bias, queries, grad_out, kv0, kv1, kv2):
    wide = GROUP * HEAD_DIM

    def head(i, core_ref):
        return (2 - 2 * core_ref[0] + i) % KV_HEADS

    rows = pl.BlockSpec((LAYERS, TOK, wide), lambda i, c: (0, 0, head(i, c)))
    key_cols = pl.BlockSpec((TOK, HEAD_DIM), lambda i, c: (0, head(i, c)))
    value_cols = pl.BlockSpec((TOK, HEAD_DIM), lambda i, c: (0, KV_HEADS + head(i, c)))
    theirs = pl.BlockSpec((3 * TOK, PAIR), lambda i, c: (0, jnp.minimum(i, 1)))
    mine = pl.BlockSpec((3 * TOK, PAIR), lambda i, c: (0, jnp.maximum(i - 2, 0)))
    return pl.pallas_call(
        attention_kernel,
        grid_spec=pltpu.PrefetchScalarGridSpec(
            num_scalar_prefetch=1,
            grid=(KV_HEADS,),
            in_specs=[pl.BlockSpec((2 * TOK, TOK), lambda i, c: (0, 0)), rows, rows] + [key_cols] * 3 + [value_cols] * 3,
            out_specs=[rows, theirs, mine],
        ),
        out_shape=[
            jax.ShapeDtypeStruct(queries.shape, jnp.bfloat16),
            jax.ShapeDtypeStruct((3 * TOK, 2 * PAIR), jnp.bfloat16),
            jax.ShapeDtypeStruct((3 * TOK, 2 * PAIR), jnp.float32),
        ],
        compiler_params=pltpu.CompilerParams(vmem_limit_bytes=VMEM),
        cost_estimate=pl.CostEstimate(flops=6_000_000_000, bytes_accessed=9_000_000, transcendentals=1_400_000),
        name="attention",
    )(core[None], bias, queries, grad_out, kv0, kv1, kv2, kv0, kv1, kv2)


def product_kernel(at_ref, own_ref, other_ref, *refs):
    block_refs, out_refs, acc_ref = refs[:4], refs[4:8], refs[8]
    zl, x = at_ref[0], at_ref[1]
    left = []
    for by in range(4):
        seq = (zl - by + 4) % 4
        left += [own_ref[0, seq], other_ref[0, seq]]
    left = jnp.concatenate(left, axis=1)
    right = jnp.concatenate([ref[...] for ref in block_refs], axis=0)
    acc_ref[...] = jnp.dot(left, right, preferred_element_type=jnp.float32)
    for by in range(4):
        start = pl.multiple_of((x + by) % 4 * 80, 16)
        out_refs[by][0] = acc_ref[pl.ds(start, 80)].astype(jnp.bfloat16)


def products(at, own, other, blocks):
    states = pl.BlockSpec((1, 4, WIDE, TOK), lambda i, at: ((at[2] - i + 4) % 4, 0, 0, 0))
    return pl.pallas_call(
        product_kernel,
        grid_spec=pltpu.PrefetchScalarGridSpec(
            num_scalar_prefetch=1,
            grid=(4,),
            in_specs=[states, states] + [pl.BlockSpec((2 * TOK, PAIR), lambda i, at: (0, 0))] * 4,
            out_specs=[pl.BlockSpec((1, 80, PAIR), lambda i, at: (i, 0, 0))] * 4,
            scratch_shapes=[pltpu.VMEM((WIDE, PAIR), jnp.float32)],
        ),
        out_shape=[jax.ShapeDtypeStruct((4, 80, PAIR), jnp.bfloat16)] * 4,
        compiler_params=pltpu.CompilerParams(vmem_limit_bytes=16 * 1024 * 1024),
        cost_estimate=pl.CostEstimate(flops=1_400_000_000, bytes_accessed=5_000_000, transcendentals=0),
        name="products",
    )(at, own, other, *blocks)


def mask_bias(position, ends):
    own = jnp.arange(TOK, dtype=jnp.int32)

    def doc(pos):
        return jnp.sum((pos[:, None] >= ends[None, :]).astype(jnp.int32), axis=1)

    query_doc = doc(position + own)
    zero, one, two = ((position - back * TOK + own) for back in (0, 1, 2))
    lower = own[:, None] <= own[None, :]
    seen = [(pos >= 0)[:, None] & (doc(pos)[:, None] == query_doc[None, :]) for pos in (zero, one, two)]
    seen = jnp.concatenate([jnp.where(lower, seen[0], seen[2]), seen[1]], axis=0)
    return jnp.where(seen, 0.0, -jnp.inf).astype(jnp.float32)


def pick(value, index, axis):
    return lax.dynamic_index_in_dim(value, index, axis, keepdims=False)


def total(parts):
    acc = parts[0].astype(jnp.float32)
    for part in parts[1:]:
        acc = acc + part.astype(jnp.float32)
    return acc


def on_device(queries, keys_values, grad_out, hidden_kv, doc_lengths):
    core, zh, x, y, zl = (lax.axis_index(name) for name in ("core", "zh", "x", "y", "zl"))
    first = core == 0
    position = ((x * 2 + zh) * 2 + core) * TOK
    kv = keys_values[0]
    half = KV_HEADS * HEAD_DIM
    kv2 = ctx_shift(kv, 2)
    kv1 = shift(jnp.where(first, kv, kv2), "core", 1)

    bias = mask_bias(position, jnp.cumsum(doc_lengths[0]))
    hidden = hidden_kv.transpose(0, 2, 1).reshape(4, 4, WIDE, TOK)
    states = [pick(hidden, y, 1)] + [shift(pick(hidden, (y + by) % 4, 1), "y", by) for by in (1, 2, 3)]

    dq, theirs, mine = attention(core, bias, queries[:, 0], grad_out[:, 0], kv, kv1, kv2)
    states, theirs = lax.optimization_barrier((states, theirs))
    theirs = shift(theirs, "core", 1)
    halves = []
    for part in range(2):
        cols = slice(part * PAIR, (part + 1) * PAIR)
        (m_own, m_one, m_two), (g_own, g_one, g_two) = mine[:, cols].reshape(3, TOK, PAIR), theirs[:, cols].reshape(3, TOK, PAIR)
        g_own, g_one, g_two = (term.astype(jnp.float32) for term in (g_own, g_one, g_two))
        back = jnp.concatenate([m_two + jnp.where(first, 0.0, g_one), g_two + jnp.where(first, m_one, 0.0)], axis=0)
        here = jnp.concatenate([m_own + jnp.where(first, g_one, 0.0), g_own + jnp.where(first, 0.0, m_one)], axis=0)
        back = back.astype(jnp.bfloat16)
        halves.append((here, ctx_shift(back, -2)))

    states, _ = lax.optimization_barrier((states, back))
    states = jnp.stack(states)
    other_states = shift(states, "core", 1)

    blocks, reduced = [], []
    for here, came in halves:
        block = (here + came.astype(jnp.float32)).astype(jnp.bfloat16)
        blocks.append(block)
        gathered = [block] + [shift(block, "zl", by) for by in (1, 2, 3)]
        pieces = products(jnp.stack([zl, x, y]).astype(jnp.int32), states, other_states, gathered)
        got = [pieces[0]] + [shift(pieces[by], "x", by) for by in (1, 2, 3)]
        reduced.append(total(got).astype(jnp.bfloat16))
    block = jnp.concatenate(blocks, axis=1)
    partial = jnp.concatenate(reduced, axis=2)

    got = lax.all_to_all(partial.reshape(8, 40, 2 * PAIR), ("y", "zh"), 0, 0)
    rows = jnp.sum(got.astype(jnp.float32), axis=0).reshape(2, 20, 2 * PAIR)
    ours = pick(rows, core, 0)
    others = shift(pick(rows, 1 - core, 0), "core", 1)

    def assemble(own, other):
        count = own.shape[0]
        cols = jnp.concatenate([jnp.where(first, own, other), jnp.where(first, other, own)], axis=1)
        return cols.reshape(count, KV_HEADS, 2, HEAD_DIM).transpose(0, 2, 1, 3).reshape(count, KV_HEADS * PAIR)

    weight = assemble(ours, others)
    kv_out = assemble(block[:TOK], shift(block[TOK:], "core", 1))
    return dq[:, None], kv_out[None], weight


def solution(mesh):
    fine = Mesh(mesh.devices.reshape(4, 4, 4, 2, 2), AXES)
    dp, ctx = ("zl", "y"), ("x", "zh", "core")
    placed = (
        P(None, dp, ctx, None),
        P(dp, ctx, None),
        P(None, dp, ctx, None),
        P(None, ctx, dp),
        P(dp, None),
    )
    return jax.shard_map(
        on_device,
        mesh=fine,
        in_specs=placed,
        out_specs=(P(None, dp, ctx, None), P(dp, ctx, None), P(dp + ctx, None)),
        check_vma=False,
    )
```

time: 143 us -> 121 us (0.85)
  waiting for transfers between devices: 56.4 us -> 23.7 us
  starting transfers between devices: 60.3 us -> 72.2 us
  other arithmetic: 1.9 us -> 4.78 us
  matrix products: 2.74 us -> 0 us
    ppermute x25 -> x20, waiting for transfers between devices: 39.4 us -> 13.7 us  [shift(): lax.ppermute(value, axis, [(i, (i + by) % size) for i in range(size)])]
    ppermute x25 -> x20, starting transfers between devices: 26.9 us -> 44.6 us  [shift(): lax.ppermute(value, axis, [(i, (i + by) % size) for i in range(size)])]
    ppermute x7 -> x0, starting transfers between devices: 15.6 us -> none  [z_shift(): return lax.ppermute(value, ('zl', 'zh'), pairs)]
    ppermute x4 -> x3, waiting for transfers between devices: 12.8 us -> 5.85 us  [ctx_shift(): return lax.ppermute(value, ('x', 'zh', 'core'), pairs)]
    all_to_all x0 -> x1, starting transfers between devices: none -> 5.79 us  [on_device(): got = lax.all_to_all(partial.reshape(8, 40, 2 * PAIR), ('y', 'zh'), 0, 0)]
    ppermute x7 -> x0, waiting for transfers between devices: 4.26 us -> none  [z_shift(): return lax.ppermute(value, ('zl', 'zh'), pairs)]
    all_to_all x0 -> x1, waiting for transfers between devices: none -> 4.14 us  [on_device(): got = lax.all_to_all(partial.reshape(8, 40, 2 * PAIR), ('y', 'zh'), 0, 0)]
    pallas_call x0 -> x2, Pallas kernels: none -> 4.1 us  [products(): pl.pallas_call(product_kernel, grid_spec=pltpu.PrefetchScalarGridSpec(num...]
  transfers between devices with their start and end apart: 36 -> 24, of which waited for: 12 -> 11; matrix products, arithmetic and copies ran while one was open for 5% -> 3% of each run, Pallas kernels for 5% -> 11%
where the time goes in v3:
time: 121 us; the launch traced here: 119 us
  starting transfers between devices  72.2 us (60%)
  waiting for transfers between devices  23.7 us (20%)
  Pallas kernels  13.5 us (11%)
  other arithmetic  4.78 us (4%)
  local copies, waits for them, and re-layouts  4.15 us (3%)
    ppermute x20, starting transfers between devices, shift(): lax.ppermute(value, axis, [(i, (i + by) % size) for i in range(size)])  44.6 us
    ppermute x3, starting transfers between devices, ctx_shift(): return lax.ppermute(value, ('x', 'zh', 'core'), pairs)  21.9 us
    ppermute x20, waiting for transfers between devices, shift(): lax.ppermute(value, axis, [(i, (i + by) % size) for i in range(size)])  13.7 us
    pallas_call x1, Pallas kernels, attention(): pl.pallas_call(attention_kernel, grid_spec=pltpu.PrefetchScalarGridSpec(n...  9.44 us
    ppermute x3, waiting for transfers between devices, ctx_shift(): return lax.ppermute(value, ('x', 'zh', 'core'), pairs)  5.85 us
    all_to_all x1, starting transfers between devices, on_device(): got = lax.all_to_all(partial.reshape(8, 40, 2 * PAIR), ('y', 'zh'), 0, 0)  5.79 us
    all_to_all x1, waiting for transfers between devices, on_device(): got = lax.all_to_all(partial.reshape(8, 40, 2 * PAIR), ('y', 'zh'), 0, 0)  4.14 us
    pallas_call x2, Pallas kernels, products(): pl.pallas_call(product_kernel, grid_spec=pltpu.PrefetchScalarGridSpec(num...  4.1 us
  transfers between devices with their start and end apart: 24, of which 11 were waited for; matrix products, arithmetic and copies ran while one was open for 3% of the time, Pallas kernels for 11%

profile of v3, /device:TPU:3, one launch (start us, length us, event | category | flops | bytes accessed | tf_op | source)
XLA Modules:
  0.0 119.3 jit_solution(12781359846394632394)
XLA Ops:
  0.6 8.8 %collective-permute-start = (bf16[128,1024]{1,0:T(8,128)(2,1)}, bf16[128,1024]{1,0:T(8,128)(2,1)S(1)}, u32[]{:S(2)}, u32[]{:S(2)}) collective-permute-start(bf16[128,1024]{1,0:T(8,128)(2,1)} %bitcast.50), channel_id=1, source_target_pairs={{0,2},{1,3},{2,4},{3,5},{4,6},{5,7},{6,8},{7,9},{8,10},{9,11},{10,... | collective-permute-start | bytes 786440 | tf_op jit(solution)/shard_map/ppermute | solution.py:31
  9.5 1.4 %dynamic-slice_bitcast_fusion = (bf16[4,320,128]{2,1,0:T(8,128)(2,1)S(1)}, bf16[4,320,128]{2,1,0:T(8,128)(2,1)S(1)}, bf16[4,320,128]{2,1,0:T(8,128)(2,1)S(1)}, bf16[4,320,128]{2,1,0:T(8,128)(2,1)S(1)}) fusion(bf16[4,4,320,128]{3,2,1,0:T(8,128)(2,1)} %bitcast.44, s32[]{:T(128)S(6)} %select_n.125, s32[]{:T(128)S(6)} %select_n.123, s32[]{:T(128)S(6)} %select_n.121, ...), kind=kLoop, calls=%fused_computation.5 | loop fusion | bytes 2621456 | tf_op jit(solution)/shard_map/jit(dynamic_index_in_dim)/squeeze | solution.py:186
  10.9 1.4 %collective-permute-start.2 = (bf16[4,320,128]{2,1,0:T(8,128)(2,1)S(1)}, bf16[4,320,128]{2,1,0:T(8,128)(2,1)S(1)}, u32[]{:S(2)}, u32[]{:S(2)}) collective-permute-start(bf16[4,320,128]{2,1,0:T(8,128)(2,1)S(1)} %get-tuple-element.60), channel_id=1, source_target_pairs={{0,16},{16,32},{32,48},{48,0},{1,17},{17,33},{33,49},{49,1},{2,18}... | collective-permute-start | bytes 983048 | tf_op jit(solution)/shard_map/ppermute | solution.py:26
  12.3 2.6 %collective-permute-start.3 = (bf16[4,320,128]{2,1,0:T(8,128)(2,1)S(1)}, bf16[4,320,128]{2,1,0:T(8,128)(2,1)S(1)}, u32[]{:S(2)}, u32[]{:S(2)}) collective-permute-start(bf16[4,320,128]{2,1,0:T(8,128)(2,1)S(1)} %get-tuple-element.59), channel_id=1, source_target_pairs={{0,32},{16,48},{32,0},{48,16},{1,33},{17,49},{33,1},{49,17},{2,34}... | collective-permute-start | bytes 983048 | tf_op jit(solution)/shard_map/ppermute | solution.py:26
  14.9 1.1 collective-permute-start.4
  16.2 0.1 reduce
  16.3 0.1 convert_reduce_fusion.2
  16.4 0.3 collective-permute-done.k2_ref.v2_ref
  16.7 1.6 %collective-permute-start.1 = (bf16[128,1024]{1,0:T(8,128)(2,1)S(1)}, bf16[128,1024]{1,0:T(8,128)(2,1)S(1)}, u32[]{:S(2)}, u32[]{:S(2)}) collective-permute-start(bf16[128,1024]{1,0:T(8,128)(2,1)S(1)} %broadcast_select_fusion), channel_id=1, source_target_pairs={{0,1},{1,0},{2,3},{3,2},{4,5},{5,4},{6,7},{7,6},{8,9},{9,8},{10,11... | collective-permute-start | bytes 786440 | tf_op jit(solution)/shard_map/ppermute | solution.py:26
  18.3 0.2 fusion.9
  18.5 0.7 add_select_fusion.bias_ref
  19.2 0.3 collective-permute-done.1.k1_ref.v1_ref
  19.5 0.7 copy-done.4
  20.2 9.4 %attention.1 = (bf16[2,128,2560]{2,1,0:T(8,128)(2,1)}, bf16[384,512]{1,0:T(8,128)(2,1)}, f32[384,512]{1,0:T(8,128)}) custom-call(s32[1]{0:T(128)} %bitcast.core_ref, f32[256,128]{1,0:T(8,128)} %add_select_fusion.bias_ref, bf16[2,128,2560]{2,1,0:T(8,128)(2,1)} %bitcast.54, bf16[2,128,2560]{2,1,0:T(8,128)(2,1)} %bitcast.55, bf16[128,1024]{1,0:T(8,128)(2,1)} %bitcast.51, ...), custom_call_target="tpu_custom_call" | custom-call | flops 6000000000 | bytes 9000000 | tf_op jit(solution)/shard_map/attention/pallas_call | solution.py:119
  29.7 1.0 collective-permute-start.5
  30.6 1.6 %collective-permute-done.5 = bf16[384,512]{1,0:T(8,128)(2,1)S(1)} collective-permute-done((bf16[384,512]{1,0:T(8,128)(2,1)}, bf16[384,512]{1,0:T(8,128)(2,1)S(1)}, u32[]{:S(2)}, u32[]{:S(2)}) %collective-permute-start.5) | collective-permute-done | bytes 393248 | tf_op jit(solution)/shard_map/ppermute | solution.py:26
  32.2 1.3 %fusion.4 = (bf16[128,256]{1,0:T(8,128)(2,1)S(1)}, bf16[128,256]{1,0:T(8,128)(2,1)S(1)}, bf16[128,256]{1,0:T(8,128)(2,1)S(1)}, bf16[128,256]{1,0:T(8,128)(2,1)S(...) fusion(f32[384,512]{1,0:T(8,128)} %get-tuple-element.24, ...), kind=kLoop, calls=%fused_computation.23 | loop fusion | flops 851968 | bytes 1966081 | tf_op jit(solution)/shard_map/convert.2
  33.5 1.1 pad_maximum_fusion.own_ref
  34.7 0.5 collective-permute-start.9
  35.1 11.1 %collective-permute-start.6 = (bf16[256,256]{1,0:T(8,128)(2,1)S(1)}, bf16[256,256]{1,0:T(8,128)(2,1)S(1)}, u32[]{:S(2)}, u32[]{:S(2)}) collective-permute-start(bf16[256,256]{1,0:T(8,128)(2,1)S(1)} %pad_maximum_fusion.4), channel_id=1, source_target_pairs={{2,0},{3,1},{4,2},{5,3},{6,4},{7,5},{8,6},{9,7},{10,8},{11,9},{12,... | collective-permute-start | bytes 393224 | tf_op jit(solution)/shard_map/ppermute | solution.py:31
  46.4 1.9 %collective-permute-start.7 = (bf16[256,256]{1,0:T(8,128)(2,1)S(1)}, bf16[256,256]{1,0:T(8,128)(2,1)S(1)}, u32[]{:S(2)}, u32[]{:S(2)}) collective-permute-start(bf16[256,256]{1,0:T(8,128)(2,1)S(1)} %pad_maximum_fusion.5), channel_id=1, source_target_pairs={{2,0},{3,1},{4,2},{5,3},{6,4},{7,5},{8,6},{9,7},{10,8},{11,9},{12,... | collective-permute-start | bytes 393224 | tf_op jit(solution)/shard_map/ppermute | solution.py:31
  48.3 1.7 %collective-permute-done.6 = bf16[256,256]{1,0:T(8,128)(2,1)S(1)} collective-permute-done((bf16[256,256]{1,0:T(8,128)(2,1)S(1)}, bf16[256,256]{1,0:T(8,128)(2,1)S(1)}, u32[]{:S(2)}, u32[]{:S(2)}) %collective-permute-start.6) | collective-permute-done | bytes 131104 | tf_op jit(solution)/shard_map/ppermute | solution.py:31
  50.2 6.4 %collective-permute-start.11 = (bf16[256,256]{1,0:T(8,128)(2,1)S(1)}, bf16[256,256]{1,0:T(8,128)(2,1)S(1)}, u32[]{:S(2)}, u32[]{:S(2)}) collective-permute-start(bf16[256,256]{1,0:T(8,128)(2,1)S(1)} %fusion.refs_0_), channel_id=1, source_target_pairs={{0,128},{64,192},{128,0},{192,64},{1,129},{65,193},{129,1},{193,65... | collective-permute-start | bytes 393224 | tf_op jit(solution)/shard_map/ppermute | solution.py:26
  56.6 1.1 collective-permute-start.12
  57.7 3.8 %collective-permute-done.7 = bf16[256,256]{1,0:T(8,128)(2,1)S(1)} collective-permute-done((bf16[256,256]{1,0:T(8,128)(2,1)S(1)}, bf16[256,256]{1,0:T(8,128)(2,1)S(1)}, u32[]{:S(2)}, u32[]{:S(2)}) %collective-permute-start.7) | collective-permute-done | bytes 131104 | tf_op jit(solution)/shard_map/ppermute | solution.py:31
  61.6 2.5 %collective-permute-start.17 = (bf16[256,256]{1,0:T(8,128)(2,1)S(1)}, bf16[256,256]{1,0:T(8,128)(2,1)S(1)}, u32[]{:S(2)}, u32[]{:S(2)}) collective-permute-start(bf16[256,256]{1,0:T(8,128)(2,1)S(1)} %fusion.1.refs_0_), channel_id=1, source_target_pairs={{0,128},{64,192},{128,0},{192,64},{1,129},{65,193},{129,1},{193,65... | collective-permute-start | bytes 393224 | tf_op jit(solution)/shard_map/ppermute | solution.py:26
  64.1 3.0 %collective-permute-done.11.refs_2_ = bf16[256,256]{1,0:T(8,128)(2,1)S(1)} collective-permute-done((bf16[256,256]{1,0:T(8,128)(2,1)S(1)}, bf16[256,256]{1,0:T(8,128)(2,1)S(1)}, u32[]{:S(2)}, u32[]{:S(2)}) %collective-permute-start.11) | collective-permute-done | bytes 131104 | tf_op jit(solution)/shard_map/ppermute | solution.py:26
  67.2 6.2 %collective-permute-start.18 = (bf16[256,256]{1,0:T(8,128)(2,1)S(1)}, bf16[256,256]{1,0:T(8,128)(2,1)S(1)}, u32[]{:S(2)}, u32[]{:S(2)}) collective-permute-start(bf16[256,256]{1,0:T(8,128)(2,1)S(1)} %fusion.1.refs_0_), channel_id=1, source_target_pairs={{0,192},{64,0},{128,64},{192,128},{1,193},{65,1},{129,65},{193,129... | collective-permute-start | bytes 393224 | tf_op jit(solution)/shard_map/ppermute | solution.py:26
  73.4 2.0 %products.2 = (bf16[4,80,256]{2,1,0:T(8,128)(2,1)S(1)}, bf16[4,80,256]{2,1,0:T(8,128)(2,1)S(1)}, bf16[4,80,256]{2,1,0:T(8,128)(2,1)S(1)}, bf16[4,80,256]{2,1,0:T(8,128)(2,1)S(1)}) custom-call(s32[3]{0:T(128)S(1)} %pad_add_fusion.at_ref, bf16[4,4,320,128]{3,2,1,0:T(8,128)(2,1)S(1)} %pad_maximum_fusion.own_ref, ...), custom_call_target="tpu_custom_call" | custom-call | flops 1400000000 | bytes 5000000 | tf_op jit(solution)/shard_map/products/pallas_call | solution.py:155
  75.5 1.4 %collective-permute-start.13 = (bf16[4,80,256]{2,1,0:T(8,128)(2,1)S(1)}, bf16[4,80,256]{2,1,0:T(8,128)(2,1)S(1)}, u32[]{:S(2)}, u32[]{:S(2)}) collective-permute-start(bf16[4,80,256]{2,1,0:T(8,128)(2,1)S(1)} %get-tuple-element.36), channel_id=1, source_target_pairs={{0,4},{4,8},{8,12},{12,0},{1,5},{5,9},{9,13},{13,1},{2,6},{6,10},{... | collective-permute-start | bytes 491528 | tf_op jit(solution)/shard_map/ppermute | solution.py:26
  76.9 2.1 %collective-permute-start.15 = (bf16[4,80,256]{2,1,0:T(8,128)(2,1)S(1)}, bf16[4,80,256]{2,1,0:T(8,128)(2,1)S(1)}, u32[]{:S(2)}, u32[]{:S(2)}) collective-permute-start(bf16[4,80,256]{2,1,0:T(8,128)(2,1)S(1)} %get-tuple-element.38), channel_id=1, source_target_pairs={{0,12},{4,0},{8,4},{12,8},{1,13},{5,1},{9,5},{13,9},{2,14},{6,2},{... | collective-permute-start | bytes 491528 | tf_op jit(solution)/shard_map/ppermute | solution.py:26
  78.9 2.1 %products.3 = (bf16[4,80,256]{2,1,0:T(8,128)(2,1)S(1)}, bf16[4,80,256]{2,1,0:T(8,128)(2,1)S(1)}, bf16[4,80,256]{2,1,0:T(8,128)(2,1)S(1)}, bf16[4,80,256]{2,1,0:T(8,128)(2,1)S(1)}) custom-call(s32[3]{0:T(128)S(1)} %pad_add_fusion.at_ref, bf16[4,4,320,128]{3,2,1,0:T(8,128)(2,1)S(1)} %pad_maximum_fusion.own_ref, ...), custom_call_target="tpu_custom_call" | custom-call | flops 1400000000 | bytes 5000000 | tf_op jit(solution)/shard_map/products/pallas_call | solution.py:155
  81.0 1.8 %collective-permute-start.19 = (bf16[4,80,256]{2,1,0:T(8,128)(2,1)S(1)}, bf16[4,80,256]{2,1,0:T(8,128)(2,1)S(1)}, u32[]{:S(2)}, u32[]{:S(2)}) collective-permute-start(bf16[4,80,256]{2,1,0:T(8,128)(2,1)S(1)} %get-tuple-element.40), channel_id=1, source_target_pairs={{0,4},{4,8},{8,12},{12,0},{1,5},{5,9},{9,13},{13,1},{2,6},{6,10},{... | collective-permute-start | bytes 491528 | tf_op jit(solution)/shard_map/ppermute | solution.py:26
  82.8 1.9 %collective-permute-start.20 = (bf16[4,80,256]{2,1,0:T(8,128)(2,1)S(1)}, bf16[4,80,256]{2,1,0:T(8,128)(2,1)S(1)}, u32[]{:S(2)}, u32[]{:S(2)}) collective-permute-start(bf16[4,80,256]{2,1,0:T(8,128)(2,1)S(1)} %get-tuple-element.41), channel_id=1, source_target_pairs={{0,8},{4,12},{8,0},{12,4},{1,9},{5,13},{9,1},{13,5},{2,10},{6,14},... | collective-permute-start | bytes 491528 | tf_op jit(solution)/shard_map/ppermute | solution.py:26
  84.7 0.1 add_convert_fusion.1
  84.8 1.1 collective-permute-done.19
  85.9 4.4 %collective-permute-done.20 = bf16[4,80,256]{2,1,0:T(8,128)(2,1)S(1)} collective-permute-done((bf16[4,80,256]{2,1,0:T(8,128)(2,1)S(1)}, bf16[4,80,256]{2,1,0:T(8,128)(2,1)S(1)}, u32[]{:S(2)}, u32[]{:S(2)}) %collective-permute-start.20) | collective-permute-done | bytes 163872 | tf_op jit(solution)/shard_map/ppermute | solution.py:26
  90.3 2.3 %collective-permute-done.21 = bf16[4,80,256]{2,1,0:T(8,128)(2,1)S(1)} collective-permute-done((bf16[4,80,256]{2,1,0:T(8,128)(2,1)S(1)}, bf16[4,80,256]{2,1,0:T(8,128)(2,1)S(1)}, u32[]{:S(2)}, u32[]{:S(2)}) %collective-permute-start.21) | collective-permute-done | bytes 163872 | tf_op jit(solution)/shard_map/ppermute | solution.py:26
  92.6 0.7 pad_maximum_fusion.1
  93.3 5.8 %all-to-all-start = ((bf16[8,40,512]{2,1,0:T(8,128)(2,1)}), bf16[8,40,512]{2,1,0:T(8,128)(2,1)S(1)}, u32[]{:S(2)}, u32[]{:S(2)}) async-start(bf16[8,40,512]{2,1,0:T(8,128)(2,1)} %bitcast.21), calls=%async_computation | async-start | bytes 655360 | tf_op jit(solution)/shard_map/all_to_all | solution.py:237
  99.1 5.4 %collective-permute-start.8 = (bf16[128,512]{1,0:T(8,128)(2,1)S(1)}, bf16[128,512]{1,0:T(8,128)(2,1)S(1)}, u32[]{:S(2)}, u32[]{:S(2)}) collective-permute-start(bf16[128,512]{1,0:T(8,128)(2,1)S(1)} %pad_maximum_fusion.3), channel_id=1, source_target_pairs={{0,1},{1,0},{2,3},{3,2},{4,5},{5,4},{6,7},{7,6},{8,9},{9,8},{10,11... | collective-permute-start | bytes 393224 | tf_op jit(solution)/shard_map/ppermute | solution.py:26
  104.5 1.0 collective-permute-done.8
  105.5 4.1 %all-to-all-done = bf16[8,40,512]{2,1,0:T(8,128)(2,1)S(1)} async-done(((bf16[8,40,512]{2,1,0:T(8,128)(2,1)}), bf16[8,40,512]{2,1,0:T(8,128)(2,1)S(1)}, u32[]{:S(2)}, u32[]{:S(2)}) %all-to-all-start) | async-done | bytes 327712 | tf_op jit(solution)/shard_map/all_to_all | solution.py:237
  109.8 7.5 %collective-permute-start.22 = (f32[20,512]{1,0:T(8,128)S(1)}, f32[20,512]{1,0:T(8,128)S(1)}, u32[]{:S(2)}, u32[]{:S(2)}) collective-permute-start(f32[20,512]{1,0:T(8,128)S(1)} %dynamic-slice_bitcast_fusion.4), channel_id=1, source_target_pairs={{0,1},{1,0},{2,3},{3,2},{4,5},{5,4},{6,7},{7,6},{8,9},{9,8},{10,11... | collective-permute-start | bytes 122888 | tf_op jit(solution)/shard_map/ppermute | solution.py:26
  117.3 0.2 reshape.104
  117.5 0.1 copy.35
  117.6 0.9 broadcast_in_dim_reshape.3
  118.6 0.7 reshape.108
  (49 shorter events, 0.9 us)
Async XLA Ops:
  0.6 16.0 %collective-permute-start = (bf16[128,1024]{1,0:T(8,128)(2,1)}, bf16[128,1024]{1,0:T(8,128)(2,1)S(1)}, u32[]{:S(2)}, u32[]{:S(2)}) collective-permute-start(bf16[128,1024]{1,0:T(8,128)(2,1)} %bitcast.50), channel_id=1, source_target_pairs={{0,2},{1,3},{2,4},{3,5},{4,6},{5,7},{6,8},{7,9},{8,10},{9,11},{10,... | collective-permute-start | bytes 786440 | tf_op jit(solution)/shard_map/ppermute | solution.py:31
  9.5 6.5 %copy-start.3 = (s32[1,16]{1,0:T(1,128)S(1)}, s32[1,16]{1,0:T(1,128)}, u32[]{:S(2)}) copy-start(s32[1,16]{1,0:T(1,128)} %param.9) | copy-start | bytes 196
  9.5 7.1 %copy-start.1 = (bf16[1,128,1024]{2,1,0:T(8,128)(2,1)S(1)}, bf16[1,128,1024]{2,1,0:T(8,128)(2,1)}, u32[]{:S(2)}) copy-start(bf16[1,128,1024]{2,1,0:T(8,128)(2,1)} %param.6) | copy-start | bytes 786436
  10.9 18.7 %collective-permute-start.2 = (bf16[4,320,128]{2,1,0:T(8,128)(2,1)S(1)}, bf16[4,320,128]{2,1,0:T(8,128)(2,1)S(1)}, u32[]{:S(2)}, u32[]{:S(2)}) collective-permute-start(bf16[4,320,128]{2,1,0:T(8,128)(2,1)S(1)} %get-tuple-element.60), channel_id=1, source_target_pairs={{0,16},{16,32},{32,48},{48,0},{1,17},{17,33},{33,49},{49,1},{2,18}... | collective-permute-start | bytes 983048 | tf_op jit(solution)/shard_map/ppermute | solution.py:26
  12.3 17.3 %collective-permute-start.3 = (bf16[4,320,128]{2,1,0:T(8,128)(2,1)S(1)}, bf16[4,320,128]{2,1,0:T(8,128)(2,1)S(1)}, u32[]{:S(2)}, u32[]{:S(2)}) collective-permute-start(bf16[4,320,128]{2,1,0:T(8,128)(2,1)S(1)} %get-tuple-element.59), channel_id=1, source_target_pairs={{0,32},{16,48},{32,0},{48,16},{1,33},{17,49},{33,1},{49,17},{2,34}... | collective-permute-start | bytes 983048 | tf_op jit(solution)/shard_map/ppermute | solution.py:26
  14.9 14.7 %collective-permute-start.4 = (bf16[4,320,128]{2,1,0:T(8,128)(2,1)S(1)}, bf16[4,320,128]{2,1,0:T(8,128)(2,1)S(1)}, u32[]{:S(2)}, u32[]{:S(2)}) collective-permute-start(bf16[4,320,128]{2,1,0:T(8,128)(2,1)S(1)} %get-tuple-element.58), channel_id=1, source_target_pairs={{0,48},{16,0},{32,16},{48,32},{1,49},{17,1},{33,17},{49,33},{2,50}... | collective-permute-start | bytes 983048 | tf_op jit(solution)/shard_map/ppermute | solution.py:26
  16.6 2.8 %copy-start.2 = (bf16[128,1024]{1,0:T(8,128)(2,1)}, bf16[128,1024]{1,0:T(8,128)(2,1)S(1)}, u32[]{:S(2)}) copy-start(bf16[128,1024]{1,0:T(8,128)(2,1)S(1)} %collective-permute-done.k2_ref.v2_ref) | copy-start | bytes 786436
  16.7 2.8 %collective-permute-start.1 = (bf16[128,1024]{1,0:T(8,128)(2,1)S(1)}, bf16[128,1024]{1,0:T(8,128)(2,1)S(1)}, u32[]{:S(2)}, u32[]{:S(2)}) collective-permute-start(bf16[128,1024]{1,0:T(8,128)(2,1)S(1)} %broadcast_select_fusion), channel_id=1, source_target_pairs={{0,1},{1,0},{2,3},{3,2},{4,5},{5,4},{6,7},{7,6},{8,9},{9,8},{10,11... | collective-permute-start | bytes 786440 | tf_op jit(solution)/shard_map/ppermute | solution.py:26
  19.5 0.7 copy-start.4
  29.7 3.9 %copy-start = (bf16[4,320,128]{2,1,0:T(8,128)(2,1)}, bf16[4,320,128]{2,1,0:T(8,128)(2,1)S(1)}, u32[]{:S(2)}) copy-start(bf16[4,320,128]{2,1,0:T(8,128)(2,1)S(1)} %collective-permute-done.4) | copy-start | bytes 983044
  29.7 2.5 %collective-permute-start.5 = (bf16[384,512]{1,0:T(8,128)(2,1)}, bf16[384,512]{1,0:T(8,128)(2,1)S(1)}, u32[]{:S(2)}, u32[]{:S(2)}) collective-permute-start(bf16[384,512]{1,0:T(8,128)(2,1)} %get-tuple-element.26), channel_id=1, source_target_pairs={{0,1},{1,0},{2,3},{3,2},{4,5},{5,4},{6,7},{7,6},{8,9},{9,8},{10,11... | collective-permute-start | bytes 1179656 | tf_op jit(solution)/shard_map/ppermute | solution.py:26
  34.7 38.8 %collective-permute-start.9 = (bf16[4,4,320,128]{3,2,1,0:T(8,128)(2,1)S(1)}, bf16[4,4,320,128]{3,2,1,0:T(8,128)(2,1)S(1)}, u32[]{:S(2)}, u32[]{:S(2)}) collective-permute-start(bf16[4,4,320,128]{3,2,1,0:T(8,128)(2,1)S(1)} %pad_maximum_fusion.own_ref), channel_id=1, source_target_pairs={{0,1},{1,0},{2,3},{3,2},{4,5},{5,4},{6,7},{7,6},{8,9},{9,8},{10,11... | collective-permute-start | bytes 3932168 | tf_op jit(solution)/shard_map/ppermute | solution.py:26
  35.1 14.9 %collective-permute-start.6 = (bf16[256,256]{1,0:T(8,128)(2,1)S(1)}, bf16[256,256]{1,0:T(8,128)(2,1)S(1)}, u32[]{:S(2)}, u32[]{:S(2)}) collective-permute-start(bf16[256,256]{1,0:T(8,128)(2,1)S(1)} %pad_maximum_fusion.4), channel_id=1, source_target_pairs={{2,0},{3,1},{4,2},{5,3},{6,4},{7,5},{8,6},{9,7},{10,8},{11,9},{12,... | collective-permute-start | bytes 393224 | tf_op jit(solution)/shard_map/ppermute | solution.py:31
  46.4 15.1 %collective-permute-start.7 = (bf16[256,256]{1,0:T(8,128)(2,1)S(1)}, bf16[256,256]{1,0:T(8,128)(2,1)S(1)}, u32[]{:S(2)}, u32[]{:S(2)}) collective-permute-start(bf16[256,256]{1,0:T(8,128)(2,1)S(1)} %pad_maximum_fusion.5), channel_id=1, source_target_pairs={{2,0},{3,1},{4,2},{5,3},{6,4},{7,5},{8,6},{9,7},{10,8},{11,9},{12,... | collective-permute-start | bytes 393224 | tf_op jit(solution)/shard_map/ppermute | solution.py:31
  50.1 11.6 %collective-permute-start.10 = (bf16[256,256]{1,0:T(8,128)(2,1)S(1)}, bf16[256,256]{1,0:T(8,128)(2,1)S(1)}, u32[]{:S(2)}, u32[]{:S(2)}) collective-permute-start(bf16[256,256]{1,0:T(8,128)(2,1)S(1)} %fusion.refs_0_), channel_id=1, source_target_pairs={{0,64},{64,128},{128,192},{192,0},{1,65},{65,129},{129,193},{193,1... | collective-permute-start | bytes 393224 | tf_op jit(solution)/shard_map/ppermute | solution.py:26
  50.2 17.0 %collective-permute-start.11 = (bf16[256,256]{1,0:T(8,128)(2,1)S(1)}, bf16[256,256]{1,0:T(8,128)(2,1)S(1)}, u32[]{:S(2)}, u32[]{:S(2)}) collective-permute-start(bf16[256,256]{1,0:T(8,128)(2,1)S(1)} %fusion.refs_0_), channel_id=1, source_target_pairs={{0,128},{64,192},{128,0},{192,64},{1,129},{65,193},{129,1},{193,65... | collective-permute-start | bytes 393224 | tf_op jit(solution)/shard_map/ppermute | solution.py:26
  56.6 16.9 %collective-permute-start.12 = (bf16[256,256]{1,0:T(8,128)(2,1)S(1)}, bf16[256,256]{1,0:T(8,128)(2,1)S(1)}, u32[]{:S(2)}, u32[]{:S(2)}) collective-permute-start(bf16[256,256]{1,0:T(8,128)(2,1)S(1)} %fusion.refs_0_), channel_id=1, source_target_pairs={{0,192},{64,0},{128,64},{192,128},{1,193},{65,1},{129,65},{193,129... | collective-permute-start | bytes 393224 | tf_op jit(solution)/shard_map/ppermute | solution.py:26
  61.5 15.3 %collective-permute-start.16 = (bf16[256,256]{1,0:T(8,128)(2,1)S(1)}, bf16[256,256]{1,0:T(8,128)(2,1)S(1)}, u32[]{:S(2)}, u32[]{:S(2)}) collective-permute-start(bf16[256,256]{1,0:T(8,128)(2,1)S(1)} %fusion.1.refs_0_), channel_id=1, source_target_pairs={{0,64},{64,128},{128,192},{192,0},{1,65},{65,129},{129,193},{193,1... | collective-permute-start | bytes 393224 | tf_op jit(solution)/shard_map/ppermute | solution.py:26
  61.6 17.3 %collective-permute-start.17 = (bf16[256,256]{1,0:T(8,128)(2,1)S(1)}, bf16[256,256]{1,0:T(8,128)(2,1)S(1)}, u32[]{:S(2)}, u32[]{:S(2)}) collective-permute-start(bf16[256,256]{1,0:T(8,128)(2,1)S(1)} %fusion.1.refs_0_), channel_id=1, source_target_pairs={{0,128},{64,192},{128,0},{192,64},{1,129},{65,193},{129,1},{193,65... | collective-permute-start | bytes 393224 | tf_op jit(solution)/shard_map/ppermute | solution.py:26
  67.2 11.8 %collective-permute-start.18 = (bf16[256,256]{1,0:T(8,128)(2,1)S(1)}, bf16[256,256]{1,0:T(8,128)(2,1)S(1)}, u32[]{:S(2)}, u32[]{:S(2)}) collective-permute-start(bf16[256,256]{1,0:T(8,128)(2,1)S(1)} %fusion.1.refs_0_), channel_id=1, source_target_pairs={{0,192},{64,0},{128,64},{192,128},{1,193},{65,1},{129,65},{193,129... | collective-permute-start | bytes 393224 | tf_op jit(solution)/shard_map/ppermute | solution.py:26
  75.5 9.2 %collective-permute-start.13 = (bf16[4,80,256]{2,1,0:T(8,128)(2,1)S(1)}, bf16[4,80,256]{2,1,0:T(8,128)(2,1)S(1)}, u32[]{:S(2)}, u32[]{:S(2)}) collective-permute-start(bf16[4,80,256]{2,1,0:T(8,128)(2,1)S(1)} %get-tuple-element.36), channel_id=1, source_target_pairs={{0,4},{4,8},{8,12},{12,0},{1,5},{5,9},{9,13},{13,1},{2,6},{6,10},{... | collective-permute-start | bytes 491528 | tf_op jit(solution)/shard_map/ppermute | solution.py:26
  76.9 7.8 %collective-permute-start.14 = (bf16[4,80,256]{2,1,0:T(8,128)(2,1)S(1)}, bf16[4,80,256]{2,1,0:T(8,128)(2,1)S(1)}, u32[]{:S(2)}, u32[]{:S(2)}) collective-permute-start(bf16[4,80,256]{2,1,0:T(8,128)(2,1)S(1)} %get-tuple-element.37), channel_id=1, source_target_pairs={{0,8},{4,12},{8,0},{12,4},{1,9},{5,13},{9,1},{13,5},{2,10},{6,14},... | collective-permute-start | bytes 491528 | tf_op jit(solution)/shard_map/ppermute | solution.py:26
  76.9 7.8 %collective-permute-start.15 = (bf16[4,80,256]{2,1,0:T(8,128)(2,1)S(1)}, bf16[4,80,256]{2,1,0:T(8,128)(2,1)S(1)}, u32[]{:S(2)}, u32[]{:S(2)}) collective-permute-start(bf16[4,80,256]{2,1,0:T(8,128)(2,1)S(1)} %get-tuple-element.38), channel_id=1, source_target_pairs={{0,12},{4,0},{8,4},{12,8},{1,13},{5,1},{9,5},{13,9},{2,14},{6,2},{... | collective-permute-start | bytes 491528 | tf_op jit(solution)/shard_map/ppermute | solution.py:26
  81.0 4.9 %collective-permute-start.19 = (bf16[4,80,256]{2,1,0:T(8,128)(2,1)S(1)}, bf16[4,80,256]{2,1,0:T(8,128)(2,1)S(1)}, u32[]{:S(2)}, u32[]{:S(2)}) collective-permute-start(bf16[4,80,256]{2,1,0:T(8,128)(2,1)S(1)} %get-tuple-element.40), channel_id=1, source_target_pairs={{0,4},{4,8},{8,12},{12,0},{1,5},{5,9},{9,13},{13,1},{2,6},{6,10},{... | collective-permute-start | bytes 491528 | tf_op jit(solution)/shard_map/ppermute | solution.py:26
  82.8 7.5 %collective-permute-start.20 = (bf16[4,80,256]{2,1,0:T(8,128)(2,1)S(1)}, bf16[4,80,256]{2,1,0:T(8,128)(2,1)S(1)}, u32[]{:S(2)}, u32[]{:S(2)}) collective-permute-start(bf16[4,80,256]{2,1,0:T(8,128)(2,1)S(1)} %get-tuple-element.41), channel_id=1, source_target_pairs={{0,8},{4,12},{8,0},{12,4},{1,9},{5,13},{9,1},{13,5},{2,10},{6,14},... | collective-permute-start | bytes 491528 | tf_op jit(solution)/shard_map/ppermute | solution.py:26
  84.7 7.8 %collective-permute-start.21 = (bf16[4,80,256]{2,1,0:T(8,128)(2,1)S(1)}, bf16[4,80,256]{2,1,0:T(8,128)(2,1)S(1)}, u32[]{:S(2)}, u32[]{:S(2)}) collective-permute-start(bf16[4,80,256]{2,1,0:T(8,128)(2,1)S(1)} %get-tuple-element.42), channel_id=1, source_target_pairs={{0,12},{4,0},{8,4},{12,8},{1,13},{5,1},{9,5},{13,9},{2,14},{6,2},{... | collective-permute-start | bytes 491528 | tf_op jit(solution)/shard_map/ppermute | solution.py:26
  93.3 16.3 %all-to-all-start = ((bf16[8,40,512]{2,1,0:T(8,128)(2,1)}), bf16[8,40,512]{2,1,0:T(8,128)(2,1)S(1)}, u32[]{:S(2)}, u32[]{:S(2)}) async-start(bf16[8,40,512]{2,1,0:T(8,128)(2,1)} %bitcast.21), calls=%async_computation | async-start | bytes 655360 | tf_op jit(solution)/shard_map/all_to_all | solution.py:237
  99.1 6.4 %collective-permute-start.8 = (bf16[128,512]{1,0:T(8,128)(2,1)S(1)}, bf16[128,512]{1,0:T(8,128)(2,1)S(1)}, u32[]{:S(2)}, u32[]{:S(2)}) collective-permute-start(bf16[128,512]{1,0:T(8,128)(2,1)S(1)} %pad_maximum_fusion.3), channel_id=1, source_target_pairs={{0,1},{1,0},{2,3},{3,2},{4,5},{5,4},{6,7},{7,6},{8,9},{9,8},{10,11... | collective-permute-start | bytes 393224 | tf_op jit(solution)/shard_map/ppermute | solution.py:26
  109.8 8.7 %collective-permute-start.22 = (f32[20,512]{1,0:T(8,128)S(1)}, f32[20,512]{1,0:T(8,128)S(1)}, u32[]{:S(2)}, u32[]{:S(2)}) collective-permute-start(f32[20,512]{1,0:T(8,128)S(1)} %dynamic-slice_bitcast_fusion.4), channel_id=1, source_target_pairs={{0,1},{1,0},{2,3},{3,2},{4,5},{5,4},{6,7},{7,6},{8,9},{9,8},{10,11... | collective-permute-start | bytes 122888 | tf_op jit(solution)/shard_map/ppermute | solution.py:26

commit v4 on v3

--- a/solution.py
+++ b/solution.py
@@ -49,9 +49,12 @@
     return p, ds
 
 
-def attention_kernel(core_ref, bias_ref, q_ref, do_ref, k0_ref, k1_ref, k2_ref, v0_ref, v1_ref, v2_ref, dq_ref, theirs_ref, mine_ref):
-    keys = jnp.concatenate([k0_ref[...], k1_ref[...], k2_ref[...]], axis=0)
-    values = jnp.concatenate([v0_ref[...], v1_ref[...], v2_ref[...]], axis=0)
+def attention_kernel(core_ref, bias_ref, q_ref, do_ref, kv0_ref, kv1_ref, kv2_ref, dq_ref, theirs_ref, mine_ref):
+    head = (2 - 2 * core_ref[0] + pl.program_id(0)) % KV_HEADS
+    key_cols = pl.ds(pl.multiple_of(head * HEAD_DIM, HEAD_DIM), HEAD_DIM)
+    value_cols = pl.ds(pl.multiple_of((KV_HEADS + head) * HEAD_DIM, HEAD_DIM), HEAD_DIM)
+    keys = jnp.concatenate([ref[:, key_cols] for ref in (kv0_ref, kv1_ref, kv2_ref)], axis=0)
+    values = jnp.concatenate([ref[:, value_cols] for ref in (kv0_ref, kv1_ref, kv2_ref)], axis=0)
     keys_t = keys.T
     bias = bias_ref[...]
     key_at = lax.broadcasted_iota(jnp.int32, (TOK, TOK), 0)
@@ -112,8 +115,7 @@
         return (2 - 2 * core_ref[0] + i) % KV_HEADS
 
     rows = pl.BlockSpec((LAYERS, TOK, wide), lambda i, c: (0, 0, head(i, c)))
-    key_cols = pl.BlockSpec((TOK, HEAD_DIM), lambda i, c: (0, head(i, c)))
-    value_cols = pl.BlockSpec((TOK, HEAD_DIM), lambda i, c: (0, KV_HEADS + head(i, c)))
+    held = pl.BlockSpec(memory_space=pltpu.VMEM)
     theirs = pl.BlockSpec((3 * TOK, PAIR), lambda i, c: (0, jnp.minimum(i, 1)))
     mine = pl.BlockSpec((3 * TOK, PAIR), lambda i, c: (0, jnp.maximum(i - 2, 0)))
     return pl.pallas_call(
@@ -121,7 +123,7 @@
         grid_spec=pltpu.PrefetchScalarGridSpec(
             num_scalar_prefetch=1,
             grid=(KV_HEADS,),
-            in_specs=[pl.BlockSpec((2 * TOK, TOK), lambda i, c: (0, 0)), rows, rows] + [key_cols] * 3 + [value_cols] * 3,
+            in_specs=[held, rows, rows, held, held, held],
             out_specs=[rows, theirs, mine],
         ),
         out_shape=[
@@ -132,7 +134,7 @@
         compiler_params=pltpu.CompilerParams(vmem_limit_bytes=VMEM),
         cost_estimate=pl.CostEstimate(flops=6_000_000_000, bytes_accessed=9_000_000, transcendentals=1_400_000),
         name="attention",
-    )(core[None], bias, queries, grad_out, kv0, kv1, kv2, kv0, kv1, kv2)
+    )(core[None], bias, queries, grad_out, kv0, kv1, kv2)
 
 
 def product_kernel(at_ref, own_ref, other_ref, *refs):
@@ -209,17 +211,26 @@
     dq, theirs, mine = attention(core, bias, queries[:, 0], grad_out[:, 0], kv, kv1, kv2)
     states, theirs = lax.optimization_barrier((states, theirs))
     theirs = shift(theirs, "core", 1)
+    def terms(cols):
+        mine_terms = mine[:, cols].reshape(3, TOK, PAIR)
+        got_terms = theirs[:, cols].reshape(3, TOK, PAIR).astype(jnp.float32)
+        return mine_terms, got_terms
+
+    cameback = []
+    parts = [slice(0, PAIR), slice(PAIR, 2 * PAIR)]
+    for cols in parts:
+        (_, m_one, m_two), (_, g_one, g_two) = terms(cols)
+        back = jnp.concatenate([m_two + jnp.where(first, 0.0, g_one), g_two + jnp.where(first, m_one, 0.0)], axis=0)
+        back = back.astype(jnp.bfloat16)
+        cameback.append(ctx_shift(back, -2))
+
+    mine, theirs, _ = lax.optimization_barrier((mine, theirs, back))
     halves = []
-    for part in range(2):
-        cols = slice(part * PAIR, (part + 1) * PAIR)
-        (m_own, m_one, m_two), (g_own, g_one, g_two) = mine[:, cols].reshape(3, TOK, PAIR), theirs[:, cols].reshape(3, TOK, PAIR)
-        g_own, g_one, g_two = (term.astype(jnp.float32) for term in (g_own, g_one, g_two))
-        back = jnp.concatenate([m_two + jnp.where(first, 0.0, g_one), g_two + jnp.where(first, m_one, 0.0)], axis=0)
+    for cols, came in zip(parts, cameback):
+        (m_own, m_one, _), (g_own, g_one, _) = terms(cols)
         here = jnp.concatenate([m_own + jnp.where(first, g_one, 0.0), g_own + jnp.where(first, 0.0, m_one)], axis=0)
-        back = back.astype(jnp.bfloat16)
-        halves.append((here, ctx_shift(back, -2)))
-
-    states, _ = lax.optimization_barrier((states, back))
+        halves.append((here, came))
+    states, _ = lax.optimization_barrier((states, here))
     states = jnp.stack(states)
     other_states = shift(states, "core", 1)
 
@@ -232,19 +243,22 @@
         got = [pieces[0]] + [shift(pieces[by], "x", by) for by in (1, 2, 3)]
         reduced.append(total(got).astype(jnp.bfloat16))
     block = jnp.concatenate(blocks, axis=1)
-    partial = jnp.concatenate(reduced, axis=2)
-
-    got = lax.all_to_all(partial.reshape(8, 40, 2 * PAIR), ("y", "zh"), 0, 0)
-    rows = jnp.sum(got.astype(jnp.float32), axis=0).reshape(2, 20, 2 * PAIR)
+    partial = []
+    for part in reduced:
+        got = [pick(part, y, 0)] + [shift(pick(part, (y + by) % 4, 0), "y", by) for by in (1, 2, 3)]
+        partial.append(total(got).astype(jnp.bfloat16))
+    partial = jnp.concatenate(partial, axis=1).reshape(2, 40, 2 * PAIR)
+    rows = total([pick(partial, zh, 0), shift(pick(partial, 1 - zh, 0), "zh", 1)]).reshape(2, 20, 2 * PAIR)
     ours = pick(rows, core, 0)
     others = shift(pick(rows, 1 - core, 0), "core", 1)
-
     def assemble(own, other):
         count = own.shape[0]
         cols = jnp.concatenate([jnp.where(first, own, other), jnp.where(first, other, own)], axis=1)
         return cols.reshape(count, KV_HEADS, 2, HEAD_DIM).transpose(0, 2, 1, 3).reshape(count, KV_HEADS * PAIR)
 
-    weight = assemble(ours, others)
+    low, high = jnp.where(first, ours, others), jnp.where(first, others, ours)
+    heads = [part[:, i * HEAD_DIM : (i + 1) * HEAD_DIM] for part in (low, high) for i in range(4)]
+    weight = jnp.concatenate(heads[0::2] + heads[1::2], axis=1)
     kv_out = assemble(block[:TOK], shift(block[TOK:], "core", 1))
     return dq[:, None], kv_out[None], weight
 

time: 121 us -> 119 us (0.983)
  other arithmetic: 4.78 us -> 2.04 us
  starting transfers between devices: 72.2 us -> 73.7 us
    ppermute x20 -> x27, starting transfers between devices: 44.6 us -> 52.2 us  [shift(): lax.ppermute(value, axis, [(i, (i + by) % size) for i in range(size)])]
    all_to_all x1 -> x0, starting transfers between devices: 5.79 us -> none  [on_device(): got = lax.all_to_all(partial.reshape(8, 40, 2 * PAIR), ('y', 'zh'), 0, 0)]
    ppermute x20 -> x27, waiting for transfers between devices: 13.7 us -> 18.9 us  [shift(): lax.ppermute(value, axis, [(i, (i + by) % size) for i in range(size)])]
    all_to_all x1 -> x0, waiting for transfers between devices: 4.14 us -> none  [on_device(): got = lax.all_to_all(partial.reshape(8, 40, 2 * PAIR), ('y', 'zh'), 0, 0)]
    another operation x3, other arithmetic: 1.46 us -> 0.23 us
  transfers between devices with their start and end apart: 24 -> 30, of which waited for: 11 -> 11; matrix products, arithmetic and copies ran while one was open for 3% -> 4% of each run, Pallas kernels for 11% -> 11%
where the time goes in v4:
time: 119 us
  starting transfers between devices  73.7 us (62%)
  waiting for transfers between devices  24.3 us (20%)
  Pallas kernels  13.2 us (11%)
  local copies, waits for them, and re-layouts  4.1 us (3%)
  other arithmetic  2.04 us (2%)
    ppermute x27, starting transfers between devices, shift(): lax.ppermute(value, axis, [(i, (i + by) % size) for i in range(size)])  52.2 us
    ppermute x3, starting transfers between devices, ctx_shift(): return lax.ppermute(value, ('x', 'zh', 'core'), pairs)  21.6 us
    ppermute x27, waiting for transfers between devices, shift(): lax.ppermute(value, axis, [(i, (i + by) % size) for i in range(size)])  18.9 us
    pallas_call x1, Pallas kernels, attention(): pl.pallas_call(attention_kernel, grid_spec=pltpu.PrefetchScalarGridSpec(n...  9.15 us
    ppermute x3, waiting for transfers between devices, ctx_shift(): return lax.ppermute(value, ('x', 'zh', 'core'), pairs)  5.47 us
    pallas_call x2, Pallas kernels, products(): pl.pallas_call(product_kernel, grid_spec=pltpu.PrefetchScalarGridSpec(num...  4.03 us
  transfers between devices with their start and end apart: 30, of which 11 were waited for; matrix products, arithmetic and copies ran while one was open for 4% of the time, Pallas kernels for 11%

profile of v4, /device:TPU:3, one launch (start us, length us, event | category | flops | bytes accessed | tf_op | source)
XLA Modules:
  0.0 118.5 jit_solution(9646519881281002839)
XLA Ops:
  0.6 8.8 %collective-permute-start = (bf16[128,1024]{1,0:T(8,128)(2,1)}, bf16[128,1024]{1,0:T(8,128)(2,1)S(1)}, u32[]{:S(2)}, u32[]{:S(2)}) collective-permute-start(bf16[128,1024]{1,0:T(8,128)(2,1)} %bitcast.73), channel_id=1, source_target_pairs={{0,2},{1,3},{2,4},{3,5},{4,6},{5,7},{6,8},{7,9},{8,10},{9,11},{10,... | collective-permute-start | bytes 786440 | tf_op jit(solution)/shard_map/ppermute | solution.py:31
  9.5 1.4 %dynamic-slice_bitcast_fusion = (bf16[4,320,128]{2,1,0:T(8,128)(2,1)S(1)}, bf16[4,320,128]{2,1,0:T(8,128)(2,1)S(1)}, bf16[4,320,128]{2,1,0:T(8,128)(2,1)S(1)}, bf16[4,320,128]{2,1,0:T(8,128)(2,1)S(1)}) fusion(bf16[4,4,320,128]{3,2,1,0:T(8,128)(2,1)} %bitcast.66, s32[]{:T(128)S(6)} %select_n.160, s32[]{:T(128)S(6)} %select_n.158, s32[]{:T(128)S(6)} %select_n.156, ...), kind=kLoop, calls=%fused_computation.3 | loop fusion | bytes 2621456 | tf_op jit(solution)/shard_map/jit(dynamic_index_in_dim)/squeeze | solution.py:188
  10.9 1.4 %collective-permute-start.2 = (bf16[4,320,128]{2,1,0:T(8,128)(2,1)S(1)}, bf16[4,320,128]{2,1,0:T(8,128)(2,1)S(1)}, u32[]{:S(2)}, u32[]{:S(2)}) collective-permute-start(bf16[4,320,128]{2,1,0:T(8,128)(2,1)S(1)} %get-tuple-element.61), channel_id=1, source_target_pairs={{0,16},{16,32},{32,48},{48,0},{1,17},{17,33},{33,49},{49,1},{2,18}... | collective-permute-start | bytes 983048 | tf_op jit(solution)/shard_map/ppermute | solution.py:26
  12.3 2.6 %collective-permute-start.3 = (bf16[4,320,128]{2,1,0:T(8,128)(2,1)S(1)}, bf16[4,320,128]{2,1,0:T(8,128)(2,1)S(1)}, u32[]{:S(2)}, u32[]{:S(2)}) collective-permute-start(bf16[4,320,128]{2,1,0:T(8,128)(2,1)S(1)} %get-tuple-element.60), channel_id=1, source_target_pairs={{0,32},{16,48},{32,0},{48,16},{1,33},{17,49},{33,1},{49,17},{2,34}... | collective-permute-start | bytes 983048 | tf_op jit(solution)/shard_map/ppermute | solution.py:26
  14.9 1.1 collective-permute-start.4
  16.2 0.1 reduce
  16.4 0.3 collective-permute-done.kv2_ref
  16.7 1.6 %collective-permute-start.1 = (bf16[128,1024]{1,0:T(8,128)(2,1)S(1)}, bf16[128,1024]{1,0:T(8,128)(2,1)S(1)}, u32[]{:S(2)}, u32[]{:S(2)}) collective-permute-start(bf16[128,1024]{1,0:T(8,128)(2,1)S(1)} %broadcast_select_fusion), channel_id=1, source_target_pairs={{0,1},{1,0},{2,3},{3,2},{4,5},{5,4},{6,7},{7,6},{8,9},{9,8},{10,11... | collective-permute-start | bytes 786440 | tf_op jit(solution)/shard_map/ppermute | solution.py:26
  18.3 0.2 fusion.16
  18.5 0.7 add_select_fusion.bias_ref
  19.2 0.3 collective-permute-done.1.kv1_ref
  19.5 0.7 copy-done.5
  20.2 9.2 %attention.1 = (bf16[2,128,2560]{2,1,0:T(8,128)(2,1)}, bf16[384,512]{1,0:T(8,128)(2,1)}, f32[384,512]{1,0:T(8,128)}) custom-call(s32[1]{0:T(128)} %bitcast.core_ref, f32[256,128]{1,0:T(8,128)} %add_select_fusion.bias_ref, bf16[2,128,2560]{2,1,0:T(8,128)(2,1)} %bitcast.76, bf16[2,128,2560]{2,1,0:T(8,128)(2,1)} %bitcast.77, bf16[128,1024]{1,0:T(8,128)(2,1)} %bitcast.74, ...), custom_call_target="tpu_custom_call" | custom-call | flops 6000000000 | bytes 9000000 | tf_op jit(solution)/shard_map/attention/pallas_call | solution.py:121
  29.4 1.3 %collective-permute-start.5 = (bf16[384,512]{1,0:T(8,128)(2,1)}, bf16[384,512]{1,0:T(8,128)(2,1)S(1)}, u32[]{:S(2)}, u32[]{:S(2)}) collective-permute-start(bf16[384,512]{1,0:T(8,128)(2,1)} %get-tuple-element.28), channel_id=1, source_target_pairs={{0,1},{1,0},{2,3},{3,2},{4,5},{5,4},{6,7},{7,6},{8,9},{9,8},{10,11... | collective-permute-start | bytes 1179656 | tf_op jit(solution)/shard_map/ppermute | solution.py:26
  30.7 0.2 pad_maximum_fusion.own_ref
  30.9 0.1 collective-permute-start.9
  31.0 1.2 %collective-permute-done.5 = bf16[384,512]{1,0:T(8,128)(2,1)S(1)} collective-permute-done((bf16[384,512]{1,0:T(8,128)(2,1)}, bf16[384,512]{1,0:T(8,128)(2,1)S(1)}, u32[]{:S(2)}, u32[]{:S(2)}) %collective-permute-start.5) | collective-permute-done | bytes 393248 | tf_op jit(solution)/shard_map/ppermute | solution.py:26
  32.4 10.8 %collective-permute-start.7 = (bf16[256,256]{1,0:T(8,128)(2,1)S(1)}, bf16[256,256]{1,0:T(8,128)(2,1)S(1)}, u32[]{:S(2)}, u32[]{:S(2)}) collective-permute-start(bf16[256,256]{1,0:T(8,128)(2,1)S(1)} %pad_maximum_fusion.4), channel_id=1, source_target_pairs={{2,0},{3,1},{4,2},{5,3},{6,4},{7,5},{8,6},{9,7},{10,8},{11,9},{12,... | collective-permute-start | bytes 393224 | tf_op jit(solution)/shard_map/ppermute | solution.py:31
  43.2 1.9 %collective-permute-start.6 = (bf16[256,256]{1,0:T(8,128)(2,1)S(1)}, bf16[256,256]{1,0:T(8,128)(2,1)S(1)}, u32[]{:S(2)}, u32[]{:S(2)}) collective-permute-start(bf16[256,256]{1,0:T(8,128)(2,1)S(1)} %pad_maximum_fusion.5), channel_id=1, source_target_pairs={{2,0},{3,1},{4,2},{5,3},{6,4},{7,5},{8,6},{9,7},{10,8},{11,9},{12,... | collective-permute-start | bytes 393224 | tf_op jit(solution)/shard_map/ppermute | solution.py:31
  45.3 1.5 %collective-permute-done.7 = bf16[256,256]{1,0:T(8,128)(2,1)S(1)} collective-permute-done((bf16[256,256]{1,0:T(8,128)(2,1)S(1)}, bf16[256,256]{1,0:T(8,128)(2,1)S(1)}, u32[]{:S(2)}, u32[]{:S(2)}) %collective-permute-start.7) | collective-permute-done | bytes 131104 | tf_op jit(solution)/shard_map/ppermute | solution.py:31
  46.9 6.6 %collective-permute-start.20 = (bf16[256,256]{1,0:T(8,128)(2,1)S(1)}, bf16[256,256]{1,0:T(8,128)(2,1)S(1)}, u32[]{:S(2)}, u32[]{:S(2)}) collective-permute-start(bf16[256,256]{1,0:T(8,128)(2,1)S(1)} %add_convert_fusion.2.refs_0_), channel_id=1, source_target_pairs={{0,128},{64,192},{128,0},{192,64},{1,129},{65,193},{129,1},{193,65... | collective-permute-start | bytes 393224 | tf_op jit(solution)/shard_map/ppermute | solution.py:26
  53.5 1.1 collective-permute-start.21
  54.5 3.7 %collective-permute-done.6 = bf16[256,256]{1,0:T(8,128)(2,1)S(1)} collective-permute-done((bf16[256,256]{1,0:T(8,128)(2,1)S(1)}, bf16[256,256]{1,0:T(8,128)(2,1)S(1)}, u32[]{:S(2)}, u32[]{:S(2)}) %collective-permute-start.6) | collective-permute-done | bytes 131104 | tf_op jit(solution)/shard_map/ppermute | solution.py:31
  58.4 2.9 %collective-permute-start.11 = (bf16[256,256]{1,0:T(8,128)(2,1)S(1)}, bf16[256,256]{1,0:T(8,128)(2,1)S(1)}, u32[]{:S(2)}, u32[]{:S(2)}) collective-permute-start(bf16[256,256]{1,0:T(8,128)(2,1)S(1)} %fusion.refs_0_), channel_id=1, source_target_pairs={{0,128},{64,192},{128,0},{192,64},{1,129},{65,193},{129,1},{193,65... | collective-permute-start | bytes 393224 | tf_op jit(solution)/shard_map/ppermute | solution.py:26
  61.3 2.7 %collective-permute-done.20.refs_2_ = bf16[256,256]{1,0:T(8,128)(2,1)S(1)} collective-permute-done((bf16[256,256]{1,0:T(8,128)(2,1)S(1)}, bf16[256,256]{1,0:T(8,128)(2,1)S(1)}, u32[]{:S(2)}, u32[]{:S(2)}) %collective-permute-start.20) | collective-permute-done | bytes 131104 | tf_op jit(solution)/shard_map/ppermute | solution.py:26
  64.0 6.6 %collective-permute-start.12 = (bf16[256,256]{1,0:T(8,128)(2,1)S(1)}, bf16[256,256]{1,0:T(8,128)(2,1)S(1)}, u32[]{:S(2)}, u32[]{:S(2)}) collective-permute-start(bf16[256,256]{1,0:T(8,128)(2,1)S(1)} %fusion.refs_0_), channel_id=1, source_target_pairs={{0,192},{64,0},{128,64},{192,128},{1,193},{65,1},{129,65},{193,129... | collective-permute-start | bytes 393224 | tf_op jit(solution)/shard_map/ppermute | solution.py:26
  70.6 2.0 %products.3 = (bf16[4,80,256]{2,1,0:T(8,128)(2,1)S(1)}, bf16[4,80,256]{2,1,0:T(8,128)(2,1)S(1)}, bf16[4,80,256]{2,1,0:T(8,128)(2,1)S(1)}, bf16[4,80,256]{2,1,0:T(8,128)(2,1)S(1)}) custom-call(s32[3]{0:T(128)S(1)} %pad_add_fusion.at_ref, bf16[4,4,320,128]{3,2,1,0:T(8,128)(2,1)S(1)} %pad_maximum_fusion.own_ref, ...), custom_call_target="tpu_custom_call" | custom-call | flops 1400000000 | bytes 5000000 | tf_op jit(solution)/shard_map/products/pallas_call | solution.py:157
  72.7 2.5 %collective-permute-start.23 = (bf16[4,80,256]{2,1,0:T(8,128)(2,1)S(1)}, bf16[4,80,256]{2,1,0:T(8,128)(2,1)S(1)}, u32[]{:S(2)}, u32[]{:S(2)}) collective-permute-start(bf16[4,80,256]{2,1,0:T(8,128)(2,1)S(1)} %get-tuple-element.45), channel_id=1, source_target_pairs={{0,8},{4,12},{8,0},{12,4},{1,9},{5,13},{9,1},{13,5},{2,10},{6,14},... | collective-permute-start | bytes 491528 | tf_op jit(solution)/shard_map/ppermute | solution.py:26
  75.2 8.6 %collective-permute-start.8 = (bf16[128,512]{1,0:T(8,128)(2,1)S(1)}, bf16[128,512]{1,0:T(8,128)(2,1)S(1)}, u32[]{:S(2)}, u32[]{:S(2)}) collective-permute-start(bf16[128,512]{1,0:T(8,128)(2,1)S(1)} %pad_maximum_fusion.3), channel_id=1, source_target_pairs={{0,1},{1,0},{2,3},{3,2},{4,5},{5,4},{6,7},{7,6},{8,9},{9,8},{10,11... | collective-permute-start | bytes 393224 | tf_op jit(solution)/shard_map/ppermute | solution.py:26
  83.8 2.0 %products.2 = (bf16[4,80,256]{2,1,0:T(8,128)(2,1)S(1)}, bf16[4,80,256]{2,1,0:T(8,128)(2,1)S(1)}, bf16[4,80,256]{2,1,0:T(8,128)(2,1)S(1)}, bf16[4,80,256]{2,1,0:T(8,128)(2,1)S(1)}) custom-call(s32[3]{0:T(128)S(1)} %pad_add_fusion.at_ref, bf16[4,4,320,128]{3,2,1,0:T(8,128)(2,1)S(1)} %pad_maximum_fusion.own_ref, ...), custom_call_target="tpu_custom_call" | custom-call | flops 1400000000 | bytes 5000000 | tf_op jit(solution)/shard_map/products/pallas_call | solution.py:157
  85.9 0.9 collective-permute-start.14
  86.8 1.5 %collective-permute-start.13 = (bf16[4,80,256]{2,1,0:T(8,128)(2,1)S(1)}, bf16[4,80,256]{2,1,0:T(8,128)(2,1)S(1)}, u32[]{:S(2)}, u32[]{:S(2)}) collective-permute-start(bf16[4,80,256]{2,1,0:T(8,128)(2,1)S(1)} %get-tuple-element.40), channel_id=1, source_target_pairs={{0,4},{4,8},{8,12},{12,0},{1,5},{5,9},{9,13},{13,1},{2,6},{6,10},{... | collective-permute-start | bytes 491528 | tf_op jit(solution)/shard_map/ppermute | solution.py:26
  88.3 0.1 add_convert_fusion
  88.4 2.8 %collective-permute-start.27 = (bf16[80,256]{1,0:T(8,128)(2,1)S(1)}, bf16[80,256]{1,0:T(8,128)(2,1)S(1)}, u32[]{:S(2)}, u32[]{:S(2)}) collective-permute-start(bf16[80,256]{1,0:T(8,128)(2,1)S(1)} %get-tuple-element.85), channel_id=1, source_target_pairs={{0,48},{16,0},{32,16},{48,32},{1,49},{17,1},{33,17},{49,33},{2,50}... | collective-permute-start | bytes 122888 | tf_op jit(solution)/shard_map/ppermute | solution.py:26
  91.2 4.0 %collective-permute-done.15 = bf16[4,80,256]{2,1,0:T(8,128)(2,1)S(1)} collective-permute-done((bf16[4,80,256]{2,1,0:T(8,128)(2,1)S(1)}, bf16[4,80,256]{2,1,0:T(8,128)(2,1)S(1)}, u32[]{:S(2)}, u32[]{:S(2)}) %collective-permute-start.15) | collective-permute-done | bytes 163872 | tf_op jit(solution)/shard_map/ppermute | solution.py:26
  95.2 2.9 %collective-permute-start.26 = (bf16[80,256]{1,0:T(8,128)(2,1)S(1)}, bf16[80,256]{1,0:T(8,128)(2,1)S(1)}, u32[]{:S(2)}, u32[]{:S(2)}) collective-permute-start(bf16[80,256]{1,0:T(8,128)(2,1)S(1)} %get-tuple-element.86), channel_id=1, source_target_pairs={{0,32},{16,48},{32,0},{48,16},{1,33},{17,49},{33,1},{49,17},{2,34}... | collective-permute-start | bytes 122888 | tf_op jit(solution)/shard_map/ppermute | solution.py:26
  98.1 0.4 collective-permute-start.25
  98.6 2.4 %collective-permute-start.18 = (bf16[80,256]{1,0:T(8,128)(2,1)S(1)}, bf16[80,256]{1,0:T(8,128)(2,1)S(1)}, u32[]{:S(2)}, u32[]{:S(2)}) collective-permute-start(bf16[80,256]{1,0:T(8,128)(2,1)S(1)} %get-tuple-element.82), channel_id=1, source_target_pairs={{0,48},{16,0},{32,16},{48,32},{1,49},{17,1},{33,17},{49,33},{2,50}... | collective-permute-start | bytes 122888 | tf_op jit(solution)/shard_map/ppermute | solution.py:26
  101.0 0.7 collective-permute-start.16
  101.7 0.5 collective-permute-done.25
  102.2 3.2 %collective-permute-done.17 = bf16[80,256]{1,0:T(8,128)(2,1)S(1)} collective-permute-done((bf16[80,256]{1,0:T(8,128)(2,1)S(1)}, bf16[80,256]{1,0:T(8,128)(2,1)S(1)}, u32[]{:S(2)}, u32[]{:S(2)}) %collective-permute-start.17) | collective-permute-done | bytes 40992 | tf_op jit(solution)/shard_map/ppermute | solution.py:26
  105.5 0.1 collective-permute-done.16
  105.6 0.1 collective-permute-start.28
  105.8 6.7 %collective-permute-done.28 = bf16[40,512]{1,0:T(8,128)(2,1)S(1)} collective-permute-done((bf16[40,512]{1,0:T(8,128)(2,1)S(1)}, bf16[40,512]{1,0:T(8,128)(2,1)S(1)}, u32[]{:S(2)}, u32[]{:S(2)}) %collective-permute-start.28) | collective-permute-done | bytes 40992 | tf_op jit(solution)/shard_map/ppermute | solution.py:26
  112.5 4.0 %collective-permute-start.29 = (f32[20,512]{1,0:T(8,128)S(1)}, f32[20,512]{1,0:T(8,128)S(1)}, u32[]{:S(2)}, u32[]{:S(2)}) collective-permute-start(f32[20,512]{1,0:T(8,128)S(1)} %dynamic-slice_bitcast_fusion.4), channel_id=1, source_target_pairs={{0,1},{1,0},{2,3},{3,2},{4,5},{5,4},{6,7},{7,6},{8,9},{9,8},{10,11... | collective-permute-start | bytes 122888 | tf_op jit(solution)/shard_map/ppermute | solution.py:26
  116.6 0.2 reshape.144
  116.9 0.9 broadcast_in_dim_reshape.3
  117.9 0.6 copy-done.3
  (75 shorter events, 1.6 us)
Async XLA Ops:
  0.6 16.0 %collective-permute-start = (bf16[128,1024]{1,0:T(8,128)(2,1)}, bf16[128,1024]{1,0:T(8,128)(2,1)S(1)}, u32[]{:S(2)}, u32[]{:S(2)}) collective-permute-start(bf16[128,1024]{1,0:T(8,128)(2,1)} %bitcast.73), channel_id=1, source_target_pairs={{0,2},{1,3},{2,4},{3,5},{4,6},{5,7},{6,8},{7,9},{8,10},{9,11},{10,... | collective-permute-start | bytes 786440 | tf_op jit(solution)/shard_map/ppermute | solution.py:31
  9.5 6.5 %copy-start.4 = (s32[1,16]{1,0:T(1,128)S(1)}, s32[1,16]{1,0:T(1,128)}, u32[]{:S(2)}) copy-start(s32[1,16]{1,0:T(1,128)} %param.9) | copy-start | bytes 196
  9.5 7.1 %copy-start.1 = (bf16[1,128,1024]{2,1,0:T(8,128)(2,1)S(1)}, bf16[1,128,1024]{2,1,0:T(8,128)(2,1)}, u32[]{:S(2)}) copy-start(bf16[1,128,1024]{2,1,0:T(8,128)(2,1)} %param.6) | copy-start | bytes 786436
  10.9 18.4 %collective-permute-start.2 = (bf16[4,320,128]{2,1,0:T(8,128)(2,1)S(1)}, bf16[4,320,128]{2,1,0:T(8,128)(2,1)S(1)}, u32[]{:S(2)}, u32[]{:S(2)}) collective-permute-start(bf16[4,320,128]{2,1,0:T(8,128)(2,1)S(1)} %get-tuple-element.61), channel_id=1, source_target_pairs={{0,16},{16,32},{32,48},{48,0},{1,17},{17,33},{33,49},{49,1},{2,18}... | collective-permute-start | bytes 983048 | tf_op jit(solution)/shard_map/ppermute | solution.py:26
  12.3 17.0 %collective-permute-start.3 = (bf16[4,320,128]{2,1,0:T(8,128)(2,1)S(1)}, bf16[4,320,128]{2,1,0:T(8,128)(2,1)S(1)}, u32[]{:S(2)}, u32[]{:S(2)}) collective-permute-start(bf16[4,320,128]{2,1,0:T(8,128)(2,1)S(1)} %get-tuple-element.60), channel_id=1, source_target_pairs={{0,32},{16,48},{32,0},{48,16},{1,33},{17,49},{33,1},{49,17},{2,34}... | collective-permute-start | bytes 983048 | tf_op jit(solution)/shard_map/ppermute | solution.py:26
  14.9 14.4 %collective-permute-start.4 = (bf16[4,320,128]{2,1,0:T(8,128)(2,1)S(1)}, bf16[4,320,128]{2,1,0:T(8,128)(2,1)S(1)}, u32[]{:S(2)}, u32[]{:S(2)}) collective-permute-start(bf16[4,320,128]{2,1,0:T(8,128)(2,1)S(1)} %get-tuple-element.59), channel_id=1, source_target_pairs={{0,48},{16,0},{32,16},{48,32},{1,49},{17,1},{33,17},{49,33},{2,50}... | collective-permute-start | bytes 983048 | tf_op jit(solution)/shard_map/ppermute | solution.py:26
  16.6 2.8 %copy-start.2 = (bf16[128,1024]{1,0:T(8,128)(2,1)}, bf16[128,1024]{1,0:T(8,128)(2,1)S(1)}, u32[]{:S(2)}) copy-start(bf16[128,1024]{1,0:T(8,128)(2,1)S(1)} %collective-permute-done.kv2_ref) | copy-start | bytes 786436
  16.7 2.8 %collective-permute-start.1 = (bf16[128,1024]{1,0:T(8,128)(2,1)S(1)}, bf16[128,1024]{1,0:T(8,128)(2,1)S(1)}, u32[]{:S(2)}, u32[]{:S(2)}) collective-permute-start(bf16[128,1024]{1,0:T(8,128)(2,1)S(1)} %broadcast_select_fusion), channel_id=1, source_target_pairs={{0,1},{1,0},{2,3},{3,2},{4,5},{5,4},{6,7},{7,6},{8,9},{9,8},{10,11... | collective-permute-start | bytes 786440 | tf_op jit(solution)/shard_map/ppermute | solution.py:26
  19.5 0.7 copy-start.5
  29.4 2.8 %collective-permute-start.5 = (bf16[384,512]{1,0:T(8,128)(2,1)}, bf16[384,512]{1,0:T(8,128)(2,1)S(1)}, u32[]{:S(2)}, u32[]{:S(2)}) collective-permute-start(bf16[384,512]{1,0:T(8,128)(2,1)} %get-tuple-element.28), channel_id=1, source_target_pairs={{0,1},{1,0},{2,3},{3,2},{4,5},{5,4},{6,7},{7,6},{8,9},{9,8},{10,11... | collective-permute-start | bytes 1179656 | tf_op jit(solution)/shard_map/ppermute | solution.py:26
  30.7 1.5 %copy-start = (f32[384,512]{1,0:T(8,128)S(1)}, f32[384,512]{1,0:T(8,128)}, u32[]{:S(2)}) copy-start(f32[384,512]{1,0:T(8,128)} %get-tuple-element.29) | copy-start | bytes 2359300
  30.9 39.7 %collective-permute-start.9 = (bf16[4,4,320,128]{3,2,1,0:T(8,128)(2,1)S(1)}, bf16[4,4,320,128]{3,2,1,0:T(8,128)(2,1)S(1)}, u32[]{:S(2)}, u32[]{:S(2)}) collective-permute-start(bf16[4,4,320,128]{3,2,1,0:T(8,128)(2,1)S(1)} %pad_maximum_fusion.own_ref), channel_id=1, source_target_pairs={{0,1},{1,0},{2,3},{3,2},{4,5},{5,4},{6,7},{7,6},{8,9},{9,8},{10,11... | collective-permute-start | bytes 3932168 | tf_op jit(solution)/shard_map/ppermute | solution.py:26
  32.4 14.4 %collective-permute-start.7 = (bf16[256,256]{1,0:T(8,128)(2,1)S(1)}, bf16[256,256]{1,0:T(8,128)(2,1)S(1)}, u32[]{:S(2)}, u32[]{:S(2)}) collective-permute-start(bf16[256,256]{1,0:T(8,128)(2,1)S(1)} %pad_maximum_fusion.4), channel_id=1, source_target_pairs={{2,0},{3,1},{4,2},{5,3},{6,4},{7,5},{8,6},{9,7},{10,8},{11,9},{12,... | collective-permute-start | bytes 393224 | tf_op jit(solution)/shard_map/ppermute | solution.py:31
  43.2 15.0 %collective-permute-start.6 = (bf16[256,256]{1,0:T(8,128)(2,1)S(1)}, bf16[256,256]{1,0:T(8,128)(2,1)S(1)}, u32[]{:S(2)}, u32[]{:S(2)}) collective-permute-start(bf16[256,256]{1,0:T(8,128)(2,1)S(1)} %pad_maximum_fusion.5), channel_id=1, source_target_pairs={{2,0},{3,1},{4,2},{5,3},{6,4},{7,5},{8,6},{9,7},{10,8},{11,9},{12,... | collective-permute-start | bytes 393224 | tf_op jit(solution)/shard_map/ppermute | solution.py:31
  46.8 11.6 %collective-permute-start.19 = (bf16[256,256]{1,0:T(8,128)(2,1)S(1)}, bf16[256,256]{1,0:T(8,128)(2,1)S(1)}, u32[]{:S(2)}, u32[]{:S(2)}) collective-permute-start(bf16[256,256]{1,0:T(8,128)(2,1)S(1)} %add_convert_fusion.2.refs_0_), channel_id=1, source_target_pairs={{0,64},{64,128},{128,192},{192,0},{1,65},{65,129},{129,193},{193,1... | collective-permute-start | bytes 393224 | tf_op jit(solution)/shard_map/ppermute | solution.py:26
  46.9 17.1 %collective-permute-start.20 = (bf16[256,256]{1,0:T(8,128)(2,1)S(1)}, bf16[256,256]{1,0:T(8,128)(2,1)S(1)}, u32[]{:S(2)}, u32[]{:S(2)}) collective-permute-start(bf16[256,256]{1,0:T(8,128)(2,1)S(1)} %add_convert_fusion.2.refs_0_), channel_id=1, source_target_pairs={{0,128},{64,192},{128,0},{192,64},{1,129},{65,193},{129,1},{193,65... | collective-permute-start | bytes 393224 | tf_op jit(solution)/shard_map/ppermute | solution.py:26
  53.5 17.1 %collective-permute-start.21 = (bf16[256,256]{1,0:T(8,128)(2,1)S(1)}, bf16[256,256]{1,0:T(8,128)(2,1)S(1)}, u32[]{:S(2)}, u32[]{:S(2)}) collective-permute-start(bf16[256,256]{1,0:T(8,128)(2,1)S(1)} %add_convert_fusion.2.refs_0_), channel_id=1, source_target_pairs={{0,192},{64,0},{128,64},{192,128},{1,193},{65,1},{129,65},{193,129... | collective-permute-start | bytes 393224 | tf_op jit(solution)/shard_map/ppermute | solution.py:26
  58.3 16.9 %collective-permute-start.10 = (bf16[256,256]{1,0:T(8,128)(2,1)S(1)}, bf16[256,256]{1,0:T(8,128)(2,1)S(1)}, u32[]{:S(2)}, u32[]{:S(2)}) collective-permute-start(bf16[256,256]{1,0:T(8,128)(2,1)S(1)} %fusion.refs_0_), channel_id=1, source_target_pairs={{0,64},{64,128},{128,192},{192,0},{1,65},{65,129},{129,193},{193,1... | collective-permute-start | bytes 393224 | tf_op jit(solution)/shard_map/ppermute | solution.py:26
  58.4 16.8 %collective-permute-start.11 = (bf16[256,256]{1,0:T(8,128)(2,1)S(1)}, bf16[256,256]{1,0:T(8,128)(2,1)S(1)}, u32[]{:S(2)}, u32[]{:S(2)}) collective-permute-start(bf16[256,256]{1,0:T(8,128)(2,1)S(1)} %fusion.refs_0_), channel_id=1, source_target_pairs={{0,128},{64,192},{128,0},{192,64},{1,129},{65,193},{129,1},{193,65... | collective-permute-start | bytes 393224 | tf_op jit(solution)/shard_map/ppermute | solution.py:26
  64.0 19.8 %collective-permute-start.12 = (bf16[256,256]{1,0:T(8,128)(2,1)S(1)}, bf16[256,256]{1,0:T(8,128)(2,1)S(1)}, u32[]{:S(2)}, u32[]{:S(2)}) collective-permute-start(bf16[256,256]{1,0:T(8,128)(2,1)S(1)} %fusion.refs_0_), channel_id=1, source_target_pairs={{0,192},{64,0},{128,64},{192,128},{1,193},{65,1},{129,65},{193,129... | collective-permute-start | bytes 393224 | tf_op jit(solution)/shard_map/ppermute | solution.py:26
  72.6 13.3 %collective-permute-start.24 = (bf16[4,80,256]{2,1,0:T(8,128)(2,1)S(1)}, bf16[4,80,256]{2,1,0:T(8,128)(2,1)S(1)}, u32[]{:S(2)}, u32[]{:S(2)}) collective-permute-start(bf16[4,80,256]{2,1,0:T(8,128)(2,1)S(1)} %get-tuple-element.46), channel_id=1, source_target_pairs={{0,12},{4,0},{8,4},{12,8},{1,13},{5,1},{9,5},{13,9},{2,14},{6,2},{... | collective-permute-start | bytes 491528 | tf_op jit(solution)/shard_map/ppermute | solution.py:26
  72.7 14.1 %collective-permute-start.23 = (bf16[4,80,256]{2,1,0:T(8,128)(2,1)S(1)}, bf16[4,80,256]{2,1,0:T(8,128)(2,1)S(1)}, u32[]{:S(2)}, u32[]{:S(2)}) collective-permute-start(bf16[4,80,256]{2,1,0:T(8,128)(2,1)S(1)} %get-tuple-element.45), channel_id=1, source_target_pairs={{0,8},{4,12},{8,0},{12,4},{1,9},{5,13},{9,1},{13,5},{2,10},{6,14},... | collective-permute-start | bytes 491528 | tf_op jit(solution)/shard_map/ppermute | solution.py:26
  75.2 13.1 %collective-permute-start.22 = (bf16[4,80,256]{2,1,0:T(8,128)(2,1)S(1)}, bf16[4,80,256]{2,1,0:T(8,128)(2,1)S(1)}, u32[]{:S(2)}, u32[]{:S(2)}) collective-permute-start(bf16[4,80,256]{2,1,0:T(8,128)(2,1)S(1)} %get-tuple-element.44), channel_id=1, source_target_pairs={{0,4},{4,8},{8,12},{12,0},{1,5},{5,9},{9,13},{13,1},{2,6},{6,10},{... | collective-permute-start | bytes 491528 | tf_op jit(solution)/shard_map/ppermute | solution.py:26
  75.2 30.5 %collective-permute-start.8 = (bf16[128,512]{1,0:T(8,128)(2,1)S(1)}, bf16[128,512]{1,0:T(8,128)(2,1)S(1)}, u32[]{:S(2)}, u32[]{:S(2)}) collective-permute-start(bf16[128,512]{1,0:T(8,128)(2,1)S(1)} %pad_maximum_fusion.3), channel_id=1, source_target_pairs={{0,1},{1,0},{2,3},{3,2},{4,5},{5,4},{6,7},{7,6},{8,9},{9,8},{10,11... | collective-permute-start | bytes 393224 | tf_op jit(solution)/shard_map/ppermute | solution.py:26
  85.8 9.4 %collective-permute-start.15 = (bf16[4,80,256]{2,1,0:T(8,128)(2,1)S(1)}, bf16[4,80,256]{2,1,0:T(8,128)(2,1)S(1)}, u32[]{:S(2)}, u32[]{:S(2)}) collective-permute-start(bf16[4,80,256]{2,1,0:T(8,128)(2,1)S(1)} %get-tuple-element.42), channel_id=1, source_target_pairs={{0,12},{4,0},{8,4},{12,8},{1,13},{5,1},{9,5},{13,9},{2,14},{6,2},{... | collective-permute-start | bytes 491528 | tf_op jit(solution)/shard_map/ppermute | solution.py:26
  85.9 12.2 %collective-permute-start.14 = (bf16[4,80,256]{2,1,0:T(8,128)(2,1)S(1)}, bf16[4,80,256]{2,1,0:T(8,128)(2,1)S(1)}, u32[]{:S(2)}, u32[]{:S(2)}) collective-permute-start(bf16[4,80,256]{2,1,0:T(8,128)(2,1)S(1)} %get-tuple-element.41), channel_id=1, source_target_pairs={{0,8},{4,12},{8,0},{12,4},{1,9},{5,13},{9,1},{13,5},{2,10},{6,14},... | collective-permute-start | bytes 491528 | tf_op jit(solution)/shard_map/ppermute | solution.py:26
  86.8 11.7 %collective-permute-start.13 = (bf16[4,80,256]{2,1,0:T(8,128)(2,1)S(1)}, bf16[4,80,256]{2,1,0:T(8,128)(2,1)S(1)}, u32[]{:S(2)}, u32[]{:S(2)}) collective-permute-start(bf16[4,80,256]{2,1,0:T(8,128)(2,1)S(1)} %get-tuple-element.40), channel_id=1, source_target_pairs={{0,4},{4,8},{8,12},{12,0},{1,5},{5,9},{9,13},{13,1},{2,6},{6,10},{... | collective-permute-start | bytes 491528 | tf_op jit(solution)/shard_map/ppermute | solution.py:26
  88.4 12.6 %collective-permute-start.27 = (bf16[80,256]{1,0:T(8,128)(2,1)S(1)}, bf16[80,256]{1,0:T(8,128)(2,1)S(1)}, u32[]{:S(2)}, u32[]{:S(2)}) collective-permute-start(bf16[80,256]{1,0:T(8,128)(2,1)S(1)} %get-tuple-element.85), channel_id=1, source_target_pairs={{0,48},{16,0},{32,16},{48,32},{1,49},{17,1},{33,17},{49,33},{2,50}... | collective-permute-start | bytes 122888 | tf_op jit(solution)/shard_map/ppermute | solution.py:26
  95.2 5.8 %collective-permute-start.26 = (bf16[80,256]{1,0:T(8,128)(2,1)S(1)}, bf16[80,256]{1,0:T(8,128)(2,1)S(1)}, u32[]{:S(2)}, u32[]{:S(2)}) collective-permute-start(bf16[80,256]{1,0:T(8,128)(2,1)S(1)} %get-tuple-element.86), channel_id=1, source_target_pairs={{0,32},{16,48},{32,0},{48,16},{1,33},{17,49},{33,1},{49,17},{2,34}... | collective-permute-start | bytes 122888 | tf_op jit(solution)/shard_map/ppermute | solution.py:26
  98.1 4.1 %collective-permute-start.25 = (bf16[80,256]{1,0:T(8,128)(2,1)S(1)}, bf16[80,256]{1,0:T(8,128)(2,1)S(1)}, u32[]{:S(2)}, u32[]{:S(2)}) collective-permute-start(bf16[80,256]{1,0:T(8,128)(2,1)S(1)} %get-tuple-element.84), channel_id=1, source_target_pairs={{0,16},{16,32},{32,48},{48,0},{1,17},{17,33},{33,49},{49,1},{2,18}... | collective-permute-start | bytes 122888 | tf_op jit(solution)/shard_map/ppermute | solution.py:26
  98.6 3.6 %collective-permute-start.18 = (bf16[80,256]{1,0:T(8,128)(2,1)S(1)}, bf16[80,256]{1,0:T(8,128)(2,1)S(1)}, u32[]{:S(2)}, u32[]{:S(2)}) collective-permute-start(bf16[80,256]{1,0:T(8,128)(2,1)S(1)} %get-tuple-element.82), channel_id=1, source_target_pairs={{0,48},{16,0},{32,16},{48,32},{1,49},{17,1},{33,17},{49,33},{2,50}... | collective-permute-start | bytes 122888 | tf_op jit(solution)/shard_map/ppermute | solution.py:26
  101.0 4.5 %collective-permute-start.17 = (bf16[80,256]{1,0:T(8,128)(2,1)S(1)}, bf16[80,256]{1,0:T(8,128)(2,1)S(1)}, u32[]{:S(2)}, u32[]{:S(2)}) collective-permute-start(bf16[80,256]{1,0:T(8,128)(2,1)S(1)} %get-tuple-element.83), channel_id=1, source_target_pairs={{0,32},{16,48},{32,0},{48,16},{1,33},{17,49},{33,1},{49,17},{2,34}... | collective-permute-start | bytes 122888 | tf_op jit(solution)/shard_map/ppermute | solution.py:26
  101.0 4.6 %collective-permute-start.16 = (bf16[80,256]{1,0:T(8,128)(2,1)S(1)}, bf16[80,256]{1,0:T(8,128)(2,1)S(1)}, u32[]{:S(2)}, u32[]{:S(2)}) collective-permute-start(bf16[80,256]{1,0:T(8,128)(2,1)S(1)} %get-tuple-element.81), channel_id=1, source_target_pairs={{0,16},{16,32},{32,48},{48,0},{1,17},{17,33},{33,49},{49,1},{2,18}... | collective-permute-start | bytes 122888 | tf_op jit(solution)/shard_map/ppermute | solution.py:26
  105.6 6.8 %collective-permute-start.28 = (bf16[40,512]{1,0:T(8,128)(2,1)S(1)}, bf16[40,512]{1,0:T(8,128)(2,1)S(1)}, u32[]{:S(2)}, u32[]{:S(2)}) collective-permute-start(bf16[40,512]{1,0:T(8,128)(2,1)S(1)} %dynamic-slice_bitcast_fusion.5), channel_id=1, source_target_pairs={{0,2},{2,0},{1,3},{3,1},{4,6},{6,4},{5,7},{7,5},{8,10},{10,8},{9,1... | collective-permute-start | bytes 122888 | tf_op jit(solution)/shard_map/ppermute | solution.py:26
  112.5 5.2 %collective-permute-start.29 = (f32[20,512]{1,0:T(8,128)S(1)}, f32[20,512]{1,0:T(8,128)S(1)}, u32[]{:S(2)}, u32[]{:S(2)}) collective-permute-start(f32[20,512]{1,0:T(8,128)S(1)} %dynamic-slice_bitcast_fusion.4), channel_id=1, source_target_pairs={{0,1},{1,0},{2,3},{3,2},{4,5},{5,4},{6,7},{7,6},{8,9},{9,8},{10,11... | collective-permute-start | bytes 122888 | tf_op jit(solution)/shard_map/ppermute | solution.py:26
  117.9 0.6 copy-start.3

commit v5 on v4

--- a/solution.py
+++ b/solution.py
@@ -139,33 +139,30 @@
 
 def product_kernel(at_ref, own_ref, other_ref, *refs):
     block_refs, out_refs, acc_ref = refs[:4], refs[4:8], refs[8]
-    zl, x = at_ref[0], at_ref[1]
-    left = []
-    for by in range(4):
-        seq = (zl - by + 4) % 4
-        left += [own_ref[0, seq], other_ref[0, seq]]
-    left = jnp.concatenate(left, axis=1)
+    zl, x, y = at_ref[0], at_ref[1], at_ref[2]
     right = jnp.concatenate([ref[...] for ref in block_refs], axis=0)
-    acc_ref[...] = jnp.dot(left, right, preferred_element_type=jnp.float32)
+    for place in range(4):
+        left = []
+        for by in range(4):
+            seq = (zl - by + 4) % 4
+            left += [own_ref[place, seq], other_ref[place, seq]]
+        acc_ref[place] = jnp.dot(jnp.concatenate(left, axis=1), right, preferred_element_type=jnp.float32)
     for by in range(4):
         start = pl.multiple_of((x + by) % 4 * 80, 16)
-        out_refs[by][0] = acc_ref[pl.ds(start, 80)].astype(jnp.bfloat16)
+        for place in range(4):
+            out_refs[by][(y - place + 4) % 4] = acc_ref[place, pl.ds(start, 80)].astype(jnp.bfloat16)
 
 
 def products(at, own, other, blocks):
-    states = pl.BlockSpec((1, 4, WIDE, TOK), lambda i, at: ((at[2] - i + 4) % 4, 0, 0, 0))
+    held = pl.BlockSpec(memory_space=pltpu.VMEM)
     return pl.pallas_call(
         product_kernel,
-        grid_spec=pltpu.PrefetchScalarGridSpec(
-            num_scalar_prefetch=1,
-            grid=(4,),
-            in_specs=[states, states] + [pl.BlockSpec((2 * TOK, PAIR), lambda i, at: (0, 0))] * 4,
-            out_specs=[pl.BlockSpec((1, 80, PAIR), lambda i, at: (i, 0, 0))] * 4,
-            scratch_shapes=[pltpu.VMEM((WIDE, PAIR), jnp.float32)],
-        ),
+        in_specs=[pl.BlockSpec(memory_space=pltpu.SMEM)] + [held] * 6,
+        out_specs=[held] * 4,
         out_shape=[jax.ShapeDtypeStruct((4, 80, PAIR), jnp.bfloat16)] * 4,
+        scratch_shapes=[pltpu.VMEM((4, WIDE, PAIR), jnp.float32)],
         compiler_params=pltpu.CompilerParams(vmem_limit_bytes=16 * 1024 * 1024),
-        cost_estimate=pl.CostEstimate(flops=1_400_000_000, bytes_accessed=5_000_000, transcendentals=0),
+        cost_estimate=pl.CostEstimate(flops=700_000_000, bytes_accessed=4_000_000, transcendentals=0),
         name="products",
     )(at, own, other, *blocks)
 
@@ -249,17 +246,18 @@
         partial.append(total(got).astype(jnp.bfloat16))
     partial = jnp.concatenate(partial, axis=1).reshape(2, 40, 2 * PAIR)
     rows = total([pick(partial, zh, 0), shift(pick(partial, 1 - zh, 0), "zh", 1)]).reshape(2, 20, 2 * PAIR)
-    ours = pick(rows, core, 0)
-    others = shift(pick(rows, 1 - core, 0), "core", 1)
     def assemble(own, other):
         count = own.shape[0]
         cols = jnp.concatenate([jnp.where(first, own, other), jnp.where(first, other, own)], axis=1)
         return cols.reshape(count, KV_HEADS, 2, HEAD_DIM).transpose(0, 2, 1, 3).reshape(count, KV_HEADS * PAIR)
 
+    kv_out = assemble(block[:TOK], shift(block[TOK:], "core", 1))
+    rows, kv_out = lax.optimization_barrier((rows, kv_out))
+    ours = pick(rows, core, 0)
+    others = shift(pick(rows, 1 - core, 0), "core", 1)
     low, high = jnp.where(first, ours, others), jnp.where(first, others, ours)
     heads = [part[:, i * HEAD_DIM : (i + 1) * HEAD_DIM] for part in (low, high) for i in range(4)]
     weight = jnp.concatenate(heads[0::2] + heads[1::2], axis=1)
-    kv_out = assemble(block[:TOK], shift(block[TOK:], "core", 1))
     return dq[:, None], kv_out[None], weight
 
 

time: 119 us -> 114 us (0.958); the launches traced: 119 us -> 112 us
  waiting for transfers between devices: 24.3 us -> 20 us
  starting transfers between devices: 73.7 us -> 72.5 us
  Pallas kernels: 13.2 us -> 12 us
    ppermute x27, waiting for transfers between devices: 18.9 us -> 13.6 us  [shift(): lax.ppermute(value, axis, [(i, (i + by) % size) for i in range(size)])]
  transfers between devices with their start and end apart: 30 -> 30, of which waited for: 11 -> 13; matrix products, arithmetic and copies ran while one was open for 4% -> 4% of each run, Pallas kernels for 11% -> 11%
where the time goes in v5:
time: 114 us; the launch traced here: 112 us
  starting transfers between devices  72.5 us (64%)
  waiting for transfers between devices  20 us (18%)
  Pallas kernels  12 us (11%)
  local copies, waits for them, and re-layouts  4.1 us (4%)
  other arithmetic  2.04 us (2%)
    ppermute x27, starting transfers between devices, shift(): lax.ppermute(value, axis, [(i, (i + by) % size) for i in range(size)])  51 us
    ppermute x3, starting transfers between devices, ctx_shift(): return lax.ppermute(value, ('x', 'zh', 'core'), pairs)  21.6 us
    ppermute x27, waiting for transfers between devices, shift(): lax.ppermute(value, axis, [(i, (i + by) % size) for i in range(size)])  13.6 us
    pallas_call x1, Pallas kernels, attention(): pl.pallas_call(attention_kernel, grid_spec=pltpu.PrefetchScalarGridSpec(n...  9.15 us
    ppermute x3, waiting for transfers between devices, ctx_shift(): return lax.ppermute(value, ('x', 'zh', 'core'), pairs)  6.37 us
    pallas_call x2, Pallas kernels, products(): pl.pallas_call(product_kernel, in_specs=[pl.BlockSpec(memory_space=pltpu....  2.89 us
  transfers between devices with their start and end apart: 30, of which 13 were waited for; matrix products, arithmetic and copies ran while one was open for 4% of the time, Pallas kernels for 11%

profile of v5, /device:TPU:3, one launch (start us, length us, event | category | flops | bytes accessed | tf_op | source)
XLA Modules:
  0.0 111.8 jit_solution(13418205423369201039)
XLA Ops:
  0.6 8.8 %collective-permute-start = (bf16[128,1024]{1,0:T(8,128)(2,1)}, bf16[128,1024]{1,0:T(8,128)(2,1)S(1)}, u32[]{:S(2)}, u32[]{:S(2)}) collective-permute-start(bf16[128,1024]{1,0:T(8,128)(2,1)} %bitcast.75), channel_id=1, source_target_pairs={{0,2},{1,3},{2,4},{3,5},{4,6},{5,7},{6,8},{7,9},{8,10},{9,11},{10,... | collective-permute-start | bytes 786440 | tf_op jit(solution)/shard_map/ppermute | solution.py:31
  9.5 1.4 %dynamic-slice_bitcast_fusion = (bf16[4,320,128]{2,1,0:T(8,128)(2,1)S(1)}, bf16[4,320,128]{2,1,0:T(8,128)(2,1)S(1)}, bf16[4,320,128]{2,1,0:T(8,128)(2,1)S(1)}, bf16[4,320,128]{2,1,0:T(8,128)(2,1)S(1)}) fusion(bf16[4,4,320,128]{3,2,1,0:T(8,128)(2,1)} %bitcast.67, s32[]{:T(128)S(6)} %select_n.159, s32[]{:T(128)S(6)} %select_n.157, s32[]{:T(128)S(6)} %select_n.155, ...), kind=kLoop, calls=%fused_computation.3 | loop fusion | bytes 2621456 | tf_op jit(solution)/shard_map/jit(dynamic_index_in_dim)/squeeze | solution.py:185
  10.9 1.4 %collective-permute-start.2 = (bf16[4,320,128]{2,1,0:T(8,128)(2,1)S(1)}, bf16[4,320,128]{2,1,0:T(8,128)(2,1)S(1)}, u32[]{:S(2)}, u32[]{:S(2)}) collective-permute-start(bf16[4,320,128]{2,1,0:T(8,128)(2,1)S(1)} %get-tuple-element.65), channel_id=1, source_target_pairs={{0,16},{16,32},{32,48},{48,0},{1,17},{17,33},{33,49},{49,1},{2,18}... | collective-permute-start | bytes 983048 | tf_op jit(solution)/shard_map/ppermute | solution.py:26
  12.3 2.6 %collective-permute-start.3 = (bf16[4,320,128]{2,1,0:T(8,128)(2,1)S(1)}, bf16[4,320,128]{2,1,0:T(8,128)(2,1)S(1)}, u32[]{:S(2)}, u32[]{:S(2)}) collective-permute-start(bf16[4,320,128]{2,1,0:T(8,128)(2,1)S(1)} %get-tuple-element.64), channel_id=1, source_target_pairs={{0,32},{16,48},{32,0},{48,16},{1,33},{17,49},{33,1},{49,17},{2,34}... | collective-permute-start | bytes 983048 | tf_op jit(solution)/shard_map/ppermute | solution.py:26
  14.9 1.1 collective-permute-start.4
  16.4 0.3 collective-permute-done.kv2_ref
  16.7 1.6 %collective-permute-start.1 = (bf16[128,1024]{1,0:T(8,128)(2,1)S(1)}, bf16[128,1024]{1,0:T(8,128)(2,1)S(1)}, u32[]{:S(2)}, u32[]{:S(2)}) collective-permute-start(bf16[128,1024]{1,0:T(8,128)(2,1)S(1)} %broadcast_select_fusion), channel_id=1, source_target_pairs={{0,1},{1,0},{2,3},{3,2},{4,5},{5,4},{6,7},{7,6},{8,9},{9,8},{10,11... | collective-permute-start | bytes 786440 | tf_op jit(solution)/shard_map/ppermute | solution.py:26
  18.3 0.2 fusion.16
  18.5 0.7 add_select_fusion.bias_ref
  19.2 0.3 collective-permute-done.1.kv1_ref
  19.5 0.7 copy-done.5
  20.2 9.2 %attention.1 = (bf16[2,128,2560]{2,1,0:T(8,128)(2,1)}, bf16[384,512]{1,0:T(8,128)(2,1)}, f32[384,512]{1,0:T(8,128)}) custom-call(s32[1]{0:T(128)} %bitcast.core_ref, f32[256,128]{1,0:T(8,128)} %add_select_fusion.bias_ref, bf16[2,128,2560]{2,1,0:T(8,128)(2,1)} %bitcast.78, bf16[2,128,2560]{2,1,0:T(8,128)(2,1)} %bitcast.79, bf16[128,1024]{1,0:T(8,128)(2,1)} %bitcast.76, ...), custom_call_target="tpu_custom_call" | custom-call | flops 6000000000 | bytes 9000000 | tf_op jit(solution)/shard_map/attention/pallas_call | solution.py:121
  29.4 1.3 %collective-permute-start.5 = (bf16[384,512]{1,0:T(8,128)(2,1)}, bf16[384,512]{1,0:T(8,128)(2,1)S(1)}, u32[]{:S(2)}, u32[]{:S(2)}) collective-permute-start(bf16[384,512]{1,0:T(8,128)(2,1)} %get-tuple-element.34), channel_id=1, source_target_pairs={{0,1},{1,0},{2,3},{3,2},{4,5},{5,4},{6,7},{7,6},{8,9},{9,8},{10,11... | collective-permute-start | bytes 1179656 | tf_op jit(solution)/shard_map/ppermute | solution.py:26
  30.6 0.2 pad_maximum_fusion.own_ref
  30.9 1.3 %collective-permute-done.5 = bf16[384,512]{1,0:T(8,128)(2,1)S(1)} collective-permute-done((bf16[384,512]{1,0:T(8,128)(2,1)}, bf16[384,512]{1,0:T(8,128)(2,1)S(1)}, u32[]{:S(2)}, u32[]{:S(2)}) %collective-permute-start.5) | collective-permute-done | bytes 393248 | tf_op jit(solution)/shard_map/ppermute | solution.py:26
  32.4 10.8 %collective-permute-start.7 = (bf16[256,256]{1,0:T(8,128)(2,1)S(1)}, bf16[256,256]{1,0:T(8,128)(2,1)S(1)}, u32[]{:S(2)}, u32[]{:S(2)}) collective-permute-start(bf16[256,256]{1,0:T(8,128)(2,1)S(1)} %pad_maximum_fusion.5), channel_id=1, source_target_pairs={{2,0},{3,1},{4,2},{5,3},{6,4},{7,5},{8,6},{9,7},{10,8},{11,9},{12,... | collective-permute-start | bytes 393224 | tf_op jit(solution)/shard_map/ppermute | solution.py:31
  43.2 1.9 %collective-permute-start.17 = (bf16[256,256]{1,0:T(8,128)(2,1)S(1)}, bf16[256,256]{1,0:T(8,128)(2,1)S(1)}, u32[]{:S(2)}, u32[]{:S(2)}) collective-permute-start(bf16[256,256]{1,0:T(8,128)(2,1)S(1)} %pad_maximum_fusion.4), channel_id=1, source_target_pairs={{2,0},{3,1},{4,2},{5,3},{6,4},{7,5},{8,6},{9,7},{10,8},{11,9},{12,... | collective-permute-start | bytes 393224 | tf_op jit(solution)/shard_map/ppermute | solution.py:31
  45.3 1.5 %collective-permute-done.7 = bf16[256,256]{1,0:T(8,128)(2,1)S(1)} collective-permute-done((bf16[256,256]{1,0:T(8,128)(2,1)S(1)}, bf16[256,256]{1,0:T(8,128)(2,1)S(1)}, u32[]{:S(2)}, u32[]{:S(2)}) %collective-permute-start.7) | collective-permute-done | bytes 131104 | tf_op jit(solution)/shard_map/ppermute | solution.py:31
  46.8 6.4 %collective-permute-start.10 = (bf16[256,256]{1,0:T(8,128)(2,1)S(1)}, bf16[256,256]{1,0:T(8,128)(2,1)S(1)}, u32[]{:S(2)}, u32[]{:S(2)}) collective-permute-start(bf16[256,256]{1,0:T(8,128)(2,1)S(1)} %fusion.refs_0_), channel_id=1, source_target_pairs={{0,192},{64,0},{128,64},{192,128},{1,193},{65,1},{129,65},{193,129... | collective-permute-start | bytes 393224 | tf_op jit(solution)/shard_map/ppermute | solution.py:26
  53.2 0.5 collective-permute-start.9
  53.6 4.6 %collective-permute-done.17 = bf16[256,256]{1,0:T(8,128)(2,1)S(1)} collective-permute-done((bf16[256,256]{1,0:T(8,128)(2,1)S(1)}, bf16[256,256]{1,0:T(8,128)(2,1)S(1)}, u32[]{:S(2)}, u32[]{:S(2)}) %collective-permute-start.17) | collective-permute-done | bytes 131104 | tf_op jit(solution)/shard_map/ppermute | solution.py:31
  58.4 1.3 %collective-permute-start.28 = (bf16[128,512]{1,0:T(8,128)(2,1)S(1)}, bf16[128,512]{1,0:T(8,128)(2,1)S(1)}, u32[]{:S(2)}, u32[]{:S(2)}) collective-permute-start(bf16[128,512]{1,0:T(8,128)(2,1)S(1)} %pad_maximum_fusion.3), channel_id=1, source_target_pairs={{0,1},{1,0},{2,3},{3,2},{4,5},{5,4},{6,7},{7,6},{8,9},{9,8},{10,11... | collective-permute-start | bytes 393224 | tf_op jit(solution)/shard_map/ppermute | solution.py:26
  59.8 0.9 collective-permute-done.8.refs_1_
  60.6 3.4 %collective-permute-start.19 = (bf16[256,256]{1,0:T(8,128)(2,1)S(1)}, bf16[256,256]{1,0:T(8,128)(2,1)S(1)}, u32[]{:S(2)}, u32[]{:S(2)}) collective-permute-start(bf16[256,256]{1,0:T(8,128)(2,1)S(1)} %add_convert_fusion.2.refs_0_), channel_id=1, source_target_pairs={{0,128},{64,192},{128,0},{192,64},{1,129},{65,193},{129,1},{193,65... | collective-permute-start | bytes 393224 | tf_op jit(solution)/shard_map/ppermute | solution.py:26
  64.0 7.0 %collective-permute-done.9.refs_2_ = bf16[256,256]{1,0:T(8,128)(2,1)S(1)} collective-permute-done((bf16[256,256]{1,0:T(8,128)(2,1)S(1)}, bf16[256,256]{1,0:T(8,128)(2,1)S(1)}, u32[]{:S(2)}, u32[]{:S(2)}) %collective-permute-start.9) | collective-permute-done | bytes 131104 | tf_op jit(solution)/shard_map/ppermute | solution.py:26
  71.1 1.4 %products.2 = (bf16[4,80,256]{2,1,0:T(8,128)(2,1)S(1)}, bf16[4,80,256]{2,1,0:T(8,128)(2,1)S(1)}, bf16[4,80,256]{2,1,0:T(8,128)(2,1)S(1)}, bf16[4,80,256]{2,1,0:T(8,128)(2,1)S(1)}) custom-call(s32[3]{0:T(128)S(1)} %pad_add_fusion.at_ref, bf16[4,4,320,128]{3,2,1,0:T(8,128)(2,1)S(1)} %pad_maximum_fusion.own_ref, ...), custom_call_target="tpu_custom_call" | custom-call | flops 700000000 | bytes 4000000 | tf_op jit(solution)/shard_map/products/pallas_call | solution.py:158
  72.5 2.5 %collective-permute-start.11 = (bf16[4,80,256]{2,1,0:T(8,128)(2,1)S(1)}, bf16[4,80,256]{2,1,0:T(8,128)(2,1)S(1)}, u32[]{:S(2)}, u32[]{:S(2)}) collective-permute-start(bf16[4,80,256]{2,1,0:T(8,128)(2,1)S(1)} %get-tuple-element.42), channel_id=1, source_target_pairs={{0,4},{4,8},{8,12},{12,0},{1,5},{5,9},{9,13},{13,1},{2,6},{6,10},{... | collective-permute-start | bytes 491528 | tf_op jit(solution)/shard_map/ppermute | solution.py:26
  75.0 0.2 collective-permute-start.12
  75.2 2.0 %collective-permute-start.13 = (bf16[4,80,256]{2,1,0:T(8,128)(2,1)S(1)}, bf16[4,80,256]{2,1,0:T(8,128)(2,1)S(1)}, u32[]{:S(2)}, u32[]{:S(2)}) collective-permute-start(bf16[4,80,256]{2,1,0:T(8,128)(2,1)S(1)} %get-tuple-element.44), channel_id=1, source_target_pairs={{0,12},{4,0},{8,4},{12,8},{1,13},{5,1},{9,5},{13,9},{2,14},{6,2},{... | collective-permute-start | bytes 491528 | tf_op jit(solution)/shard_map/ppermute | solution.py:26
  77.3 1.4 %products.3 = (bf16[4,80,256]{2,1,0:T(8,128)(2,1)S(1)}, bf16[4,80,256]{2,1,0:T(8,128)(2,1)S(1)}, bf16[4,80,256]{2,1,0:T(8,128)(2,1)S(1)}, bf16[4,80,256]{2,1,0:T(8,128)(2,1)S(1)}) custom-call(s32[3]{0:T(128)S(1)} %pad_add_fusion.at_ref, bf16[4,4,320,128]{3,2,1,0:T(8,128)(2,1)S(1)} %pad_maximum_fusion.own_ref, ...), custom_call_target="tpu_custom_call" | custom-call | flops 700000000 | bytes 4000000 | tf_op jit(solution)/shard_map/products/pallas_call | solution.py:158
  78.7 1.0 collective-permute-start.21
  79.8 2.5 %collective-permute-start.22 = (bf16[4,80,256]{2,1,0:T(8,128)(2,1)S(1)}, bf16[4,80,256]{2,1,0:T(8,128)(2,1)S(1)}, u32[]{:S(2)}, u32[]{:S(2)}) collective-permute-start(bf16[4,80,256]{2,1,0:T(8,128)(2,1)S(1)} %get-tuple-element.47), channel_id=1, source_target_pairs={{0,8},{4,12},{8,0},{12,4},{1,9},{5,13},{9,1},{13,5},{2,10},{6,14},... | collective-permute-start | bytes 491528 | tf_op jit(solution)/shard_map/ppermute | solution.py:26
  82.4 1.4 %collective-permute-start.14 = (bf16[80,256]{1,0:T(8,128)(2,1)S(1)}, bf16[80,256]{1,0:T(8,128)(2,1)S(1)}, u32[]{:S(2)}, u32[]{:S(2)}) collective-permute-start(bf16[80,256]{1,0:T(8,128)(2,1)S(1)} %get-tuple-element.85), channel_id=1, source_target_pairs={{0,16},{16,32},{32,48},{48,0},{1,17},{17,33},{33,49},{49,1},{2,18}... | collective-permute-start | bytes 122888 | tf_op jit(solution)/shard_map/ppermute | solution.py:26
  83.8 2.6 %collective-permute-start.15 = (bf16[80,256]{1,0:T(8,128)(2,1)S(1)}, bf16[80,256]{1,0:T(8,128)(2,1)S(1)}, u32[]{:S(2)}, u32[]{:S(2)}) collective-permute-start(bf16[80,256]{1,0:T(8,128)(2,1)S(1)} %get-tuple-element.87), channel_id=1, source_target_pairs={{0,32},{16,48},{32,0},{48,16},{1,33},{17,49},{33,1},{49,17},{2,34}... | collective-permute-start | bytes 122888 | tf_op jit(solution)/shard_map/ppermute | solution.py:26
  86.4 0.9 collective-permute-done.21
  87.3 2.7 %collective-permute-start.16 = (bf16[80,256]{1,0:T(8,128)(2,1)S(1)}, bf16[80,256]{1,0:T(8,128)(2,1)S(1)}, u32[]{:S(2)}, u32[]{:S(2)}) collective-permute-start(bf16[80,256]{1,0:T(8,128)(2,1)S(1)} %get-tuple-element.86), channel_id=1, source_target_pairs={{0,48},{16,0},{32,16},{48,32},{1,49},{17,1},{33,17},{49,33},{2,50}... | collective-permute-start | bytes 122888 | tf_op jit(solution)/shard_map/ppermute | solution.py:26
  90.2 2.2 %collective-permute-start.25 = (bf16[80,256]{1,0:T(8,128)(2,1)S(1)}, bf16[80,256]{1,0:T(8,128)(2,1)S(1)}, u32[]{:S(2)}, u32[]{:S(2)}) collective-permute-start(bf16[80,256]{1,0:T(8,128)(2,1)S(1)} %get-tuple-element.90), channel_id=1, source_target_pairs={{0,32},{16,48},{32,0},{48,16},{1,33},{17,49},{33,1},{49,17},{2,34}... | collective-permute-start | bytes 122888 | tf_op jit(solution)/shard_map/ppermute | solution.py:26
  92.5 1.1 collective-permute-start.26
  93.6 0.7 collective-permute-done.24
  94.3 0.4 collective-permute-done.25
  94.7 0.9 collective-permute-done.26
  95.7 5.5 %collective-permute-start.27 = (bf16[40,512]{1,0:T(8,128)(2,1)S(1)}, bf16[40,512]{1,0:T(8,128)(2,1)S(1)}, u32[]{:S(2)}, u32[]{:S(2)}) collective-permute-start(bf16[40,512]{1,0:T(8,128)(2,1)S(1)} %dynamic-slice_bitcast_fusion.5), channel_id=1, source_target_pairs={{0,2},{2,0},{1,3},{3,1},{4,6},{6,4},{5,7},{7,5},{8,10},{10,8},{9,1... | collective-permute-start | bytes 122888 | tf_op jit(solution)/shard_map/ppermute | solution.py:26
  101.2 0.2 reshape.149
  101.5 0.9 reshape.150
  102.3 0.2 collective-permute-done.27
  102.6 7.6 %collective-permute-start.29 = (f32[20,512]{1,0:T(8,128)S(1)}, f32[20,512]{1,0:T(8,128)S(1)}, u32[]{:S(2)}, u32[]{:S(2)}) collective-permute-start(f32[20,512]{1,0:T(8,128)S(1)} %dynamic-slice_bitcast_fusion.4), channel_id=1, source_target_pairs={{0,1},{1,0},{2,3},{3,2},{4,5},{5,4},{6,7},{7,6},{8,9},{9,8},{10,11... | collective-permute-start | bytes 122888 | tf_op jit(solution)/shard_map/ppermute | solution.py:26
  110.2 0.9 collective-permute-done.29
  111.2 0.6 copy-done.3
  (75 shorter events, 1.7 us)
Async XLA Ops:
  0.6 16.0 %collective-permute-start = (bf16[128,1024]{1,0:T(8,128)(2,1)}, bf16[128,1024]{1,0:T(8,128)(2,1)S(1)}, u32[]{:S(2)}, u32[]{:S(2)}) collective-permute-start(bf16[128,1024]{1,0:T(8,128)(2,1)} %bitcast.75), channel_id=1, source_target_pairs={{0,2},{1,3},{2,4},{3,5},{4,6},{5,7},{6,8},{7,9},{8,10},{9,11},{10,... | collective-permute-start | bytes 786440 | tf_op jit(solution)/shard_map/ppermute | solution.py:31
  9.5 6.5 %copy-start.4 = (s32[1,16]{1,0:T(1,128)S(1)}, s32[1,16]{1,0:T(1,128)}, u32[]{:S(2)}) copy-start(s32[1,16]{1,0:T(1,128)} %param.9) | copy-start | bytes 196
  9.5 7.1 %copy-start.1 = (bf16[1,128,1024]{2,1,0:T(8,128)(2,1)S(1)}, bf16[1,128,1024]{2,1,0:T(8,128)(2,1)}, u32[]{:S(2)}) copy-start(bf16[1,128,1024]{2,1,0:T(8,128)(2,1)} %param.6) | copy-start | bytes 786436
  10.9 18.4 %collective-permute-start.2 = (bf16[4,320,128]{2,1,0:T(8,128)(2,1)S(1)}, bf16[4,320,128]{2,1,0:T(8,128)(2,1)S(1)}, u32[]{:S(2)}, u32[]{:S(2)}) collective-permute-start(bf16[4,320,128]{2,1,0:T(8,128)(2,1)S(1)} %get-tuple-element.65), channel_id=1, source_target_pairs={{0,16},{16,32},{32,48},{48,0},{1,17},{17,33},{33,49},{49,1},{2,18}... | collective-permute-start | bytes 983048 | tf_op jit(solution)/shard_map/ppermute | solution.py:26
  12.3 17.0 %collective-permute-start.3 = (bf16[4,320,128]{2,1,0:T(8,128)(2,1)S(1)}, bf16[4,320,128]{2,1,0:T(8,128)(2,1)S(1)}, u32[]{:S(2)}, u32[]{:S(2)}) collective-permute-start(bf16[4,320,128]{2,1,0:T(8,128)(2,1)S(1)} %get-tuple-element.64), channel_id=1, source_target_pairs={{0,32},{16,48},{32,0},{48,16},{1,33},{17,49},{33,1},{49,17},{2,34}... | collective-permute-start | bytes 983048 | tf_op jit(solution)/shard_map/ppermute | solution.py:26
  14.9 14.4 %collective-permute-start.4 = (bf16[4,320,128]{2,1,0:T(8,128)(2,1)S(1)}, bf16[4,320,128]{2,1,0:T(8,128)(2,1)S(1)}, u32[]{:S(2)}, u32[]{:S(2)}) collective-permute-start(bf16[4,320,128]{2,1,0:T(8,128)(2,1)S(1)} %get-tuple-element.63), channel_id=1, source_target_pairs={{0,48},{16,0},{32,16},{48,32},{1,49},{17,1},{33,17},{49,33},{2,50}... | collective-permute-start | bytes 983048 | tf_op jit(solution)/shard_map/ppermute | solution.py:26
  16.6 2.8 %copy-start.2 = (bf16[128,1024]{1,0:T(8,128)(2,1)}, bf16[128,1024]{1,0:T(8,128)(2,1)S(1)}, u32[]{:S(2)}) copy-start(bf16[128,1024]{1,0:T(8,128)(2,1)S(1)} %collective-permute-done.kv2_ref) | copy-start | bytes 786436
  16.7 2.8 %collective-permute-start.1 = (bf16[128,1024]{1,0:T(8,128)(2,1)S(1)}, bf16[128,1024]{1,0:T(8,128)(2,1)S(1)}, u32[]{:S(2)}, u32[]{:S(2)}) collective-permute-start(bf16[128,1024]{1,0:T(8,128)(2,1)S(1)} %broadcast_select_fusion), channel_id=1, source_target_pairs={{0,1},{1,0},{2,3},{3,2},{4,5},{5,4},{6,7},{7,6},{8,9},{9,8},{10,11... | collective-permute-start | bytes 786440 | tf_op jit(solution)/shard_map/ppermute | solution.py:26
  19.5 0.7 copy-start.5
  29.4 2.8 %collective-permute-start.5 = (bf16[384,512]{1,0:T(8,128)(2,1)}, bf16[384,512]{1,0:T(8,128)(2,1)S(1)}, u32[]{:S(2)}, u32[]{:S(2)}) collective-permute-start(bf16[384,512]{1,0:T(8,128)(2,1)} %get-tuple-element.34), channel_id=1, source_target_pairs={{0,1},{1,0},{2,3},{3,2},{4,5},{5,4},{6,7},{7,6},{8,9},{9,8},{10,11... | collective-permute-start | bytes 1179656 | tf_op jit(solution)/shard_map/ppermute | solution.py:26
  30.6 1.6 %copy-start = (f32[384,512]{1,0:T(8,128)S(1)}, f32[384,512]{1,0:T(8,128)}, u32[]{:S(2)}) copy-start(f32[384,512]{1,0:T(8,128)} %get-tuple-element.35) | copy-start | bytes 2359300
  30.8 40.3 %collective-permute-start.6 = (bf16[4,4,320,128]{3,2,1,0:T(8,128)(2,1)S(1)}, bf16[4,4,320,128]{3,2,1,0:T(8,128)(2,1)S(1)}, u32[]{:S(2)}, u32[]{:S(2)}) collective-permute-start(bf16[4,4,320,128]{3,2,1,0:T(8,128)(2,1)S(1)} %pad_maximum_fusion.own_ref), channel_id=1, source_target_pairs={{0,1},{1,0},{2,3},{3,2},{4,5},{5,4},{6,7},{7,6},{8,9},{9,8},{10,11... | collective-permute-start | bytes 3932168 | tf_op jit(solution)/shard_map/ppermute | solution.py:26
  32.4 14.4 %collective-permute-start.7 = (bf16[256,256]{1,0:T(8,128)(2,1)S(1)}, bf16[256,256]{1,0:T(8,128)(2,1)S(1)}, u32[]{:S(2)}, u32[]{:S(2)}) collective-permute-start(bf16[256,256]{1,0:T(8,128)(2,1)S(1)} %pad_maximum_fusion.5), channel_id=1, source_target_pairs={{2,0},{3,1},{4,2},{5,3},{6,4},{7,5},{8,6},{9,7},{10,8},{11,9},{12,... | collective-permute-start | bytes 393224 | tf_op jit(solution)/shard_map/ppermute | solution.py:31
  43.2 15.0 %collective-permute-start.17 = (bf16[256,256]{1,0:T(8,128)(2,1)S(1)}, bf16[256,256]{1,0:T(8,128)(2,1)S(1)}, u32[]{:S(2)}, u32[]{:S(2)}) collective-permute-start(bf16[256,256]{1,0:T(8,128)(2,1)S(1)} %pad_maximum_fusion.4), channel_id=1, source_target_pairs={{2,0},{3,1},{4,2},{5,3},{6,4},{7,5},{8,6},{9,7},{10,8},{11,9},{12,... | collective-permute-start | bytes 393224 | tf_op jit(solution)/shard_map/ppermute | solution.py:31
  46.8 11.6 %collective-permute-start.10 = (bf16[256,256]{1,0:T(8,128)(2,1)S(1)}, bf16[256,256]{1,0:T(8,128)(2,1)S(1)}, u32[]{:S(2)}, u32[]{:S(2)}) collective-permute-start(bf16[256,256]{1,0:T(8,128)(2,1)S(1)} %fusion.refs_0_), channel_id=1, source_target_pairs={{0,192},{64,0},{128,64},{192,128},{1,193},{65,1},{129,65},{193,129... | collective-permute-start | bytes 393224 | tf_op jit(solution)/shard_map/ppermute | solution.py:26
  53.2 7.5 %collective-permute-start.8 = (bf16[256,256]{1,0:T(8,128)(2,1)S(1)}, bf16[256,256]{1,0:T(8,128)(2,1)S(1)}, u32[]{:S(2)}, u32[]{:S(2)}) collective-permute-start(bf16[256,256]{1,0:T(8,128)(2,1)S(1)} %fusion.refs_0_), channel_id=1, source_target_pairs={{0,64},{64,128},{128,192},{192,0},{1,65},{65,129},{129,193},{193,1... | collective-permute-start | bytes 393224 | tf_op jit(solution)/shard_map/ppermute | solution.py:26
  53.2 17.9 %collective-permute-start.9 = (bf16[256,256]{1,0:T(8,128)(2,1)S(1)}, bf16[256,256]{1,0:T(8,128)(2,1)S(1)}, u32[]{:S(2)}, u32[]{:S(2)}) collective-permute-start(bf16[256,256]{1,0:T(8,128)(2,1)S(1)} %fusion.refs_0_), channel_id=1, source_target_pairs={{0,128},{64,192},{128,0},{192,64},{1,129},{65,193},{129,1},{193,65... | collective-permute-start | bytes 393224 | tf_op jit(solution)/shard_map/ppermute | solution.py:26
  58.3 16.9 %collective-permute-start.18 = (bf16[256,256]{1,0:T(8,128)(2,1)S(1)}, bf16[256,256]{1,0:T(8,128)(2,1)S(1)}, u32[]{:S(2)}, u32[]{:S(2)}) collective-permute-start(bf16[256,256]{1,0:T(8,128)(2,1)S(1)} %add_convert_fusion.2.refs_0_), channel_id=1, source_target_pairs={{0,64},{64,128},{128,192},{192,0},{1,65},{65,129},{129,193},{193,1... | collective-permute-start | bytes 393224 | tf_op jit(solution)/shard_map/ppermute | solution.py:26
  58.4 16.6 %collective-permute-start.28 = (bf16[128,512]{1,0:T(8,128)(2,1)S(1)}, bf16[128,512]{1,0:T(8,128)(2,1)S(1)}, u32[]{:S(2)}, u32[]{:S(2)}) collective-permute-start(bf16[128,512]{1,0:T(8,128)(2,1)S(1)} %pad_maximum_fusion.3), channel_id=1, source_target_pairs={{0,1},{1,0},{2,3},{3,2},{4,5},{5,4},{6,7},{7,6},{8,9},{9,8},{10,11... | collective-permute-start | bytes 393224 | tf_op jit(solution)/shard_map/ppermute | solution.py:26
  60.6 16.6 %collective-permute-start.19 = (bf16[256,256]{1,0:T(8,128)(2,1)S(1)}, bf16[256,256]{1,0:T(8,128)(2,1)S(1)}, u32[]{:S(2)}, u32[]{:S(2)}) collective-permute-start(bf16[256,256]{1,0:T(8,128)(2,1)S(1)} %add_convert_fusion.2.refs_0_), channel_id=1, source_target_pairs={{0,128},{64,192},{128,0},{192,64},{1,129},{65,193},{129,1},{193,65... | collective-permute-start | bytes 393224 | tf_op jit(solution)/shard_map/ppermute | solution.py:26
  71.1 6.2 %collective-permute-start.20 = (bf16[256,256]{1,0:T(8,128)(2,1)S(1)}, bf16[256,256]{1,0:T(8,128)(2,1)S(1)}, u32[]{:S(2)}, u32[]{:S(2)}) collective-permute-start(bf16[256,256]{1,0:T(8,128)(2,1)S(1)} %add_convert_fusion.2.refs_0_), channel_id=1, source_target_pairs={{0,192},{64,0},{128,64},{192,128},{1,193},{65,1},{129,65},{193,129... | collective-permute-start | bytes 393224 | tf_op jit(solution)/shard_map/ppermute | solution.py:26
  72.5 9.8 %collective-permute-start.11 = (bf16[4,80,256]{2,1,0:T(8,128)(2,1)S(1)}, bf16[4,80,256]{2,1,0:T(8,128)(2,1)S(1)}, u32[]{:S(2)}, u32[]{:S(2)}) collective-permute-start(bf16[4,80,256]{2,1,0:T(8,128)(2,1)S(1)} %get-tuple-element.42), channel_id=1, source_target_pairs={{0,4},{4,8},{8,12},{12,0},{1,5},{5,9},{9,13},{13,1},{2,6},{6,10},{... | collective-permute-start | bytes 491528 | tf_op jit(solution)/shard_map/ppermute | solution.py:26
  75.0 7.3 %collective-permute-start.12 = (bf16[4,80,256]{2,1,0:T(8,128)(2,1)S(1)}, bf16[4,80,256]{2,1,0:T(8,128)(2,1)S(1)}, u32[]{:S(2)}, u32[]{:S(2)}) collective-permute-start(bf16[4,80,256]{2,1,0:T(8,128)(2,1)S(1)} %get-tuple-element.43), channel_id=1, source_target_pairs={{0,8},{4,12},{8,0},{12,4},{1,9},{5,13},{9,1},{13,5},{2,10},{6,14},... | collective-permute-start | bytes 491528 | tf_op jit(solution)/shard_map/ppermute | solution.py:26
  75.2 7.0 %collective-permute-start.13 = (bf16[4,80,256]{2,1,0:T(8,128)(2,1)S(1)}, bf16[4,80,256]{2,1,0:T(8,128)(2,1)S(1)}, u32[]{:S(2)}, u32[]{:S(2)}) collective-permute-start(bf16[4,80,256]{2,1,0:T(8,128)(2,1)S(1)} %get-tuple-element.44), channel_id=1, source_target_pairs={{0,12},{4,0},{8,4},{12,8},{1,13},{5,1},{9,5},{13,9},{2,14},{6,2},{... | collective-permute-start | bytes 491528 | tf_op jit(solution)/shard_map/ppermute | solution.py:26
  78.7 8.6 %collective-permute-start.21 = (bf16[4,80,256]{2,1,0:T(8,128)(2,1)S(1)}, bf16[4,80,256]{2,1,0:T(8,128)(2,1)S(1)}, u32[]{:S(2)}, u32[]{:S(2)}) collective-permute-start(bf16[4,80,256]{2,1,0:T(8,128)(2,1)S(1)} %get-tuple-element.46), channel_id=1, source_target_pairs={{0,4},{4,8},{8,12},{12,0},{1,5},{5,9},{9,13},{13,1},{2,6},{6,10},{... | collective-permute-start | bytes 491528 | tf_op jit(solution)/shard_map/ppermute | solution.py:26
  79.8 10.2 %collective-permute-start.22 = (bf16[4,80,256]{2,1,0:T(8,128)(2,1)S(1)}, bf16[4,80,256]{2,1,0:T(8,128)(2,1)S(1)}, u32[]{:S(2)}, u32[]{:S(2)}) collective-permute-start(bf16[4,80,256]{2,1,0:T(8,128)(2,1)S(1)} %get-tuple-element.47), channel_id=1, source_target_pairs={{0,8},{4,12},{8,0},{12,4},{1,9},{5,13},{9,1},{13,5},{2,10},{6,14},... | collective-permute-start | bytes 491528 | tf_op jit(solution)/shard_map/ppermute | solution.py:26
  82.3 7.8 %collective-permute-start.23 = (bf16[4,80,256]{2,1,0:T(8,128)(2,1)S(1)}, bf16[4,80,256]{2,1,0:T(8,128)(2,1)S(1)}, u32[]{:S(2)}, u32[]{:S(2)}) collective-permute-start(bf16[4,80,256]{2,1,0:T(8,128)(2,1)S(1)} %get-tuple-element.48), channel_id=1, source_target_pairs={{0,12},{4,0},{8,4},{12,8},{1,13},{5,1},{9,5},{13,9},{2,14},{6,2},{... | collective-permute-start | bytes 491528 | tf_op jit(solution)/shard_map/ppermute | solution.py:26
  82.4 10.0 %collective-permute-start.14 = (bf16[80,256]{1,0:T(8,128)(2,1)S(1)}, bf16[80,256]{1,0:T(8,128)(2,1)S(1)}, u32[]{:S(2)}, u32[]{:S(2)}) collective-permute-start(bf16[80,256]{1,0:T(8,128)(2,1)S(1)} %get-tuple-element.85), channel_id=1, source_target_pairs={{0,16},{16,32},{32,48},{48,0},{1,17},{17,33},{33,49},{49,1},{2,18}... | collective-permute-start | bytes 122888 | tf_op jit(solution)/shard_map/ppermute | solution.py:26
  83.8 9.7 %collective-permute-start.15 = (bf16[80,256]{1,0:T(8,128)(2,1)S(1)}, bf16[80,256]{1,0:T(8,128)(2,1)S(1)}, u32[]{:S(2)}, u32[]{:S(2)}) collective-permute-start(bf16[80,256]{1,0:T(8,128)(2,1)S(1)} %get-tuple-element.87), channel_id=1, source_target_pairs={{0,32},{16,48},{32,0},{48,16},{1,33},{17,49},{33,1},{49,17},{2,34}... | collective-permute-start | bytes 122888 | tf_op jit(solution)/shard_map/ppermute | solution.py:26
  87.3 6.2 %collective-permute-start.16 = (bf16[80,256]{1,0:T(8,128)(2,1)S(1)}, bf16[80,256]{1,0:T(8,128)(2,1)S(1)}, u32[]{:S(2)}, u32[]{:S(2)}) collective-permute-start(bf16[80,256]{1,0:T(8,128)(2,1)S(1)} %get-tuple-element.86), channel_id=1, source_target_pairs={{0,48},{16,0},{32,16},{48,32},{1,49},{17,1},{33,17},{49,33},{2,50}... | collective-permute-start | bytes 122888 | tf_op jit(solution)/shard_map/ppermute | solution.py:26
  90.2 4.2 %collective-permute-start.24 = (bf16[80,256]{1,0:T(8,128)(2,1)S(1)}, bf16[80,256]{1,0:T(8,128)(2,1)S(1)}, u32[]{:S(2)}, u32[]{:S(2)}) collective-permute-start(bf16[80,256]{1,0:T(8,128)(2,1)S(1)} %get-tuple-element.88), channel_id=1, source_target_pairs={{0,16},{16,32},{32,48},{48,0},{1,17},{17,33},{33,49},{49,1},{2,18}... | collective-permute-start | bytes 122888 | tf_op jit(solution)/shard_map/ppermute | solution.py:26
  90.2 4.5 %collective-permute-start.25 = (bf16[80,256]{1,0:T(8,128)(2,1)S(1)}, bf16[80,256]{1,0:T(8,128)(2,1)S(1)}, u32[]{:S(2)}, u32[]{:S(2)}) collective-permute-start(bf16[80,256]{1,0:T(8,128)(2,1)S(1)} %get-tuple-element.90), channel_id=1, source_target_pairs={{0,32},{16,48},{32,0},{48,16},{1,33},{17,49},{33,1},{49,17},{2,34}... | collective-permute-start | bytes 122888 | tf_op jit(solution)/shard_map/ppermute | solution.py:26
  92.5 3.2 %collective-permute-start.26 = (bf16[80,256]{1,0:T(8,128)(2,1)S(1)}, bf16[80,256]{1,0:T(8,128)(2,1)S(1)}, u32[]{:S(2)}, u32[]{:S(2)}) collective-permute-start(bf16[80,256]{1,0:T(8,128)(2,1)S(1)} %get-tuple-element.89), channel_id=1, source_target_pairs={{0,48},{16,0},{32,16},{48,32},{1,49},{17,1},{33,17},{49,33},{2,50}... | collective-permute-start | bytes 122888 | tf_op jit(solution)/shard_map/ppermute | solution.py:26
  95.7 6.8 %collective-permute-start.27 = (bf16[40,512]{1,0:T(8,128)(2,1)S(1)}, bf16[40,512]{1,0:T(8,128)(2,1)S(1)}, u32[]{:S(2)}, u32[]{:S(2)}) collective-permute-start(bf16[40,512]{1,0:T(8,128)(2,1)S(1)} %dynamic-slice_bitcast_fusion.5), channel_id=1, source_target_pairs={{0,2},{2,0},{1,3},{3,1},{4,6},{6,4},{5,7},{7,5},{8,10},{10,8},{9,1... | collective-permute-start | bytes 122888 | tf_op jit(solution)/shard_map/ppermute | solution.py:26
  102.6 8.5 %collective-permute-start.29 = (f32[20,512]{1,0:T(8,128)S(1)}, f32[20,512]{1,0:T(8,128)S(1)}, u32[]{:S(2)}, u32[]{:S(2)}) collective-permute-start(f32[20,512]{1,0:T(8,128)S(1)} %dynamic-slice_bitcast_fusion.4), channel_id=1, source_target_pairs={{0,1},{1,0},{2,3},{3,2},{4,5},{5,4},{6,7},{7,6},{8,9},{9,8},{10,11... | collective-permute-start | bytes 122888 | tf_op jit(solution)/shard_map/ppermute | solution.py:26
  111.2 0.6 copy-start.3

commit v6 on v5

--- a/solution.py
+++ b/solution.py
@@ -235,7 +235,8 @@
     for here, came in halves:
         block = (here + came.astype(jnp.float32)).astype(jnp.bfloat16)
         blocks.append(block)
-        gathered = [block] + [shift(block, "zl", by) for by in (1, 2, 3)]
+        two = shift(block, "zl", 2)
+        gathered = [block, shift(block, "zl", 1), two, shift(block, "zl", 3)]
         pieces = products(jnp.stack([zl, x, y]).astype(jnp.int32), states, other_states, gathered)
         got = [pieces[0]] + [shift(pieces[by], "x", by) for by in (1, 2, 3)]
         reduced.append(total(got).astype(jnp.bfloat16))

time: 114 us -> 114 us (level)
  no operation moved by 1% of the time
where the time goes in v6:
time: 114 us; the launch traced here: 112 us
  starting transfers between devices  72.5 us (64%)
  waiting for transfers between devices  20 us (18%)
  Pallas kernels  12 us (11%)
  local copies, waits for them, and re-layouts  4.1 us (4%)
  other arithmetic  2.04 us (2%)
    ppermute x27, starting transfers between devices, shift(): lax.ppermute(value, axis, [(i, (i + by) % size) for i in range(size)])  51 us
    ppermute x3, starting transfers between devices, ctx_shift(): return lax.ppermute(value, ('x', 'zh', 'core'), pairs)  21.6 us
    ppermute x27, waiting for transfers between devices, shift(): lax.ppermute(value, axis, [(i, (i + by) % size) for i in range(size)])  13.6 us
    pallas_call x1, Pallas kernels, attention(): pl.pallas_call(attention_kernel, grid_spec=pltpu.PrefetchScalarGridSpec(n...  9.15 us
    ppermute x3, waiting for transfers between devices, ctx_shift(): return lax.ppermute(value, ('x', 'zh', 'core'), pairs)  6.37 us
    pallas_call x2, Pallas kernels, products(): pl.pallas_call(product_kernel, in_specs=[pl.BlockSpec(memory_space=pltpu....  2.89 us
  transfers between devices with their start and end apart: 30, of which 13 were waited for; matrix products, arithmetic and copies ran while one was open for 4% of the time, Pallas kernels for 11%

profile of v6, /device:TPU:3, one launch (start us, length us, event | category | flops | bytes accessed | tf_op | source)
XLA Modules:
  0.0 111.8 jit_solution(13418205423369201039)
XLA Ops:
  0.6 8.8 %collective-permute-start = (bf16[128,1024]{1,0:T(8,128)(2,1)}, bf16[128,1024]{1,0:T(8,128)(2,1)S(1)}, u32[]{:S(2)}, u32[]{:S(2)}) collective-permute-start(bf16[128,1024]{1,0:T(8,128)(2,1)} %bitcast.75), channel_id=1, source_target_pairs={{0,2},{1,3},{2,4},{3,5},{4,6},{5,7},{6,8},{7,9},{8,10},{9,11},{10,... | collective-permute-start | bytes 786440 | tf_op jit(solution)/shard_map/ppermute | solution.py:31
  9.5 1.4 %dynamic-slice_bitcast_fusion = (bf16[4,320,128]{2,1,0:T(8,128)(2,1)S(1)}, bf16[4,320,128]{2,1,0:T(8,128)(2,1)S(1)}, bf16[4,320,128]{2,1,0:T(8,128)(2,1)S(1)}, bf16[4,320,128]{2,1,0:T(8,128)(2,1)S(1)}) fusion(bf16[4,4,320,128]{3,2,1,0:T(8,128)(2,1)} %bitcast.67, s32[]{:T(128)S(6)} %select_n.159, s32[]{:T(128)S(6)} %select_n.157, s32[]{:T(128)S(6)} %select_n.155, ...), kind=kLoop, calls=%fused_computation.3 | loop fusion | bytes 2621456 | tf_op jit(solution)/shard_map/jit(dynamic_index_in_dim)/squeeze | solution.py:185
  10.9 1.4 %collective-permute-start.2 = (bf16[4,320,128]{2,1,0:T(8,128)(2,1)S(1)}, bf16[4,320,128]{2,1,0:T(8,128)(2,1)S(1)}, u32[]{:S(2)}, u32[]{:S(2)}) collective-permute-start(bf16[4,320,128]{2,1,0:T(8,128)(2,1)S(1)} %get-tuple-element.65), channel_id=1, source_target_pairs={{0,16},{16,32},{32,48},{48,0},{1,17},{17,33},{33,49},{49,1},{2,18}... | collective-permute-start | bytes 983048 | tf_op jit(solution)/shard_map/ppermute | solution.py:26
  12.3 2.6 %collective-permute-start.3 = (bf16[4,320,128]{2,1,0:T(8,128)(2,1)S(1)}, bf16[4,320,128]{2,1,0:T(8,128)(2,1)S(1)}, u32[]{:S(2)}, u32[]{:S(2)}) collective-permute-start(bf16[4,320,128]{2,1,0:T(8,128)(2,1)S(1)} %get-tuple-element.64), channel_id=1, source_target_pairs={{0,32},{16,48},{32,0},{48,16},{1,33},{17,49},{33,1},{49,17},{2,34}... | collective-permute-start | bytes 983048 | tf_op jit(solution)/shard_map/ppermute | solution.py:26
  14.9 1.1 collective-permute-start.4
  16.4 0.3 collective-permute-done.kv2_ref
  16.7 1.6 %collective-permute-start.1 = (bf16[128,1024]{1,0:T(8,128)(2,1)S(1)}, bf16[128,1024]{1,0:T(8,128)(2,1)S(1)}, u32[]{:S(2)}, u32[]{:S(2)}) collective-permute-start(bf16[128,1024]{1,0:T(8,128)(2,1)S(1)} %broadcast_select_fusion), channel_id=1, source_target_pairs={{0,1},{1,0},{2,3},{3,2},{4,5},{5,4},{6,7},{7,6},{8,9},{9,8},{10,11... | collective-permute-start | bytes 786440 | tf_op jit(solution)/shard_map/ppermute | solution.py:26
  18.3 0.2 fusion.16
  18.5 0.7 add_select_fusion.bias_ref
  19.2 0.3 collective-permute-done.1.kv1_ref
  19.5 0.7 copy-done.5
  20.2 9.2 %attention.1 = (bf16[2,128,2560]{2,1,0:T(8,128)(2,1)}, bf16[384,512]{1,0:T(8,128)(2,1)}, f32[384,512]{1,0:T(8,128)}) custom-call(s32[1]{0:T(128)} %bitcast.core_ref, f32[256,128]{1,0:T(8,128)} %add_select_fusion.bias_ref, bf16[2,128,2560]{2,1,0:T(8,128)(2,1)} %bitcast.78, bf16[2,128,2560]{2,1,0:T(8,128)(2,1)} %bitcast.79, bf16[128,1024]{1,0:T(8,128)(2,1)} %bitcast.76, ...), custom_call_target="tpu_custom_call" | custom-call | flops 6000000000 | bytes 9000000 | tf_op jit(solution)/shard_map/attention/pallas_call | solution.py:121
  29.4 1.3 %collective-permute-start.5 = (bf16[384,512]{1,0:T(8,128)(2,1)}, bf16[384,512]{1,0:T(8,128)(2,1)S(1)}, u32[]{:S(2)}, u32[]{:S(2)}) collective-permute-start(bf16[384,512]{1,0:T(8,128)(2,1)} %get-tuple-element.34), channel_id=1, source_target_pairs={{0,1},{1,0},{2,3},{3,2},{4,5},{5,4},{6,7},{7,6},{8,9},{9,8},{10,11... | collective-permute-start | bytes 1179656 | tf_op jit(solution)/shard_map/ppermute | solution.py:26
  30.6 0.2 pad_maximum_fusion.own_ref
  30.9 1.3 %collective-permute-done.5 = bf16[384,512]{1,0:T(8,128)(2,1)S(1)} collective-permute-done((bf16[384,512]{1,0:T(8,128)(2,1)}, bf16[384,512]{1,0:T(8,128)(2,1)S(1)}, u32[]{:S(2)}, u32[]{:S(2)}) %collective-permute-start.5) | collective-permute-done | bytes 393248 | tf_op jit(solution)/shard_map/ppermute | solution.py:26
  32.4 10.8 %collective-permute-start.7 = (bf16[256,256]{1,0:T(8,128)(2,1)S(1)}, bf16[256,256]{1,0:T(8,128)(2,1)S(1)}, u32[]{:S(2)}, u32[]{:S(2)}) collective-permute-start(bf16[256,256]{1,0:T(8,128)(2,1)S(1)} %pad_maximum_fusion.5), channel_id=1, source_target_pairs={{2,0},{3,1},{4,2},{5,3},{6,4},{7,5},{8,6},{9,7},{10,8},{11,9},{12,... | collective-permute-start | bytes 393224 | tf_op jit(solution)/shard_map/ppermute | solution.py:31
  43.2 1.9 %collective-permute-start.17 = (bf16[256,256]{1,0:T(8,128)(2,1)S(1)}, bf16[256,256]{1,0:T(8,128)(2,1)S(1)}, u32[]{:S(2)}, u32[]{:S(2)}) collective-permute-start(bf16[256,256]{1,0:T(8,128)(2,1)S(1)} %pad_maximum_fusion.4), channel_id=1, source_target_pairs={{2,0},{3,1},{4,2},{5,3},{6,4},{7,5},{8,6},{9,7},{10,8},{11,9},{12,... | collective-permute-start | bytes 393224 | tf_op jit(solution)/shard_map/ppermute | solution.py:31
  45.3 1.5 %collective-permute-done.7 = bf16[256,256]{1,0:T(8,128)(2,1)S(1)} collective-permute-done((bf16[256,256]{1,0:T(8,128)(2,1)S(1)}, bf16[256,256]{1,0:T(8,128)(2,1)S(1)}, u32[]{:S(2)}, u32[]{:S(2)}) %collective-permute-start.7) | collective-permute-done | bytes 131104 | tf_op jit(solution)/shard_map/ppermute | solution.py:31
  46.8 6.4 %collective-permute-start.10 = (bf16[256,256]{1,0:T(8,128)(2,1)S(1)}, bf16[256,256]{1,0:T(8,128)(2,1)S(1)}, u32[]{:S(2)}, u32[]{:S(2)}) collective-permute-start(bf16[256,256]{1,0:T(8,128)(2,1)S(1)} %fusion.refs_0_), channel_id=1, source_target_pairs={{0,192},{64,0},{128,64},{192,128},{1,193},{65,1},{129,65},{193,129... | collective-permute-start | bytes 393224 | tf_op jit(solution)/shard_map/ppermute | solution.py:26
  53.2 0.5 collective-permute-start.9
  53.6 4.6 %collective-permute-done.17 = bf16[256,256]{1,0:T(8,128)(2,1)S(1)} collective-permute-done((bf16[256,256]{1,0:T(8,128)(2,1)S(1)}, bf16[256,256]{1,0:T(8,128)(2,1)S(1)}, u32[]{:S(2)}, u32[]{:S(2)}) %collective-permute-start.17) | collective-permute-done | bytes 131104 | tf_op jit(solution)/shard_map/ppermute | solution.py:31
  58.4 1.3 %collective-permute-start.28 = (bf16[128,512]{1,0:T(8,128)(2,1)S(1)}, bf16[128,512]{1,0:T(8,128)(2,1)S(1)}, u32[]{:S(2)}, u32[]{:S(2)}) collective-permute-start(bf16[128,512]{1,0:T(8,128)(2,1)S(1)} %pad_maximum_fusion.3), channel_id=1, source_target_pairs={{0,1},{1,0},{2,3},{3,2},{4,5},{5,4},{6,7},{7,6},{8,9},{9,8},{10,11... | collective-permute-start | bytes 393224 | tf_op jit(solution)/shard_map/ppermute | solution.py:26
  59.8 0.9 collective-permute-done.8.refs_1_
  60.6 3.4 %collective-permute-start.19 = (bf16[256,256]{1,0:T(8,128)(2,1)S(1)}, bf16[256,256]{1,0:T(8,128)(2,1)S(1)}, u32[]{:S(2)}, u32[]{:S(2)}) collective-permute-start(bf16[256,256]{1,0:T(8,128)(2,1)S(1)} %add_convert_fusion.2.refs_0_), channel_id=1, source_target_pairs={{0,128},{64,192},{128,0},{192,64},{1,129},{65,193},{129,1},{193,65... | collective-permute-start | bytes 393224 | tf_op jit(solution)/shard_map/ppermute | solution.py:26
  64.0 7.0 %collective-permute-done.9.refs_2_ = bf16[256,256]{1,0:T(8,128)(2,1)S(1)} collective-permute-done((bf16[256,256]{1,0:T(8,128)(2,1)S(1)}, bf16[256,256]{1,0:T(8,128)(2,1)S(1)}, u32[]{:S(2)}, u32[]{:S(2)}) %collective-permute-start.9) | collective-permute-done | bytes 131104 | tf_op jit(solution)/shard_map/ppermute | solution.py:26
  71.1 1.4 %products.2 = (bf16[4,80,256]{2,1,0:T(8,128)(2,1)S(1)}, bf16[4,80,256]{2,1,0:T(8,128)(2,1)S(1)}, bf16[4,80,256]{2,1,0:T(8,128)(2,1)S(1)}, bf16[4,80,256]{2,1,0:T(8,128)(2,1)S(1)}) custom-call(s32[3]{0:T(128)S(1)} %pad_add_fusion.at_ref, bf16[4,4,320,128]{3,2,1,0:T(8,128)(2,1)S(1)} %pad_maximum_fusion.own_ref, ...), custom_call_target="tpu_custom_call" | custom-call | flops 700000000 | bytes 4000000 | tf_op jit(solution)/shard_map/products/pallas_call | solution.py:158
  72.5 2.5 %collective-permute-start.11 = (bf16[4,80,256]{2,1,0:T(8,128)(2,1)S(1)}, bf16[4,80,256]{2,1,0:T(8,128)(2,1)S(1)}, u32[]{:S(2)}, u32[]{:S(2)}) collective-permute-start(bf16[4,80,256]{2,1,0:T(8,128)(2,1)S(1)} %get-tuple-element.42), channel_id=1, source_target_pairs={{0,4},{4,8},{8,12},{12,0},{1,5},{5,9},{9,13},{13,1},{2,6},{6,10},{... | collective-permute-start | bytes 491528 | tf_op jit(solution)/shard_map/ppermute | solution.py:26
  75.0 0.2 collective-permute-start.12
  75.2 2.0 %collective-permute-start.13 = (bf16[4,80,256]{2,1,0:T(8,128)(2,1)S(1)}, bf16[4,80,256]{2,1,0:T(8,128)(2,1)S(1)}, u32[]{:S(2)}, u32[]{:S(2)}) collective-permute-start(bf16[4,80,256]{2,1,0:T(8,128)(2,1)S(1)} %get-tuple-element.44), channel_id=1, source_target_pairs={{0,12},{4,0},{8,4},{12,8},{1,13},{5,1},{9,5},{13,9},{2,14},{6,2},{... | collective-permute-start | bytes 491528 | tf_op jit(solution)/shard_map/ppermute | solution.py:26
  77.3 1.4 %products.3 = (bf16[4,80,256]{2,1,0:T(8,128)(2,1)S(1)}, bf16[4,80,256]{2,1,0:T(8,128)(2,1)S(1)}, bf16[4,80,256]{2,1,0:T(8,128)(2,1)S(1)}, bf16[4,80,256]{2,1,0:T(8,128)(2,1)S(1)}) custom-call(s32[3]{0:T(128)S(1)} %pad_add_fusion.at_ref, bf16[4,4,320,128]{3,2,1,0:T(8,128)(2,1)S(1)} %pad_maximum_fusion.own_ref, ...), custom_call_target="tpu_custom_call" | custom-call | flops 700000000 | bytes 4000000 | tf_op jit(solution)/shard_map/products/pallas_call | solution.py:158
  78.7 1.0 collective-permute-start.21
  79.8 2.5 %collective-permute-start.22 = (bf16[4,80,256]{2,1,0:T(8,128)(2,1)S(1)}, bf16[4,80,256]{2,1,0:T(8,128)(2,1)S(1)}, u32[]{:S(2)}, u32[]{:S(2)}) collective-permute-start(bf16[4,80,256]{2,1,0:T(8,128)(2,1)S(1)} %get-tuple-element.47), channel_id=1, source_target_pairs={{0,8},{4,12},{8,0},{12,4},{1,9},{5,13},{9,1},{13,5},{2,10},{6,14},... | collective-permute-start | bytes 491528 | tf_op jit(solution)/shard_map/ppermute | solution.py:26
  82.4 1.4 %collective-permute-start.14 = (bf16[80,256]{1,0:T(8,128)(2,1)S(1)}, bf16[80,256]{1,0:T(8,128)(2,1)S(1)}, u32[]{:S(2)}, u32[]{:S(2)}) collective-permute-start(bf16[80,256]{1,0:T(8,128)(2,1)S(1)} %get-tuple-element.85), channel_id=1, source_target_pairs={{0,16},{16,32},{32,48},{48,0},{1,17},{17,33},{33,49},{49,1},{2,18}... | collective-permute-start | bytes 122888 | tf_op jit(solution)/shard_map/ppermute | solution.py:26
  83.8 2.6 %collective-permute-start.15 = (bf16[80,256]{1,0:T(8,128)(2,1)S(1)}, bf16[80,256]{1,0:T(8,128)(2,1)S(1)}, u32[]{:S(2)}, u32[]{:S(2)}) collective-permute-start(bf16[80,256]{1,0:T(8,128)(2,1)S(1)} %get-tuple-element.87), channel_id=1, source_target_pairs={{0,32},{16,48},{32,0},{48,16},{1,33},{17,49},{33,1},{49,17},{2,34}... | collective-permute-start | bytes 122888 | tf_op jit(solution)/shard_map/ppermute | solution.py:26
  86.4 0.9 collective-permute-done.21
  87.3 2.7 %collective-permute-start.16 = (bf16[80,256]{1,0:T(8,128)(2,1)S(1)}, bf16[80,256]{1,0:T(8,128)(2,1)S(1)}, u32[]{:S(2)}, u32[]{:S(2)}) collective-permute-start(bf16[80,256]{1,0:T(8,128)(2,1)S(1)} %get-tuple-element.86), channel_id=1, source_target_pairs={{0,48},{16,0},{32,16},{48,32},{1,49},{17,1},{33,17},{49,33},{2,50}... | collective-permute-start | bytes 122888 | tf_op jit(solution)/shard_map/ppermute | solution.py:26
  90.2 2.2 %collective-permute-start.25 = (bf16[80,256]{1,0:T(8,128)(2,1)S(1)}, bf16[80,256]{1,0:T(8,128)(2,1)S(1)}, u32[]{:S(2)}, u32[]{:S(2)}) collective-permute-start(bf16[80,256]{1,0:T(8,128)(2,1)S(1)} %get-tuple-element.90), channel_id=1, source_target_pairs={{0,32},{16,48},{32,0},{48,16},{1,33},{17,49},{33,1},{49,17},{2,34}... | collective-permute-start | bytes 122888 | tf_op jit(solution)/shard_map/ppermute | solution.py:26
  92.5 1.1 collective-permute-start.26
  93.6 0.7 collective-permute-done.24
  94.3 0.4 collective-permute-done.25
  94.7 0.9 collective-permute-done.26
  95.7 5.5 %collective-permute-start.27 = (bf16[40,512]{1,0:T(8,128)(2,1)S(1)}, bf16[40,512]{1,0:T(8,128)(2,1)S(1)}, u32[]{:S(2)}, u32[]{:S(2)}) collective-permute-start(bf16[40,512]{1,0:T(8,128)(2,1)S(1)} %dynamic-slice_bitcast_fusion.5), channel_id=1, source_target_pairs={{0,2},{2,0},{1,3},{3,1},{4,6},{6,4},{5,7},{7,5},{8,10},{10,8},{9,1... | collective-permute-start | bytes 122888 | tf_op jit(solution)/shard_map/ppermute | solution.py:26
  101.2 0.2 reshape.149
  101.5 0.9 reshape.150
  102.3 0.2 collective-permute-done.27
  102.6 7.6 %collective-permute-start.29 = (f32[20,512]{1,0:T(8,128)S(1)}, f32[20,512]{1,0:T(8,128)S(1)}, u32[]{:S(2)}, u32[]{:S(2)}) collective-permute-start(f32[20,512]{1,0:T(8,128)S(1)} %dynamic-slice_bitcast_fusion.4), channel_id=1, source_target_pairs={{0,1},{1,0},{2,3},{3,2},{4,5},{5,4},{6,7},{7,6},{8,9},{9,8},{10,11... | collective-permute-start | bytes 122888 | tf_op jit(solution)/shard_map/ppermute | solution.py:26
  110.2 0.9 collective-permute-done.29
  111.2 0.6 copy-done.3
  (75 shorter events, 1.7 us)
Async XLA Ops:
  0.6 16.0 %collective-permute-start = (bf16[128,1024]{1,0:T(8,128)(2,1)}, bf16[128,1024]{1,0:T(8,128)(2,1)S(1)}, u32[]{:S(2)}, u32[]{:S(2)}) collective-permute-start(bf16[128,1024]{1,0:T(8,128)(2,1)} %bitcast.75), channel_id=1, source_target_pairs={{0,2},{1,3},{2,4},{3,5},{4,6},{5,7},{6,8},{7,9},{8,10},{9,11},{10,... | collective-permute-start | bytes 786440 | tf_op jit(solution)/shard_map/ppermute | solution.py:31
  9.5 6.5 %copy-start.4 = (s32[1,16]{1,0:T(1,128)S(1)}, s32[1,16]{1,0:T(1,128)}, u32[]{:S(2)}) copy-start(s32[1,16]{1,0:T(1,128)} %param.9) | copy-start | bytes 196
  9.5 7.1 %copy-start.1 = (bf16[1,128,1024]{2,1,0:T(8,128)(2,1)S(1)}, bf16[1,128,1024]{2,1,0:T(8,128)(2,1)}, u32[]{:S(2)}) copy-start(bf16[1,128,1024]{2,1,0:T(8,128)(2,1)} %param.6) | copy-start | bytes 786436
  10.9 18.4 %collective-permute-start.2 = (bf16[4,320,128]{2,1,0:T(8,128)(2,1)S(1)}, bf16[4,320,128]{2,1,0:T(8,128)(2,1)S(1)}, u32[]{:S(2)}, u32[]{:S(2)}) collective-permute-start(bf16[4,320,128]{2,1,0:T(8,128)(2,1)S(1)} %get-tuple-element.65), channel_id=1, source_target_pairs={{0,16},{16,32},{32,48},{48,0},{1,17},{17,33},{33,49},{49,1},{2,18}... | collective-permute-start | bytes 983048 | tf_op jit(solution)/shard_map/ppermute | solution.py:26
  12.3 17.0 %collective-permute-start.3 = (bf16[4,320,128]{2,1,0:T(8,128)(2,1)S(1)}, bf16[4,320,128]{2,1,0:T(8,128)(2,1)S(1)}, u32[]{:S(2)}, u32[]{:S(2)}) collective-permute-start(bf16[4,320,128]{2,1,0:T(8,128)(2,1)S(1)} %get-tuple-element.64), channel_id=1, source_target_pairs={{0,32},{16,48},{32,0},{48,16},{1,33},{17,49},{33,1},{49,17},{2,34}... | collective-permute-start | bytes 983048 | tf_op jit(solution)/shard_map/ppermute | solution.py:26
  14.9 14.4 %collective-permute-start.4 = (bf16[4,320,128]{2,1,0:T(8,128)(2,1)S(1)}, bf16[4,320,128]{2,1,0:T(8,128)(2,1)S(1)}, u32[]{:S(2)}, u32[]{:S(2)}) collective-permute-start(bf16[4,320,128]{2,1,0:T(8,128)(2,1)S(1)} %get-tuple-element.63), channel_id=1, source_target_pairs={{0,48},{16,0},{32,16},{48,32},{1,49},{17,1},{33,17},{49,33},{2,50}... | collective-permute-start | bytes 983048 | tf_op jit(solution)/shard_map/ppermute | solution.py:26
  16.6 2.8 %copy-start.2 = (bf16[128,1024]{1,0:T(8,128)(2,1)}, bf16[128,1024]{1,0:T(8,128)(2,1)S(1)}, u32[]{:S(2)}) copy-start(bf16[128,1024]{1,0:T(8,128)(2,1)S(1)} %collective-permute-done.kv2_ref) | copy-start | bytes 786436
  16.7 2.8 %collective-permute-start.1 = (bf16[128,1024]{1,0:T(8,128)(2,1)S(1)}, bf16[128,1024]{1,0:T(8,128)(2,1)S(1)}, u32[]{:S(2)}, u32[]{:S(2)}) collective-permute-start(bf16[128,1024]{1,0:T(8,128)(2,1)S(1)} %broadcast_select_fusion), channel_id=1, source_target_pairs={{0,1},{1,0},{2,3},{3,2},{4,5},{5,4},{6,7},{7,6},{8,9},{9,8},{10,11... | collective-permute-start | bytes 786440 | tf_op jit(solution)/shard_map/ppermute | solution.py:26
  19.5 0.7 copy-start.5
  29.4 2.8 %collective-permute-start.5 = (bf16[384,512]{1,0:T(8,128)(2,1)}, bf16[384,512]{1,0:T(8,128)(2,1)S(1)}, u32[]{:S(2)}, u32[]{:S(2)}) collective-permute-start(bf16[384,512]{1,0:T(8,128)(2,1)} %get-tuple-element.34), channel_id=1, source_target_pairs={{0,1},{1,0},{2,3},{3,2},{4,5},{5,4},{6,7},{7,6},{8,9},{9,8},{10,11... | collective-permute-start | bytes 1179656 | tf_op jit(solution)/shard_map/ppermute | solution.py:26
  30.6 1.6 %copy-start = (f32[384,512]{1,0:T(8,128)S(1)}, f32[384,512]{1,0:T(8,128)}, u32[]{:S(2)}) copy-start(f32[384,512]{1,0:T(8,128)} %get-tuple-element.35) | copy-start | bytes 2359300
  30.8 40.3 %collective-permute-start.6 = (bf16[4,4,320,128]{3,2,1,0:T(8,128)(2,1)S(1)}, bf16[4,4,320,128]{3,2,1,0:T(8,128)(2,1)S(1)}, u32[]{:S(2)}, u32[]{:S(2)}) collective-permute-start(bf16[4,4,320,128]{3,2,1,0:T(8,128)(2,1)S(1)} %pad_maximum_fusion.own_ref), channel_id=1, source_target_pairs={{0,1},{1,0},{2,3},{3,2},{4,5},{5,4},{6,7},{7,6},{8,9},{9,8},{10,11... | collective-permute-start | bytes 3932168 | tf_op jit(solution)/shard_map/ppermute | solution.py:26
  32.4 14.4 %collective-permute-start.7 = (bf16[256,256]{1,0:T(8,128)(2,1)S(1)}, bf16[256,256]{1,0:T(8,128)(2,1)S(1)}, u32[]{:S(2)}, u32[]{:S(2)}) collective-permute-start(bf16[256,256]{1,0:T(8,128)(2,1)S(1)} %pad_maximum_fusion.5), channel_id=1, source_target_pairs={{2,0},{3,1},{4,2},{5,3},{6,4},{7,5},{8,6},{9,7},{10,8},{11,9},{12,... | collective-permute-start | bytes 393224 | tf_op jit(solution)/shard_map/ppermute | solution.py:31
  43.2 15.0 %collective-permute-start.17 = (bf16[256,256]{1,0:T(8,128)(2,1)S(1)}, bf16[256,256]{1,0:T(8,128)(2,1)S(1)}, u32[]{:S(2)}, u32[]{:S(2)}) collective-permute-start(bf16[256,256]{1,0:T(8,128)(2,1)S(1)} %pad_maximum_fusion.4), channel_id=1, source_target_pairs={{2,0},{3,1},{4,2},{5,3},{6,4},{7,5},{8,6},{9,7},{10,8},{11,9},{12,... | collective-permute-start | bytes 393224 | tf_op jit(solution)/shard_map/ppermute | solution.py:31
  46.8 11.6 %collective-permute-start.10 = (bf16[256,256]{1,0:T(8,128)(2,1)S(1)}, bf16[256,256]{1,0:T(8,128)(2,1)S(1)}, u32[]{:S(2)}, u32[]{:S(2)}) collective-permute-start(bf16[256,256]{1,0:T(8,128)(2,1)S(1)} %fusion.refs_0_), channel_id=1, source_target_pairs={{0,192},{64,0},{128,64},{192,128},{1,193},{65,1},{129,65},{193,129... | collective-permute-start | bytes 393224 | tf_op jit(solution)/shard_map/ppermute | solution.py:26
  53.2 7.5 %collective-permute-start.8 = (bf16[256,256]{1,0:T(8,128)(2,1)S(1)}, bf16[256,256]{1,0:T(8,128)(2,1)S(1)}, u32[]{:S(2)}, u32[]{:S(2)}) collective-permute-start(bf16[256,256]{1,0:T(8,128)(2,1)S(1)} %fusion.refs_0_), channel_id=1, source_target_pairs={{0,64},{64,128},{128,192},{192,0},{1,65},{65,129},{129,193},{193,1... | collective-permute-start | bytes 393224 | tf_op jit(solution)/shard_map/ppermute | solution.py:26
  53.2 17.9 %collective-permute-start.9 = (bf16[256,256]{1,0:T(8,128)(2,1)S(1)}, bf16[256,256]{1,0:T(8,128)(2,1)S(1)}, u32[]{:S(2)}, u32[]{:S(2)}) collective-permute-start(bf16[256,256]{1,0:T(8,128)(2,1)S(1)} %fusion.refs_0_), channel_id=1, source_target_pairs={{0,128},{64,192},{128,0},{192,64},{1,129},{65,193},{129,1},{193,65... | collective-permute-start | bytes 393224 | tf_op jit(solution)/shard_map/ppermute | solution.py:26
  58.3 16.9 %collective-permute-start.18 = (bf16[256,256]{1,0:T(8,128)(2,1)S(1)}, bf16[256,256]{1,0:T(8,128)(2,1)S(1)}, u32[]{:S(2)}, u32[]{:S(2)}) collective-permute-start(bf16[256,256]{1,0:T(8,128)(2,1)S(1)} %add_convert_fusion.2.refs_0_), channel_id=1, source_target_pairs={{0,64},{64,128},{128,192},{192,0},{1,65},{65,129},{129,193},{193,1... | collective-permute-start | bytes 393224 | tf_op jit(solution)/shard_map/ppermute | solution.py:26
  58.4 16.6 %collective-permute-start.28 = (bf16[128,512]{1,0:T(8,128)(2,1)S(1)}, bf16[128,512]{1,0:T(8,128)(2,1)S(1)}, u32[]{:S(2)}, u32[]{:S(2)}) collective-permute-start(bf16[128,512]{1,0:T(8,128)(2,1)S(1)} %pad_maximum_fusion.3), channel_id=1, source_target_pairs={{0,1},{1,0},{2,3},{3,2},{4,5},{5,4},{6,7},{7,6},{8,9},{9,8},{10,11... | collective-permute-start | bytes 393224 | tf_op jit(solution)/shard_map/ppermute | solution.py:26
  60.6 16.6 %collective-permute-start.19 = (bf16[256,256]{1,0:T(8,128)(2,1)S(1)}, bf16[256,256]{1,0:T(8,128)(2,1)S(1)}, u32[]{:S(2)}, u32[]{:S(2)}) collective-permute-start(bf16[256,256]{1,0:T(8,128)(2,1)S(1)} %add_convert_fusion.2.refs_0_), channel_id=1, source_target_pairs={{0,128},{64,192},{128,0},{192,64},{1,129},{65,193},{129,1},{193,65... | collective-permute-start | bytes 393224 | tf_op jit(solution)/shard_map/ppermute | solution.py:26
  71.1 6.2 %collective-permute-start.20 = (bf16[256,256]{1,0:T(8,128)(2,1)S(1)}, bf16[256,256]{1,0:T(8,128)(2,1)S(1)}, u32[]{:S(2)}, u32[]{:S(2)}) collective-permute-start(bf16[256,256]{1,0:T(8,128)(2,1)S(1)} %add_convert_fusion.2.refs_0_), channel_id=1, source_target_pairs={{0,192},{64,0},{128,64},{192,128},{1,193},{65,1},{129,65},{193,129... | collective-permute-start | bytes 393224 | tf_op jit(solution)/shard_map/ppermute | solution.py:26
  72.5 9.8 %collective-permute-start.11 = (bf16[4,80,256]{2,1,0:T(8,128)(2,1)S(1)}, bf16[4,80,256]{2,1,0:T(8,128)(2,1)S(1)}, u32[]{:S(2)}, u32[]{:S(2)}) collective-permute-start(bf16[4,80,256]{2,1,0:T(8,128)(2,1)S(1)} %get-tuple-element.42), channel_id=1, source_target_pairs={{0,4},{4,8},{8,12},{12,0},{1,5},{5,9},{9,13},{13,1},{2,6},{6,10},{... | collective-permute-start | bytes 491528 | tf_op jit(solution)/shard_map/ppermute | solution.py:26
  75.0 7.3 %collective-permute-start.12 = (bf16[4,80,256]{2,1,0:T(8,128)(2,1)S(1)}, bf16[4,80,256]{2,1,0:T(8,128)(2,1)S(1)}, u32[]{:S(2)}, u32[]{:S(2)}) collective-permute-start(bf16[4,80,256]{2,1,0:T(8,128)(2,1)S(1)} %get-tuple-element.43), channel_id=1, source_target_pairs={{0,8},{4,12},{8,0},{12,4},{1,9},{5,13},{9,1},{13,5},{2,10},{6,14},... | collective-permute-start | bytes 491528 | tf_op jit(solution)/shard_map/ppermute | solution.py:26
  75.2 7.0 %collective-permute-start.13 = (bf16[4,80,256]{2,1,0:T(8,128)(2,1)S(1)}, bf16[4,80,256]{2,1,0:T(8,128)(2,1)S(1)}, u32[]{:S(2)}, u32[]{:S(2)}) collective-permute-start(bf16[4,80,256]{2,1,0:T(8,128)(2,1)S(1)} %get-tuple-element.44), channel_id=1, source_target_pairs={{0,12},{4,0},{8,4},{12,8},{1,13},{5,1},{9,5},{13,9},{2,14},{6,2},{... | collective-permute-start | bytes 491528 | tf_op jit(solution)/shard_map/ppermute | solution.py:26
  78.7 8.6 %collective-permute-start.21 = (bf16[4,80,256]{2,1,0:T(8,128)(2,1)S(1)}, bf16[4,80,256]{2,1,0:T(8,128)(2,1)S(1)}, u32[]{:S(2)}, u32[]{:S(2)}) collective-permute-start(bf16[4,80,256]{2,1,0:T(8,128)(2,1)S(1)} %get-tuple-element.46), channel_id=1, source_target_pairs={{0,4},{4,8},{8,12},{12,0},{1,5},{5,9},{9,13},{13,1},{2,6},{6,10},{... | collective-permute-start | bytes 491528 | tf_op jit(solution)/shard_map/ppermute | solution.py:26
  79.8 10.2 %collective-permute-start.22 = (bf16[4,80,256]{2,1,0:T(8,128)(2,1)S(1)}, bf16[4,80,256]{2,1,0:T(8,128)(2,1)S(1)}, u32[]{:S(2)}, u32[]{:S(2)}) collective-permute-start(bf16[4,80,256]{2,1,0:T(8,128)(2,1)S(1)} %get-tuple-element.47), channel_id=1, source_target_pairs={{0,8},{4,12},{8,0},{12,4},{1,9},{5,13},{9,1},{13,5},{2,10},{6,14},... | collective-permute-start | bytes 491528 | tf_op jit(solution)/shard_map/ppermute | solution.py:26
  82.3 7.8 %collective-permute-start.23 = (bf16[4,80,256]{2,1,0:T(8,128)(2,1)S(1)}, bf16[4,80,256]{2,1,0:T(8,128)(2,1)S(1)}, u32[]{:S(2)}, u32[]{:S(2)}) collective-permute-start(bf16[4,80,256]{2,1,0:T(8,128)(2,1)S(1)} %get-tuple-element.48), channel_id=1, source_target_pairs={{0,12},{4,0},{8,4},{12,8},{1,13},{5,1},{9,5},{13,9},{2,14},{6,2},{... | collective-permute-start | bytes 491528 | tf_op jit(solution)/shard_map/ppermute | solution.py:26
  82.4 10.0 %collective-permute-start.14 = (bf16[80,256]{1,0:T(8,128)(2,1)S(1)}, bf16[80,256]{1,0:T(8,128)(2,1)S(1)}, u32[]{:S(2)}, u32[]{:S(2)}) collective-permute-start(bf16[80,256]{1,0:T(8,128)(2,1)S(1)} %get-tuple-element.85), channel_id=1, source_target_pairs={{0,16},{16,32},{32,48},{48,0},{1,17},{17,33},{33,49},{49,1},{2,18}... | collective-permute-start | bytes 122888 | tf_op jit(solution)/shard_map/ppermute | solution.py:26
  83.8 9.7 %collective-permute-start.15 = (bf16[80,256]{1,0:T(8,128)(2,1)S(1)}, bf16[80,256]{1,0:T(8,128)(2,1)S(1)}, u32[]{:S(2)}, u32[]{:S(2)}) collective-permute-start(bf16[80,256]{1,0:T(8,128)(2,1)S(1)} %get-tuple-element.87), channel_id=1, source_target_pairs={{0,32},{16,48},{32,0},{48,16},{1,33},{17,49},{33,1},{49,17},{2,34}... | collective-permute-start | bytes 122888 | tf_op jit(solution)/shard_map/ppermute | solution.py:26
  87.3 6.2 %collective-permute-start.16 = (bf16[80,256]{1,0:T(8,128)(2,1)S(1)}, bf16[80,256]{1,0:T(8,128)(2,1)S(1)}, u32[]{:S(2)}, u32[]{:S(2)}) collective-permute-start(bf16[80,256]{1,0:T(8,128)(2,1)S(1)} %get-tuple-element.86), channel_id=1, source_target_pairs={{0,48},{16,0},{32,16},{48,32},{1,49},{17,1},{33,17},{49,33},{2,50}... | collective-permute-start | bytes 122888 | tf_op jit(solution)/shard_map/ppermute | solution.py:26
  90.2 4.2 %collective-permute-start.24 = (bf16[80,256]{1,0:T(8,128)(2,1)S(1)}, bf16[80,256]{1,0:T(8,128)(2,1)S(1)}, u32[]{:S(2)}, u32[]{:S(2)}) collective-permute-start(bf16[80,256]{1,0:T(8,128)(2,1)S(1)} %get-tuple-element.88), channel_id=1, source_target_pairs={{0,16},{16,32},{32,48},{48,0},{1,17},{17,33},{33,49},{49,1},{2,18}... | collective-permute-start | bytes 122888 | tf_op jit(solution)/shard_map/ppermute | solution.py:26
  90.2 4.5 %collective-permute-start.25 = (bf16[80,256]{1,0:T(8,128)(2,1)S(1)}, bf16[80,256]{1,0:T(8,128)(2,1)S(1)}, u32[]{:S(2)}, u32[]{:S(2)}) collective-permute-start(bf16[80,256]{1,0:T(8,128)(2,1)S(1)} %get-tuple-element.90), channel_id=1, source_target_pairs={{0,32},{16,48},{32,0},{48,16},{1,33},{17,49},{33,1},{49,17},{2,34}... | collective-permute-start | bytes 122888 | tf_op jit(solution)/shard_map/ppermute | solution.py:26
  92.5 3.2 %collective-permute-start.26 = (bf16[80,256]{1,0:T(8,128)(2,1)S(1)}, bf16[80,256]{1,0:T(8,128)(2,1)S(1)}, u32[]{:S(2)}, u32[]{:S(2)}) collective-permute-start(bf16[80,256]{1,0:T(8,128)(2,1)S(1)} %get-tuple-element.89), channel_id=1, source_target_pairs={{0,48},{16,0},{32,16},{48,32},{1,49},{17,1},{33,17},{49,33},{2,50}... | collective-permute-start | bytes 122888 | tf_op jit(solution)/shard_map/ppermute | solution.py:26
  95.7 6.8 %collective-permute-start.27 = (bf16[40,512]{1,0:T(8,128)(2,1)S(1)}, bf16[40,512]{1,0:T(8,128)(2,1)S(1)}, u32[]{:S(2)}, u32[]{:S(2)}) collective-permute-start(bf16[40,512]{1,0:T(8,128)(2,1)S(1)} %dynamic-slice_bitcast_fusion.5), channel_id=1, source_target_pairs={{0,2},{2,0},{1,3},{3,1},{4,6},{6,4},{5,7},{7,5},{8,10},{10,8},{9,1... | collective-permute-start | bytes 122888 | tf_op jit(solution)/shard_map/ppermute | solution.py:26
  102.6 8.5 %collective-permute-start.29 = (f32[20,512]{1,0:T(8,128)S(1)}, f32[20,512]{1,0:T(8,128)S(1)}, u32[]{:S(2)}, u32[]{:S(2)}) collective-permute-start(f32[20,512]{1,0:T(8,128)S(1)} %dynamic-slice_bitcast_fusion.4), channel_id=1, source_target_pairs={{0,1},{1,0},{2,3},{3,2},{4,5},{5,4},{6,7},{7,6},{8,9},{9,8},{10,11... | collective-permute-start | bytes 122888 | tf_op jit(solution)/shard_map/ppermute | solution.py:26
  111.2 0.6 copy-start.3
